TPU v7x, 32 devices: a whole 2x2x4 slice. The times are simulated.
32 devices in a mesh: groups: 1, fsdp: 32 (over z, y, x, core).
Axes of the slice: x: 2, y: 2, z: 4, core: 2. Of those that a mesh axis runs over, the one named last changes fastest.
Arguments:
- tokens: bfloat16 [8192, 8192], P(('groups', 'fsdp')), may hold values from -6 to 6
- frozen_value_weight: bfloat16 [8192, 1024], P('fsdp'), may hold values from -0.0625 to 0.0625
- adapter_down_weight: bfloat16 [8192, 256], P(('groups', 'fsdp')), may hold values from -0.0625 to 0.0625
- adapter_up_weight: bfloat16 [16, 16384], P('groups', 'fsdp'), may hold values from -1.5 to 1.5
- block_adapter_index: int32 [64], P(('groups', 'fsdp')), may hold values from 0 to 15
- block_valid_length: int32 [64], P(('groups', 'fsdp')), may hold values from 16 to 128
- destinations: int32 [64], P(('groups', 'fsdp')), may hold values from 0 to 31, as said below
- cotangent: bfloat16 [16384, 1024], P(('groups', 'fsdp')), may hold values from -6 to 6
Outputs:
- layer_out: bfloat16 [16384, 1024], P(('groups', 'fsdp'))
- down_gradient: float32 [8192, 256], P(('groups', 'fsdp'))
- up_gradient: float32 [16, 16384], P('groups', 'fsdp')
Inputs may be any that keep to these rules, and one draw needn't show every extreme that they name: `destinations`: block j of device d has destination d - 1, d or d + 1; each device sends at most one block to each neighbour.
All inputs are finite; a program needn't handle non-finite values.
Results may differ from a plain program's by a relative error of at most 0.0046.
Values may be sent and summed in bfloat16 or wider, within the bound.
No kernel may reach another device: no remote copies, remote signals or barrier semaphores. Data moves between devices by JAX's collectives and lax.ppermute only.
A program may use at most 128 MiB of HBM per device.

v0:
```python
import jax
import jax.numpy as jnp
from jax import lax
from jax.sharding import PartitionSpec as P

ADAPTER_RANK = 16
ADAPTER_COUNT = 16
BLOCK = 128


ADAPTER_SCALE = 2.0


def from_behind(block, axis, distance):
    devices = range(lax.axis_size(axis))
    route = [(i - distance, i) for i in devices if i - distance in devices]
    return lax.ppermute(block, axis, route)


def pick_block(block_array, chosen):
    zero_value = jnp.zeros((), block_array.dtype)
    selected_entries = jnp.where(chosen[:, None, None], block_array, zero_value)
    return jnp.sum(selected_entries, axis=0)


def pick_meta(block_adapter_index, block_valid_length, chosen):
    adapter_sent = jnp.sum(jnp.where(chosen, block_adapter_index, 0))
    length_sent = jnp.sum(jnp.where(chosen, block_valid_length, 0))
    return jnp.stack([adapter_sent, length_sent]).astype(jnp.bfloat16)


def frozen_products(source_blocks, frozen_value_weight, adapter_down_weight):
    weight = jnp.concatenate(
        (
            lax.all_gather(frozen_value_weight, "fsdp", axis=0, tiled=True),
            lax.all_gather(adapter_down_weight, "fsdp", axis=0, tiled=True),
        ),
        axis=1,
    )
    results = [
        jnp.dot(source, weight, preferred_element_type=jnp.float32) for source in source_blocks
    ]
    return jnp.concatenate(results, axis=0)


def forward(partial_products, slot_adapters, slot_lengths, up_table):
    kv_width = up_table.shape[2]
    slot_count = slot_adapters.shape[0]
    base_output = partial_products[:, :kv_width].reshape(slot_count, BLOCK, kv_width)
    down_all = partial_products[:, kv_width:].reshape(
        slot_count, BLOCK, ADAPTER_COUNT, ADAPTER_RANK
    )
    adapter_selector = (
        slot_adapters[:, None] == jnp.arange(ADAPTER_COUNT, dtype=jnp.int32)[None, :]
    ).astype(jnp.float32)
    activation_matrix = jnp.sum(down_all * adapter_selector[:, None, :, None], axis=2).astype(
        jnp.bfloat16
    )
    raising_matrix_per_position = jnp.sum(
        up_table.astype(jnp.float32)[None] * adapter_selector[:, None, :, None], axis=2
    ).astype(jnp.bfloat16)
    adapter_output = jnp.einsum(
        "kph,khb->kpb",
        activation_matrix,
        raising_matrix_per_position,
        preferred_element_type=jnp.float32,
    )
    valid_row_mask = jnp.arange(BLOCK, dtype=jnp.int32)[None, :] < slot_lengths[:, None]
    value_output = jnp.where(
        valid_row_mask[..., None], base_output + ADAPTER_SCALE * adapter_output, jnp.float32(0.0)
    ).astype(jnp.bfloat16)
    return (
        value_output,
        activation_matrix,
        raising_matrix_per_position,
        adapter_selector,
        valid_row_mask,
    )


def backward(
    source_blocks,
    activation_matrix,
    grad_out,
    raising_matrix_per_position,
    adapter_selector,
    local_row_count,
):
    slot_count = activation_matrix.shape[0]
    up_weight_terms = jnp.einsum(
        "snr,snk->srk", activation_matrix, grad_out, preferred_element_type=jnp.float32
    )
    up_weight_total = ADAPTER_SCALE * jnp.sum(
        up_weight_terms[:, :, None, :] * adapter_selector[:, None, :, None], axis=0
    )
    up_gradient = lax.psum_scatter(
        up_weight_total.reshape(ADAPTER_RANK, -1), "fsdp", scatter_dimension=1, tiled=True
    )
    low_grad = jnp.einsum(
        "snk,srk->snr", grad_out, raising_matrix_per_position, preferred_element_type=jnp.float32
    ).astype(jnp.bfloat16)
    columns = jnp.concatenate([source for source in source_blocks], axis=0).reshape(
        slot_count, BLOCK, lax.axis_size("fsdp") * local_row_count
    )
    per_slot = jnp.einsum("snd,snr->sdr", columns, low_grad, preferred_element_type=jnp.float32)
    summed_output = jnp.sum(per_slot[:, :, None, :] * adapter_selector[:, None, :, None], axis=0)
    down_gradient = lax.psum_scatter(
        ADAPTER_SCALE * summed_output.reshape(lax.axis_size("fsdp") * local_row_count, -1),
        "fsdp",
        scatter_dimension=0,
        tiled=True,
    )
    return (down_gradient, up_gradient)


def body(
    tokens,
    frozen_value_weight,
    adapter_down_weight,
    adapter_up_weight,
    block_adapter_index,
    block_valid_length,
    destinations,
    cotangent,
):
    tok_rows, model_width = tokens.shape
    blocks = tok_rows // BLOCK
    kv_width = frozen_value_weight.shape[1]
    my_index = lax.axis_index("fsdp")
    moving_right = destinations == my_index + 1
    moving_left = destinations == my_index - 1
    staying = destinations == my_index
    token_blocks = tokens.reshape(blocks, BLOCK, model_width)
    every_up_weight = lax.all_gather(adapter_up_weight, "fsdp", axis=1, tiled=True)
    up_table = every_up_weight.reshape(ADAPTER_RANK, ADAPTER_COUNT, kv_width)
    slot_grads = cotangent.reshape(-1, BLOCK, kv_width)
    zero_grad = jnp.zeros((), jnp.bfloat16)
    right_block = pick_block(token_blocks, moving_right)
    left_block = pick_block(token_blocks, moving_left)
    right_meta = pick_meta(block_adapter_index, block_valid_length, moving_right)
    left_meta = pick_meta(block_adapter_index, block_valid_length, moving_left)
    from_lower, lower_info = from_behind((right_block, right_meta), "fsdp", 1)
    from_upper, upper_info = from_behind((left_block, left_meta), "fsdp", -1)
    source_blocks = [from_lower, tokens, from_upper]
    slot_adapters = jnp.concatenate(
        [lower_info[0:1].astype(jnp.int32), block_adapter_index, upper_info[0:1].astype(jnp.int32)]
    )
    slot_lengths = jnp.concatenate(
        [
            lower_info[1:2].astype(jnp.int32),
            jnp.where(staying, block_valid_length, 0),
            upper_info[1:2].astype(jnp.int32),
        ]
    )
    partial_products = frozen_products(source_blocks, frozen_value_weight, adapter_down_weight)
    (
        value_output,
        activation_matrix,
        raising_matrix_per_position,
        adapter_selector,
        valid_row_mask,
    ) = forward(partial_products, slot_adapters, slot_lengths, up_table)
    layer_out = value_output.reshape(-1, kv_width)
    grad_out = jnp.where(valid_row_mask[..., None], slot_grads, zero_grad)
    local_row_count = model_width // lax.axis_size("fsdp")
    down_gradient, up_gradient = backward(
        source_blocks,
        activation_matrix,
        grad_out,
        raising_matrix_per_position,
        adapter_selector,
        local_row_count,
    )
    return (layer_out, down_gradient, up_gradient)


def solution(mesh):
    in_specs = (
        P(("groups", "fsdp"), None),
        P("fsdp", None),
        P(("groups", "fsdp"), None),
        P("groups", "fsdp"),
        P(("groups", "fsdp")),
        P(("groups", "fsdp")),
        P(("groups", "fsdp")),
        P(("groups", "fsdp"), None),
    )
    out_specs = (P(("groups", "fsdp"), None), P(("groups", "fsdp"), None), P("groups", "fsdp"))
    return jax.shard_map(body, mesh=mesh, in_specs=in_specs, out_specs=out_specs, check_vma=False)
```

profile of v0, /device:TPU:0, one launch (start us, length us, event | category | flops | bytes accessed | tf_op | source)
XLA Modules:
  0.0 559.4 jit_solution(16803301212376851177)
XLA Ops:
  7.2 0.0 all-gather.3.cloned.1.call-start
  7.2 0.7 all-gather.3.cloned.1.call-update
  7.9 0.0 all-gather.5.cloned.1.call-start
  7.9 0.7 all-gather.5.cloned.1.call-update
  8.6 0.0 reduce-scatter.3.cloned.1.call-start
  8.7 1.4 select_reduce_fusion.5
  10.1 6.6 %select_reduce_fusion.1 = (bf16[128,8192]{1,0:T(8,128)(2,1)}, bf16[128,8192]{1,0:T(8,128)(2,1)}) fusion(bf16[2,128,8192]{2,1,0:T(8,128)(2,1)} %bitcast.30, pred[2]{0:T(512)(128)(4,1)S(1)} %get-tuple-element.24, pred[2]{0:T(512)(128)(4,1)S(1)} %get-tuple-element.23), kind=kLoop, calls=%fused_computation.6 | loop fusion | flops 6291456 | bytes 8388612 | tf_op jit(solution)/shard_map/reduce_sum | solution.py:23
  16.7 2.5 collective-permute-start.2
  19.2 1.3 collective-permute-start.3
  21.7 0.1 pad_maximum_fusion.3
  21.7 5.0 collective-permute-start
  28.0 0.1 pad_maximum_fusion.4
  28.1 1.3 collective-permute-start.1
  29.4 0.0 copy-done.6
  29.4 94.8 %all_gather.11 = bf16[16,16384]{1,0:T(8,128)(2,1)S(1)} all-gather(bf16[16,512]{1,0:T(8,128)(2,1)S(1)} %copy-done.6), channel_id=1, replica_groups=mesh['groups'=1,'fsdp'=32] {'fsdp'}, dimensions={1}, use_global_device_ids=true | all-gather | bytes 540672 | tf_op jit(solution)/shard_map/all_gather | solution.py:134
  124.2 1.3 copy.35
  125.5 0.0 collective-permute-done
  125.5 0.6 fusion.15
  126.7 0.0 collective-permute-done.1
  126.7 0.6 fusion.16
  127.9 0.0 copy-done.7
  127.9 0.1 pad_add_fusion.1
  128.0 0.1 fusion.11
  128.1 0.1 copy.31
  129.4 0.1 pad_add_fusion
  129.5 0.1 iota_compare_fusion.1
  129.5 0.0 collective-permute-done.2
  129.6 0.0 collective-permute-done.3
  129.6 6.8 %pad_maximum_fusion = bf16[512,8192]{1,0:T(8,128)(2,1)} fusion(bf16[128,8192]{1,0:T(8,128)(2,1)} %collective-permute-done.3, bf16[256,8192]{1,0:T(8,128)(2,1)} %param.8, bf16[128,8192]{1,0:T(8,128)(2,1)S(1)} %collective-permute-done.2), kind=kLoop, calls=%fused_computation.1 | loop fusion | flops 25165824 | bytes 16777216 | tf_op jit(solution)/shard_map/concatenate | solution.py:102
  136.4 16.4 %all-gather.3.cloned.1.call-done = bf16[8192,1024]{1,0:T(8,128)(2,1)} async-done(((bf16[256,1024]{1,0:T(8,128)(2,1)}), bf16[8192,1024]{1,0:T(8,128)(2,1)}) %all-gather.3.cloned.1.call-update) | async-done | bytes 16777232 | tf_op jit(solution)/shard_map/all_gather | solution.py:35
  152.7 13.9 %constant_dynamic-update-slice_fusion.1 = bf16[8192,1280]{1,0:T(8,128)(2,1)} fusion(bf16[8192,1024]{1,0:T(8,128)(2,1)} %all-gather.3.cloned.1.call-done), kind=kLoop, calls=%fused_computation.25 | loop fusion | bytes 33554432
  166.7 49.5 %all-gather.5.cloned.1.call-done = bf16[8192,256]{1,0:T(8,128)(2,1)} async-done(((bf16[256,256]{1,0:T(8,128)(2,1)}), bf16[8192,256]{1,0:T(8,128)(2,1)}) %all-gather.5.cloned.1.call-update) | async-done | bytes 4194320 | tf_op jit(solution)/shard_map/all_gather | solution.py:36
  216.2 4.6 constant_dynamic-update-slice_fusion
  220.7 14.6 %convolution_bitcast_fusion = f32[256,1280]{1,0:T(8,128)} fusion(bf16[256,8192]{1,0:T(8,128)(2,1)} %param.8, bf16[8192,1280]{1,0:T(8,128)(2,1)} %constant_dynamic-update-slice_fusion), kind=kOutput, calls=%fused_computation.7 | convolution fusion | flops 5368709120 | bytes 26476544 | tf_op jit(solution)/shard_map/dot_general | solution.py:41
  235.4 0.0 copy-done
  235.4 3.0 fusion.17
  238.4 0.0 copy-start.3
  238.4 4.8 fusion.18
  243.2 0.0 copy-done.3
  243.3 0.9 pad_maximum_fusion.2
  244.2 2.1 copy.30
  246.3 2.0 reshape.87
  248.3 1.2 multiply_reduce_fusion.3
  249.5 1.5 fusion.1
  251.1 0.0 copy-done.5
  251.1 1.7 multiply_reduce_fusion.1
  252.8 0.0 copy-done.1
  252.8 5.3 fusion
  258.1 6.5 %multiply_reduce_fusion = f32[8192,16,16]{0,2,1:T(8,128)} fusion(f32[4,16]{1,0:T(4,128)S(1)} %fusion.11, f32[4,8192,16]{1,2,0:T(8,128)S(1)} %fusion), kind=kLoop, calls=%fused_computation | loop fusion | flops 14680064 | bytes 10486016 | tf_op jit(solution)/shard_map/reduce_sum | solution.py:106
  264.5 7.5 %broadcast_multiply_fusion = f32[8192,16,16]{0,2,1:T(8,128)} fusion(f32[8192,16,16]{0,2,1:T(8,128)} %multiply_reduce_fusion), kind=kLoop, calls=%fused_computation.3 | loop fusion | flops 2097152 | bytes 16777216 | tf_op jit(solution)/shard_map/mul | solution.py:108
  272.1 0.0 reduce-scatter.3.cloned.1.call-update
  272.1 0.0 reduce-scatter.5.cloned.1.call-start
  272.2 1.5 broadcast_multiply_fusion.1
  273.6 1.7 copy.36
  275.3 0.0 reduce-scatter.5.cloned.1.call-update
  275.3 0.0 copy-done.2
  275.4 0.0 copy-done.4
  275.4 0.2 pad_maximum_fusion.1
  275.5 0.3 slice.24
  275.8 0.5 fusion.7
  276.3 1.2 select_convert_fusion
  277.6 141.8 %reduce-scatter.3.cloned.1.call-done = f32[256,256]{0,1:T(8,128)} async-done(((f32[8192,256]{0,1:T(8,128)}), f32[256,256]{0,1:T(8,128)}) %reduce-scatter.3.cloned.1.call-update) | async-done | bytes 262160 | tf_op jit(solution)/shard_map/reduce_scatter | solution.py:107
  419.4 1.8 copy.34
  421.2 131.7 %reduce-scatter.5.cloned.1.call-done = f32[16,512]{1,0:T(8,128)} async-done(((f32[16,16384]{1,0:T(8,128)}), f32[16,512]{1,0:T(8,128)}) %reduce-scatter.5.cloned.1.call-update) | async-done | bytes 32784 | tf_op jit(solution)/shard_map/reduce_scatter | solution.py:96
  (7 shorter events, 0.0 us)
Async XLA Ops:
  7.2 145.6 %all-gather.3.cloned.1.call-start = ((), (), s32[]{:S(2)}) async-start(), calls=%async_computation.2 | async-start | bytes 17301504 | tf_op jit(solution)/shard_map/all_gather | solution.py:35
  7.9 208.3 %all-gather.5.cloned.1.call-start = ((), (), s32[]{:S(2)}) async-start(), calls=%async_computation.3 | async-start | bytes 4325376 | tf_op jit(solution)/shard_map/all_gather | solution.py:36
  8.6 410.8 %reduce-scatter.3.cloned.1.call-start = ((), (), s32[]{:S(2)}) async-start(), calls=%async_computation.4 | async-start | bytes 8650752 | tf_op jit(solution)/shard_map/reduce_scatter | solution.py:107
  10.1 19.4 %copy-start.6 = (bf16[16,512]{1,0:T(8,128)(2,1)S(1)}, bf16[16,512]{1,0:T(8,128)(2,1)}, u32[]{:S(2)}) copy-start(bf16[16,512]{1,0:T(8,128)(2,1)} %param.11) | copy-start | bytes 49156
  10.1 117.9 %copy-start.7 = (s32[2]{0:T(128)S(1)}, s32[2]{0:T(128)}, u32[]{:S(2)}) copy-start(s32[2]{0:T(128)} %param.12) | copy-start | bytes 28
  16.7 112.9 %collective-permute-start.2 = (bf16[128,8192]{1,0:T(8,128)(2,1)}, bf16[128,8192]{1,0:T(8,128)(2,1)S(1)}, u32[]{:S(2)}, u32[]{:S(2)}) collective-permute-start(bf16[128,8192]{1,0:T(8,128)(2,1)} %get-tuple-element.15), channel_id=1, source_target_pairs={{0,1},{1,2},{2,3},{3,4},{4,5},{5,6},{6,7},{7,8},{8,9},{9,10},{10,1... | collective-permute-start | bytes 6291464 | tf_op jit(solution)/shard_map/ppermute | solution.py:17
  19.2 110.4 %collective-permute-start.3 = (bf16[128,8192]{1,0:T(8,128)(2,1)}, bf16[128,8192]{1,0:T(8,128)(2,1)}, u32[]{:S(2)}, u32[]{:S(2)}) collective-permute-start(bf16[128,8192]{1,0:T(8,128)(2,1)} %get-tuple-element.16), channel_id=1, source_target_pairs={{1,0},{2,1},{3,2},{4,3},{5,4},{6,5},{7,6},{8,7},{9,8},{10,9},{11,1... | collective-permute-start | bytes 6291464 | tf_op jit(solution)/shard_map/ppermute | solution.py:17
  21.7 103.7 %collective-permute-start = (bf16[2]{0:T(256)(128)(2,1)S(1)}, bf16[2]{0:T(256)(128)(2,1)S(1)}, u32[]{:S(2)}, u32[]{:S(2)}) collective-permute-start(bf16[2]{0:T(256)(128)(2,1)S(1)} %pad_maximum_fusion.3), channel_id=1, source_target_pairs={{0,1},{1,2},{2,3},{3,4},{4,5},{5,6},{6,7},{7,8},{8,9},{9,10},{10,1... | collective-permute-start | bytes 20 | tf_op jit(solution)/shard_map/ppermute | solution.py:17
  28.1 98.6 %collective-permute-start.1 = (bf16[2]{0:T(256)(128)(2,1)S(1)}, bf16[2]{0:T(256)(128)(2,1)S(1)}, u32[]{:S(2)}, u32[]{:S(2)}) collective-permute-start(bf16[2]{0:T(256)(128)(2,1)S(1)} %pad_maximum_fusion.4), channel_id=1, source_target_pairs={{1,0},{2,1},{3,2},{4,3},{5,4},{6,5},{7,6},{8,7},{9,8},{10,9},{11,1... | collective-permute-start | bytes 20 | tf_op jit(solution)/shard_map/ppermute | solution.py:17
  220.7 14.6 %copy-start = (bf16[8192,1280]{1,0:T(8,128)(2,1)S(1)}, bf16[8192,1280]{1,0:T(8,128)(2,1)}, u32[]{:S(2)}) copy-start(bf16[8192,1280]{1,0:T(8,128)(2,1)} %constant_dynamic-update-slice_fusion) | copy-start | bytes 62914564
  238.4 4.9 copy-start.3
  243.3 9.6 %copy-start.1 = (f32[128,1280]{1,0:T(8,128)}, f32[128,1280]{1,0:T(8,128)S(1)}, u32[]{:S(2)}) copy-start(f32[128,1280]{1,0:T(8,128)S(1)} %fusion.18) | copy-start | bytes 1966084
  244.2 6.9 %copy-start.5 = (f32[2,8,16,1024]{3,2,1,0:T(8,128)S(1)}, f32[2,8,16,1024]{3,2,1,0:T(8,128)}, u32[]{:S(2)}) copy-start(f32[2,8,16,1024]{3,2,1,0:T(8,128)} %copy.35) | copy-start | bytes 3145732
  272.1 3.2 copy-start.2
  272.1 3.2 copy-start.4
  272.1 280.7 %reduce-scatter.5.cloned.1.call-start = ((), (), s32[]{:S(2)}) async-start(), calls=%async_computation.5 | async-start | bytes 1081344 | tf_op jit(solution)/shard_map/reduce_scatter | solution.py:96
Sparse Core Ops, SparseCore 0:
  10.9 141.8 all-gather.2
  155.6 60.5 all-gather.4
  272.2 147.1 reduce-scatter.2
  422.1 130.7 reduce-scatter.4
where the time goes:
time: 560 us; the launch traced here: 559 us
  waiting for transfers between devices  341 us (61%)
  blocking collectives  94.8 us (17%)
  other arithmetic  36 us (6%)
  matrix products  29.8 us (5%)
  local copies, waits for them, and re-layouts  28.9 us (5%)
  between operations  19 us (3%)
  starting transfers between devices  10.2 us (2%)
    reduce_scatter x1, waiting for transfers between devices, backward(): lax.psum_scatter(ADAPTER_SCALE * summed_output.reshape(lax.axis_size('fsd...  142 us
    reduce_scatter x1, waiting for transfers between devices, backward(): lax.psum_scatter(up_weight_total.reshape(ADAPTER_RANK, -1), 'fsdp', scatt...  132 us
    all_gather x1, blocking collectives, body(): lax.all_gather(adapter_up_weight, 'fsdp', axis=1, tiled=True)  94.8 us
    all_gather x1, waiting for transfers between devices, frozen_products(): lax.all_gather(adapter_down_weight, 'fsdp', axis=0, tiled=True)  49.5 us
    dot_general x3, matrix products, frozen_products(): jnp.dot(source, weight, preferred_element_type=jnp.float32)  22.5 us
    unnamed x20, local copies, waits for them, and re-layouts  18.7 us
    all_gather x1, waiting for transfers between devices, frozen_products(): lax.all_gather(frozen_value_weight, 'fsdp', axis=0, tiled=True)  16.4 us
  transfers between devices with their start and end apart: 8, of which 4 were waited for; matrix products, arithmetic and copies ran while one was open for 7% of the time, Pallas kernels for 0%

commit v1 on v0

v1 whole, which is shorter than its diff:
```python
import functools

import jax
import jax.numpy as jnp
from jax import lax
from jax.experimental import pallas as pl
from jax.experimental.pallas import tpu as pltpu
from jax.sharding import PartitionSpec as P

RANK = 16
COUNT = 16
BLOCK = 128
WIDE = RANK * COUNT
SCALE = 2.0
MIB = 1 << 20
F32 = jnp.float32
BF16 = jnp.bfloat16
VMEM = pl.BlockSpec(memory_space=pltpu.VMEM)
ANY = pl.BlockSpec(memory_space=pl.ANY)


def send_to(x, size, target):
    return lax.ppermute(x, "fsdp", [(i, target(i)) for i in range(size)])


def swap(x, size, bit):
    return send_to(x, size, lambda i: i ^ bit)


def ring(x, size):
    return send_to(x, size, lambda i: (i + 8) % size)


def shift(x, size, step):
    pairs = [(i, i + step) for i in range(size) if 0 <= i + step < size]
    return lax.ppermute(x, "fsdp", pairs)


def chip_at(me, planes, group, step):
    chip = me // 2
    z = chip // 4
    y = (chip // 2) % 2
    x = chip % 2
    if group & 1:
        x = 1 - x
    if group & 2:
        y = 1 - y
    return lax.rem(z + planes - step, planes) * 4 + y * 2 + x


def gather_pieces(piece, size):
    held = [piece]
    for _ in range(size // 8 - 1):
        held.append(ring(held[-1], size))
    line = jnp.stack(held)
    half = line.shape[0] // 2
    across_x = swap(line, size, 2)
    across_y = swap(line, size, 4)
    first = swap(across_x[:half], size, 4)
    last = swap(across_y[half:], size, 2)
    return line, across_x, across_y, first, last


def split_tokens(tokens, size):
    rows, width = tokens.shape
    depth = width // size
    chips = size // 2
    planes = size // 8

    def kernel(tok, mine, other, sems):
        me = lax.axis_index("fsdp")
        core = lax.rem(me, 2)
        copies = []
        for i in range(chips):
            chip = chip_at(me, planes, i // planes, i % planes)
            for n, (ref, parity) in enumerate(((other, 1 - core), (mine, core))):
                start = pl.multiple_of((2 * chip + parity) * depth, depth)
                copy = pltpu.make_async_copy(
                    tok.at[:, pl.ds(start, depth)],
                    ref.at[:, pl.ds(i * depth, depth)],
                    sems.at[n, i],
                )
                copy.start()
                copies.append(copy)
        for copy in copies:
            copy.wait()

    half = jax.ShapeDtypeStruct((rows, width // 2), tokens.dtype)
    return pl.pallas_call(
        kernel,
        out_shape=(half, half),
        in_specs=[ANY],
        out_specs=(ANY, ANY),
        scratch_shapes=[pltpu.SemaphoreType.DMA((2, chips))],
        name="split_tokens",
    )(tokens)


def dot(a, b):
    return jnp.dot(a, b, preferred_element_type=F32)


def dot_nt(a, b):
    return lax.dot_general(a, b, (((1,), (1,)), ((), ())), preferred_element_type=F32)


def dot_tn(a, b):
    return lax.dot_general(a, b, (((0,), (0,)), ((), ())), preferred_element_type=F32)


def low_rank_products(tok, tok_in, pieces, grad, grad_in, size):
    rows = tok.shape[0]
    depth = tok.shape[1] * 2 // size
    planes = size // 8
    quarters = (pieces[0].shape[1] - depth - 16) // 16

    def kernel(tok, tok_in, line, ax, ay, first, last, grad, grad_in, out, table):
        me = lax.axis_index("fsdp")

        def piece(i):
            group, step = i // planes, i % planes
            if group < 3:
                return (line, ax, ay)[group].at[step]
            return first.at[step] if step < planes // 2 else last.at[step - planes // 2]

        for half, source in enumerate((tok, tok_in)):
            total = jnp.zeros((rows, WIDE), F32)
            for i in range(4 * planes):
                total += dot(source[:, i * depth : (i + 1) * depth], piece(i)[:depth])
            out[half * rows : (half + 1) * rows] = total
        meta = jnp.zeros((16, WIDE), F32)
        for i in range(4 * planes):
            chip = chip_at(me, planes, i // planes, i % planes)
            for q in range(quarters):
                flat = chip * quarters + q
                spot = pl.multiple_of(flat // 2 * RANK, RANK)
                table[lax.rem(flat, 2), pl.ds(spot, RANK), :] = piece(i)[
                    depth + q * 16 : depth + (q + 1) * 16
                ]
            meta += piece(i)[depth + quarters * 16 :].astype(F32)
        for half, source in enumerate((grad, grad_in)):
            low = dot_nt(source[:, :256], table[0]) + dot_nt(source[:, 256:], table[1])
            out[(2 + half) * rows : (3 + half) * rows] = low
        out[4 * rows :] = meta

    return pl.pallas_call(
        kernel,
        out_shape=(
            jax.ShapeDtypeStruct((4 * rows + 16, WIDE), F32),
            jax.ShapeDtypeStruct((2, WIDE, 256), BF16),
        ),
        in_specs=[VMEM] * 9,
        out_specs=(VMEM, VMEM),
        compiler_params=pltpu.CompilerParams(vmem_limit_bytes=20 * MIB),
        cost_estimate=pl.CostEstimate(
            flops=4 * rows * (tok.shape[1] + 512) * WIDE, bytes_accessed=9 * MIB, transcendentals=0
        ),
        name="low_rank_products",
    )(tok, tok_in, *pieces, grad, grad_in)


def adapter_terms(own, other, tok, tok_in, grad, grad_in, size, kind):
    rows = tok.shape[0]
    depth = tok.shape[1] * 2 // size
    planes = size // 8
    slices = 512 // depth

    def kernel(own, other, tok, tok_in, grad, grad_in, hidden, names, terms):
        me = lax.axis_index("fsdp")
        table = own[4 * rows :] + other[4 * rows :]
        names[...] = table
        lane = lax.broadcasted_iota(jnp.int32, (1, WIDE), 1)
        row = lax.broadcasted_iota(jnp.int32, (rows, 1), 0)
        adapter_of_lane = (lane // RANK).astype(F32)
        fold_row = lax.broadcasted_iota(jnp.int32, (WIDE, 2 * RANK), 0)
        fold_lane = lax.broadcasted_iota(jnp.int32, (WIDE, 2 * RANK), 1)
        fold = (fold_row % RANK == fold_lane % RANK).astype(F32).astype(BF16)
        block_lane = lax.broadcasted_iota(jnp.int32, (rows, 2 * RANK), 1) // RANK
        block_row = lax.broadcasted_iota(jnp.int32, (rows, 2 * RANK), 0) // BLOCK
        for half, source in enumerate((tok, tok_in)):
            device = me if half == 0 else me + 1 - 2 * lax.rem(me, 2)
            found = [
                jnp.sum(jnp.where(lane == device, table[b : b + 1], 0.0), axis=1, keepdims=True)
                for b in range(2)
            ]
            adapter = jnp.where(row < BLOCK, found[0], found[1])
            chosen = adapter_of_lane == adapter
            mine, theirs = half * rows, (1 - half) * rows
            act = own[mine : mine + rows] + other[theirs : theirs + rows]
            hidden[mine : mine + rows] = jnp.where(chosen, act, 0.0).astype(BF16)
            mine, theirs = mine + 2 * rows, theirs + 2 * rows
            low = own[mine : mine + rows] + other[theirs : theirs + rows]
            low = jnp.where(chosen, low, 0.0).astype(BF16)
            narrow = jnp.where(block_lane == block_row, dot(low, fold), 0.0).astype(BF16)
            for i in range(4 * planes):
                chip = chip_at(me, planes, i // planes, i % planes)
                term = dot_tn(narrow, source[:, i * depth : (i + 1) * depth])
                terms[chip, half * 32 : (half + 1) * 32, :] = term.astype(kind)
        up = dot_tn(hidden[:rows], grad[...]) + dot_tn(hidden[rows:], grad_in[...])
        for a in range(COUNT):
            for t in range(slices):
                chip, place = divmod(a * slices + t, 2)
                terms[chip, 64 + 16 * place : 80 + 16 * place, :] = up[
                    a * RANK : (a + 1) * RANK, t * depth : (t + 1) * depth
                ].astype(kind)

    return pl.pallas_call(
        kernel,
        out_shape=(
            jax.ShapeDtypeStruct((2 * rows, WIDE), BF16),
            jax.ShapeDtypeStruct((16, WIDE), F32),
            jax.ShapeDtypeStruct((size // 2, 96, depth), kind),
        ),
        in_specs=[VMEM] * 6,
        out_specs=(VMEM, VMEM, VMEM),
        compiler_params=pltpu.CompilerParams(vmem_limit_bytes=24 * MIB),
        cost_estimate=pl.CostEstimate(
            flops=4 * rows * tok.shape[1] * 128, bytes_accessed=9 * MIB, transcendentals=0
        ),
        name="adapter_terms",
    )(own, other, tok, tok_in, grad, grad_in)


def sum_terms(terms, names, size):
    chips, _, depth = terms.shape

    def kernel(terms, names, down, up):
        core = lax.rem(lax.axis_index("fsdp"), 2)
        count = chips * 64
        device = lax.broadcasted_iota(jnp.int32, (WIDE, count), 0)
        spot = lax.broadcasted_iota(jnp.int32, (WIDE, count), 1)
        block = (spot // 16) % 4
        sender = 2 * (spot // 64) + jnp.where(block < 2, core, 1 - core)
        table = names[...].astype(BF16)
        first = ((device == sender) & (block % 2 == 0)).astype(F32).astype(BF16)
        second = ((device == sender) & (block % 2 == 1)).astype(F32).astype(BF16)
        adapter = (dot(table, first)[0:1] + dot(table, second)[1:2]).astype(jnp.int32)
        pick = (device == adapter * RANK + spot % RANK).astype(F32)
        source = terms[:, :64, :].reshape(count, depth)
        if terms.dtype == BF16:
            total = dot(pick.astype(BF16), source)
        else:
            total = jnp.dot(
                pick, source, preferred_element_type=F32, precision=lax.Precision.HIGHEST
            )
        down[...] = SCALE * total.T
        for s in range(2):
            up[:, s * depth : (s + 1) * depth] = SCALE * jnp.sum(
                terms[:, 64 + 16 * s : 80 + 16 * s, :].astype(F32), axis=0
            )

    return pl.pallas_call(
        kernel,
        out_shape=(
            jax.ShapeDtypeStruct((depth, WIDE), F32),
            jax.ShapeDtypeStruct((RANK, 2 * depth), F32),
        ),
        in_specs=[VMEM] * 2,
        out_specs=(VMEM, VMEM),
        compiler_params=pltpu.CompilerParams(vmem_limit_bytes=24 * MIB),
        cost_estimate=pl.CostEstimate(
            flops=2 * WIDE * chips * 64 * depth, bytes_accessed=2 * MIB, transcendentals=0
        ),
        name="sum_terms",
    )(terms, names)


def value_products(tok, tok_in, pieces, hidden, table, start, size):
    rows = tok.shape[0]
    depth = tok.shape[1] * 2 // size
    planes = size // 8
    columns = pieces[0].shape[2]
    own_columns = 2 * depth

    def kernel(tok, tok_in, line, ax, ay, first, last, hidden, table, keep, give):
        core = lax.rem(lax.axis_index("fsdp"), 2)
        for half, (source, out) in enumerate(((tok, keep), (tok_in, give))):
            for m in range(columns // 256):
                here = slice(m * 256, (m + 1) * 256)
                begin = 0
                total = None
                for ref in (line, ax, ay, first, last):
                    deep = ref.shape[0] * depth
                    part = dot(
                        source[:, begin : begin + deep], ref[:, :, here].reshape(deep, 256)
                    )
                    total = part if total is None else total + part
                    begin += deep
                column = start + m * 256
                owner = column // own_columns
                q = (owner // 2 * own_columns + column % own_columns) // 256
                scale = jnp.where(core == owner % 2, SCALE, 0.0).astype(F32)
                extra = dot(hidden[half * rows : (half + 1) * rows], table[q])
                out[:, here] = total + scale * extra

    share = jax.ShapeDtypeStruct((rows, columns), F32)
    return pl.pallas_call(
        kernel,
        out_shape=(share, share),
        in_specs=[VMEM] * 9,
        out_specs=(VMEM, VMEM),
        compiler_params=pltpu.CompilerParams(vmem_limit_bytes=20 * MIB),
        cost_estimate=pl.CostEstimate(
            flops=4 * rows * tok.shape[1] * columns, bytes_accessed=9 * MIB, transcendentals=0
        ),
        name="value_products",
    )(tok, tok_in, *pieces, hidden, table)


def body(
    size,
    tokens,
    frozen_value_weight,
    adapter_down_weight,
    adapter_up_weight,
    block_adapter_index,
    block_valid_length,
    destinations,
    cotangent,
):
    width = frozen_value_weight.shape[1]
    own_columns = adapter_up_weight.shape[1]
    me = lax.axis_index("fsdp")
    core = me % 2
    goes_right = (destinations == me + 1)[:, None, None]
    goes_left = (destinations == me - 1)[:, None, None]
    stays = (destinations == me)[:, None, None]
    valid = (jnp.arange(BLOCK)[None, :] < block_valid_length[:, None])[..., None]
    zero = jnp.zeros((), BF16)

    lane = jnp.arange(WIDE)[None, :]
    meta = jnp.where(lane == me, block_adapter_index[:, None], 0).astype(BF16)
    meta = jnp.concatenate([meta, jnp.zeros((14, WIDE), BF16)])
    ups = [adapter_up_weight[:, q * 256 : (q + 1) * 256] for q in range(own_columns // 256)]
    piece = jnp.concatenate([adapter_down_weight, *ups, meta])
    low_pieces = gather_pieces(piece, size)

    tok, tok_out = split_tokens(tokens, size)
    tok_in = swap(tok_out, size, 1)

    slots = cotangent.reshape(-1, BLOCK, width)
    from_upper = shift(slots[0], size, -1)
    from_lower = shift(slots[-1], size, 1)
    grad = jnp.where(goes_right, from_upper[None], jnp.where(goes_left, from_lower[None], slots[1:-1]))
    grad = jnp.where(valid, grad, zero).reshape(-1, width)
    runs = [grad[:, i : i + own_columns] for i in range(0, width, own_columns)]
    even, odd = jnp.concatenate(runs[0::2], axis=1), jnp.concatenate(runs[1::2], axis=1)
    grad_mine = jnp.where(core == 0, even, odd)
    grad_in = swap(jnp.where(core == 0, odd, even), size, 1)

    share, table = low_rank_products(tok, tok_in, low_pieces, grad_mine, grad_in, size)
    hidden, names, terms = adapter_terms(
        share, swap(share, size, 1), tok, tok_in, grad_mine, grad_in, size, F32
    )
    groups = [list(range(core, size, 2)) for core in range(2)]
    terms = lax.all_to_all(terms, "fsdp", 0, 0, axis_index_groups=groups, tiled=True)
    down_gradient, up_gradient = sum_terms(terms, names, size)

    outs = []
    for start, stop in ((0, 512), (512, 1024)):
        pieces = gather_pieces(frozen_value_weight[:, start:stop], size)
        keep, give = value_products(tok, tok_in, pieces, hidden, table, start, size)
        total = (keep + swap(give, size, 1)).reshape(-1, BLOCK, stop - start)
        value = jnp.where(valid, total, 0.0).astype(BF16)
        right = jnp.sum(jnp.where(goes_right, value, zero), axis=0)
        left = jnp.sum(jnp.where(goes_left, value, zero), axis=0)
        own = jnp.where(stays, value, zero)
        lower, upper = shift(right, size, 1), shift(left, size, -1)
        outs.append(jnp.concatenate([lower[None], own, upper[None]]).reshape(-1, stop - start))
    return jnp.concatenate(outs, axis=1), down_gradient, up_gradient


def solution(mesh):
    rows = P(("groups", "fsdp"), None)
    vector = P(("groups", "fsdp"))
    in_specs = (rows, P("fsdp", None), rows, P("groups", "fsdp"), vector, vector, vector, rows)
    out_specs = (rows, rows, P("groups", "fsdp"))
    return jax.shard_map(
        functools.partial(body, mesh.shape["fsdp"]),
        mesh=mesh,
        in_specs=in_specs,
        out_specs=out_specs,
        check_vma=False,
    )
```

time: 560 us -> 319 us (0.57)
  waiting for transfers between devices: 341 us -> 115 us
  Pallas kernels: 0 us -> 148 us
  blocking collectives: 94.8 us -> 0 us
  other arithmetic: 36 us -> 5.08 us
  matrix products: 29.8 us -> 0 us
  starting transfers between devices: 10.2 us -> 37.6 us
  local copies, waits for them, and re-layouts: 28.9 us -> 7.67 us
  between operations: 19 us -> 1.05 us
    reduce_scatter x2 -> x0, waiting for transfers between devices: 273 us -> none  [the longest x1 142 us: backward(): lax.psum_scatter(ADAPTER_SCALE * summed_output.reshape(lax.axis_size('fsd...]
    pallas_call x0 -> x6, Pallas kernels: none -> 148 us  [the longest x1 128 us: split_tokens(): pl.pallas_call(kernel, out_shape=(half, half), in_specs=[ANY], out_specs=...]
    ppermute x4 -> x32, waiting for transfers between devices: 0.01 us -> 115 us  [the longest x26 112 us: send_to(): return lax.ppermute(x, 'fsdp', [(i, target(i)) for i in range(size)])]
    all_gather x1 -> x0, blocking collectives: 94.8 us -> none  [body(): lax.all_gather(adapter_up_weight, 'fsdp', axis=1, tiled=True)]
    all_gather x2 -> x0, waiting for transfers between devices: 65.9 us -> none  [the longest x1 49.5 us: frozen_products(): lax.all_gather(adapter_down_weight, 'fsdp', axis=0, tiled=True)]
    dot_general x6 -> x0, matrix products: 29.8 us -> none  [the longest x3 22.5 us: frozen_products(): jnp.dot(source, weight, preferred_element_type=jnp.float32)]
    ppermute x4 -> x32, starting transfers between devices: 10 us -> 33.2 us  [the longest x26 19.5 us: send_to(): return lax.ppermute(x, 'fsdp', [(i, target(i)) for i in range(size)])]
    unnamed x20 -> x22, local copies, waits for them, and re-layouts: 18.7 us -> 1.23 us
  transfers between devices with their start and end apart: 8 -> 33, of which waited for: 4 -> 20; matrix products, arithmetic and copies ran while one was open for 7% -> 4% of each run, Pallas kernels for 0% -> 5%
where the time goes in v1:
time: 319 us; the launch traced here: 315 us
  Pallas kernels  148 us (46%)
  waiting for transfers between devices  115 us (36%)
  starting transfers between devices  37.6 us (12%)
  local copies, waits for them, and re-layouts  7.67 us (2%)
  other arithmetic  5.08 us (2%)
    pallas_call x1, Pallas kernels, split_tokens(): pl.pallas_call(kernel, out_shape=(half, half), in_specs=[ANY], out_specs=...  128 us
    ppermute x26, waiting for transfers between devices, send_to(): return lax.ppermute(x, 'fsdp', [(i, target(i)) for i in range(size)])  112 us
    ppermute x26, starting transfers between devices, send_to(): return lax.ppermute(x, 'fsdp', [(i, target(i)) for i in range(size)])  19.5 us
    ppermute x6, starting transfers between devices, shift(): return lax.ppermute(x, 'fsdp', pairs)  13.7 us
    pallas_call x2, Pallas kernels, value_products(): pl.pallas_call(kernel, out_shape=(share, share), in_specs=[VMEM] * 9, out...  9.59 us
  transfers between devices with their start and end apart: 33, of which 20 were waited for; matrix products, arithmetic and copies ran while one was open for 4% of the time, Pallas kernels for 5%

profile of v1, /device:TPU:0, one launch (start us, length us, event | category | flops | bytes accessed | tf_op | source)
XLA Modules:
  0.0 314.7 jit_solution(4152780434644967084)
XLA Ops:
  0.7 128.5 %split_tokens.1 = (bf16[256,4096]{1,0:T(8,128)(2,1)}, bf16[256,4096]{1,0:T(8,128)(2,1)}) custom-call(bf16[256,8192]{1,0:T(8,128)(2,1)} %tok.1), custom_call_target="tpu_custom_call" | custom-call | tf_op jit(solution)/shard_map/split_tokens/pallas_call | solution.py:89
  129.2 0.5 collective-permute-start
  129.8 0.1 concatenate.12
  130.0 2.7 collective-permute-start.8
  132.6 6.7 %collective-permute-done.8 = bf16[304,256]{1,0:T(8,128)(2,1)S(1)} collective-permute-done((bf16[304,256]{1,0:T(8,128)(2,1)S(1)}, bf16[304,256]{1,0:T(8,128)(2,1)S(1)}, u32[]{:S(2)}, u32[]{:S(2)}) %collective-permute-start.8) | collective-permute-done | bytes 155680 | tf_op jit(solution)/shard_map/ppermute | solution.py:23
  139.3 0.8 fusion.3
  140.1 1.3 collective-permute-start.15
  141.4 3.7 %collective-permute-start.16 = (bf16[128,1024]{1,0:T(8,128)(2,1)}, bf16[128,1024]{1,0:T(8,128)(2,1)}, u32[]{:S(2)}, u32[]{:S(2)}) collective-permute-start(bf16[128,1024]{1,0:T(8,128)(2,1)} %get-tuple-element.40), channel_id=1, source_target_pairs={{0,1},{1,2},{2,3},{3,4},{4,5},{5,6},{6,7},{7,8},{8,9},{9,10},{10,1... | collective-permute-start | bytes 786440 | tf_op jit(solution)/shard_map/ppermute | solution.py:36
  145.2 1.8 collective-permute-done.9
  146.9 0.4 collective-permute-start.10
  147.3 7.2 %collective-permute-done.10 = bf16[304,256]{1,0:T(8,128)(2,1)S(1)} collective-permute-done((bf16[304,256]{1,0:T(8,128)(2,1)S(1)}, bf16[304,256]{1,0:T(8,128)(2,1)S(1)}, u32[]{:S(2)}, u32[]{:S(2)}) %collective-permute-start.10) | collective-permute-done | bytes 155680 | tf_op jit(solution)/shard_map/ppermute | solution.py:23
  154.7 1.2 collective-permute-start.11
  155.8 2.4 collective-permute-start.12
  158.6 1.5 fusion.1
  160.1 9.6 %collective-permute-done.11.ax = bf16[4,304,256]{2,1,0:T(8,128)(2,1)S(1)} collective-permute-done((bf16[4,304,256]{2,1,0:T(8,128)(2,1)S(1)}, bf16[4,304,256]{2,1,0:T(8,128)(2,1)S(1)}, u32[]{:S(2)}, u32[]{:S(2)}) %collective-permute-start.11) | collective-permute-done | bytes 622624 | tf_op jit(solution)/shard_map/ppermute | solution.py:23
  169.7 2.6 collective-permute-start.13
  172.3 1.0 slice.66
  173.3 1.8 collective-permute-start.14
  175.3 1.4 collective-permute-done.17.grad_in
  176.7 2.4 collective-permute-done.13.first
  179.1 2.5 collective-permute-done.14.last
  181.6 3.2 %low_rank_products.1 = (f32[1040,256]{1,0:T(8,128)S(1)}, bf16[2,256,256]{2,1,0:T(8,128)(2,1)S(1)}) custom-call(bf16[256,4096]{1,0:T(8,128)(2,1)S(1)} %copy-done, bf16[256,4096]{1,0:T(8,128)(2,1)} %collective-permute-done.tok_in, bf16[4,304,256]{2,1,0:T(8,128)(2,1)S(1)} %pad_maximum_fusion.3.line, bf16[4,304,256]{2,1,0:T(8,128)(2,1)S(1)} %collective-permute-done.11.ax, ...), custom_call_target="tpu_custom_call" | custom-call | flops 1207959552 | bytes 9437184 | tf_op jit(solution)/shard_map/low_rank_products/pallas_call | solution.py:146
  184.9 1.2 collective-permute-done.1
  186.2 5.6 %collective-permute-done.23 = bf16[256,512]{1,0:T(8,128)(2,1)S(1)} collective-permute-done((bf16[256,512]{1,0:T(8,128)(2,1)S(1)}, bf16[256,512]{1,0:T(8,128)(2,1)S(1)}, u32[]{:S(2)}, u32[]{:S(2)}) %collective-permute-start.23) | collective-permute-done | bytes 262176 | tf_op jit(solution)/shard_map/ppermute | solution.py:23
  191.8 5.6 %collective-permute-done.2 = bf16[256,512]{1,0:T(8,128)(2,1)S(1)} collective-permute-done((bf16[256,512]{1,0:T(8,128)(2,1)S(1)}, bf16[256,512]{1,0:T(8,128)(2,1)S(1)}, u32[]{:S(2)}, u32[]{:S(2)}) %collective-permute-start.2) | collective-permute-done | bytes 262176 | tf_op jit(solution)/shard_map/ppermute | solution.py:23
  197.4 5.6 %collective-permute-done.24 = bf16[256,512]{1,0:T(8,128)(2,1)S(1)} collective-permute-done((bf16[256,512]{1,0:T(8,128)(2,1)S(1)}, bf16[256,512]{1,0:T(8,128)(2,1)S(1)}, u32[]{:S(2)}, u32[]{:S(2)}) %collective-permute-start.24) | collective-permute-done | bytes 262176 | tf_op jit(solution)/shard_map/ppermute | solution.py:23
  203.0 1.1 pad_maximum_fusion.1.line
  204.1 0.1 collective-permute-start.25
  204.2 1.7 collective-permute-start.26
  205.9 2.3 collective-permute-done.3
  208.2 0.1 pad_maximum_fusion.line
  208.3 0.4 collective-permute-start.4
  208.7 1.5 collective-permute-start.5
  210.2 3.0 adapter_terms.1
  213.2 1.2 copy-done.1
  214.4 4.4 %all-to-all-start = ((f32[16,96,256]{2,1,0:T(8,128)}), f32[16,96,256]{2,1,0:T(8,128)}, u32[]{:S(2)}, u32[]{:S(2)}) async-start(f32[16,96,256]{2,1,0:T(8,128)} %copy-done.1), calls=%async_computation | async-start | bytes 3145728 | tf_op jit(solution)/shard_map/all_to_all | solution.py:356
  218.8 12.1 %collective-permute-done.25.ax = bf16[4,256,512]{2,1,0:T(8,128)(2,1)} collective-permute-done((bf16[4,256,512]{2,1,0:T(8,128)(2,1)}, bf16[4,256,512]{2,1,0:T(8,128)(2,1)}, u32[]{:S(2)}, u32[]{:S(2)}) %collective-permute-start.25) | collective-permute-done | bytes 1048608 | tf_op jit(solution)/shard_map/ppermute | solution.py:23
  230.9 1.1 slice.69
  232.0 0.4 collective-permute-start.27
  232.3 6.3 %collective-permute-done.26.ay = bf16[4,256,512]{2,1,0:T(8,128)(2,1)} collective-permute-done((bf16[4,256,512]{2,1,0:T(8,128)(2,1)}, bf16[4,256,512]{2,1,0:T(8,128)(2,1)}, u32[]{:S(2)}, u32[]{:S(2)}) %collective-permute-start.26) | collective-permute-done | bytes 1048608 | tf_op jit(solution)/shard_map/ppermute | solution.py:23
  238.6 1.1 slice.70
  239.7 2.4 collective-permute-start.28
  242.1 23.5 %collective-permute-done.4.ax = bf16[4,256,512]{2,1,0:T(8,128)(2,1)} collective-permute-done((bf16[4,256,512]{2,1,0:T(8,128)(2,1)S(1)}, bf16[4,256,512]{2,1,0:T(8,128)(2,1)}, u32[]{:S(2)}, u32[]{:S(2)}) %collective-permute-start.4) | collective-permute-done | bytes 1048608 | tf_op jit(solution)/shard_map/ppermute | solution.py:23
  265.7 1.1 slice.63
  266.7 0.2 collective-permute-start.6
  266.9 1.0 collective-permute-done.5.ay
  267.8 1.1 slice.64
  268.9 1.0 collective-permute-start.7
  269.9 11.2 %collective-permute-done.27.first = bf16[2,256,512]{2,1,0:T(8,128)(2,1)S(1)} collective-permute-done((bf16[2,256,512]{2,1,0:T(8,128)(2,1)S(1)}, bf16[2,256,512]{2,1,0:T(8,128)(2,1)S(1)}, u32[]{:S(2)}, u32[]{:S(2)}) %collective-permute-start.27) | collective-permute-done | bytes 524320 | tf_op jit(solution)/shard_map/ppermute | solution.py:23
  281.1 5.0 %value_products.3 = (f32[256,512]{1,0:T(8,128)S(1)}, f32[256,512]{1,0:T(8,128)S(1)}) custom-call(bf16[256,4096]{1,0:T(8,128)(2,1)S(1)} %copy-done, bf16[256,4096]{1,0:T(8,128)(2,1)} %collective-permute-done.tok_in, bf16[4,256,512]{2,1,0:T(8,128)(2,1)} %pad_maximum_fusion.1.line, bf16[4,256,512]{2,1,0:T(8,128)(2,1)} %collective-permute-done.25.ax, ...), custom_call_target="tpu_custom_call" | custom-call | flops 2147483648 | bytes 9437184 | tf_op jit(solution)/shard_map/value_products/pallas_call | solution.py:297
  286.1 4.5 %collective-permute-done.6.first = bf16[2,256,512]{2,1,0:T(8,128)(2,1)S(1)} collective-permute-done((bf16[2,256,512]{2,1,0:T(8,128)(2,1)S(1)}, bf16[2,256,512]{2,1,0:T(8,128)(2,1)S(1)}, u32[]{:S(2)}, u32[]{:S(2)}) %collective-permute-start.6) | collective-permute-done | bytes 524320 | tf_op jit(solution)/shard_map/ppermute | solution.py:23
  290.6 4.6 %value_products.2 = (f32[256,512]{1,0:T(8,128)S(1)}, f32[256,512]{1,0:T(8,128)S(1)}) custom-call(bf16[256,4096]{1,0:T(8,128)(2,1)S(1)} %copy-done, bf16[256,4096]{1,0:T(8,128)(2,1)} %collective-permute-done.tok_in, bf16[4,256,512]{2,1,0:T(8,128)(2,1)S(1)} %pad_maximum_fusion.line, bf16[4,256,512]{2,1,0:T(8,128)(2,1)} %collective-permute-done.4.ax, ...), custom_call_target="tpu_custom_call" | custom-call | flops 2147483648 | bytes 9437184 | tf_op jit(solution)/shard_map/value_products/pallas_call | solution.py:297
  295.3 0.1 add.17
  295.4 1.8 collective-permute-done.19
  297.2 0.1 add.16
  297.3 0.3 broadcast_select_fusion.1
  297.6 0.4 select_reduce_fusion.1
  298.0 2.0 collective-permute-start.20
  300.0 1.3 collective-permute-start.21
  301.3 4.1 %collective-permute-start.30 = (bf16[128,512]{1,0:T(8,128)(2,1)S(1)}, bf16[128,512]{1,0:T(8,128)(2,1)S(1)}, u32[]{:S(2)}, u32[]{:S(2)}) collective-permute-start(bf16[128,512]{1,0:T(8,128)(2,1)S(1)} %get-tuple-element.31), channel_id=1, source_target_pairs={{0,1},{1,2},{2,3},{3,4},{4,5},{5,6},{6,7},{7,8},{8,9},{9,10},{10,1... | collective-permute-start | bytes 393224 | tf_op jit(solution)/shard_map/ppermute | solution.py:36
  305.4 1.3 collective-permute-start.31
  306.8 3.1 collective-permute-done.31
  309.9 1.1 pad_maximum_fusion.2
  311.0 3.7 %sum_terms.1 = (f32[256,256]{1,0:T(8,128)}, f32[16,512]{1,0:T(8,128)}) custom-call(f32[16,96,256]{2,1,0:T(8,128)} %all-to-all-done.terms, f32[16,256]{1,0:T(8,128)S(1)} %get-tuple-element.26.names), custom_call_target="tpu_custom_call" | custom-call | flops 134217728 | bytes 2097152 | tf_op jit(solution)/shard_map/sum_terms/pallas_call | solution.py:252
  (58 shorter events, 1.1 us)
Async XLA Ops:
  0.6 129.1 %copy-start.7 = (bf16[16,512]{1,0:T(8,128)(2,1)S(1)}, bf16[16,512]{1,0:T(8,128)(2,1)}, u32[]{:S(2)}) copy-start(bf16[16,512]{1,0:T(8,128)(2,1)} %param.11) | copy-start | bytes 49156
  0.6 129.1 %copy-start.9 = (s32[2]{0:T(128)S(1)}, s32[2]{0:T(128)}, u32[]{:S(2)}) copy-start(s32[2]{0:T(128)} %param.12) | copy-start | bytes 28
  0.7 129.2 %copy-start.6 = (bf16[256,256]{1,0:T(8,128)(2,1)S(1)}, bf16[256,256]{1,0:T(8,128)(2,1)}, u32[]{:S(2)}) copy-start(bf16[256,256]{1,0:T(8,128)(2,1)} %param.10) | copy-start | bytes 393220
  0.7 138.7 %copy-start.4 = (bf16[512,1024]{1,0:T(8,128)(2,1)S(1)}, bf16[512,1024]{1,0:T(8,128)(2,1)}, u32[]{:S(2)}) copy-start(bf16[512,1024]{1,0:T(8,128)(2,1)} %param.15) | copy-start | bytes 3145732
  0.7 146.7 %copy-start.8 = (s32[2]{0:T(128)S(1)}, s32[2]{0:T(128)}, u32[]{:S(2)}) copy-start(s32[2]{0:T(128)} %param.14) | copy-start | bytes 28
  129.2 29.1 %copy-start.10 = (s32[2]{0:T(128)S(1)}, s32[2]{0:T(128)}, u32[]{:S(2)}) copy-start(s32[2]{0:T(128)} %param.13) | copy-start | bytes 28
  129.2 29.2 %copy-start.5 = (bf16[256,1024]{1,0:T(8,128)(2,1)S(1)}, bf16[256,1024]{1,0:T(8,128)(2,1)}, u32[]{:S(2)}) copy-start(bf16[256,1024]{1,0:T(8,128)(2,1)} %param.9) | copy-start | bytes 1572868
  129.2 52.4 %collective-permute-start = (bf16[256,4096]{1,0:T(8,128)(2,1)}, bf16[256,4096]{1,0:T(8,128)(2,1)}, u32[]{:S(2)}, u32[]{:S(2)}) collective-permute-start(bf16[256,4096]{1,0:T(8,128)(2,1)} %get-tuple-element.17), channel_id=1, source_target_pairs={{0,1},{1,0},{2,3},{3,2},{4,5},{5,4},{6,7},{7,6},{8,9},{9,8},{10,11... | collective-permute-start | bytes 6291464 | tf_op jit(solution)/shard_map/ppermute | solution.py:23
  130.0 9.3 %collective-permute-start.8 = (bf16[304,256]{1,0:T(8,128)(2,1)S(1)}, bf16[304,256]{1,0:T(8,128)(2,1)S(1)}, u32[]{:S(2)}, u32[]{:S(2)}) collective-permute-start(bf16[304,256]{1,0:T(8,128)(2,1)S(1)} %concatenate.12), channel_id=1, source_target_pairs={{0,8},{1,9},{2,10},{3,11},{4,12},{5,13},{6,14},{7,15},{8,16},{9,17... | collective-permute-start | bytes 466952 | tf_op jit(solution)/shard_map/ppermute | solution.py:23
  139.3 7.6 %collective-permute-start.9 = (bf16[304,256]{1,0:T(8,128)(2,1)S(1)}, bf16[304,256]{1,0:T(8,128)(2,1)S(1)}, u32[]{:S(2)}, u32[]{:S(2)}) collective-permute-start(bf16[304,256]{1,0:T(8,128)(2,1)S(1)} %collective-permute-done.8), channel_id=1, source_target_pairs={{0,8},{1,9},{2,10},{3,11},{4,12},{5,13},{6,14},{7,15},{8,16},{9,17... | collective-permute-start | bytes 466952 | tf_op jit(solution)/shard_map/ppermute | solution.py:23
  140.1 18.3 %collective-permute-start.15 = (bf16[128,1024]{1,0:T(8,128)(2,1)}, bf16[128,1024]{1,0:T(8,128)(2,1)}, u32[]{:S(2)}, u32[]{:S(2)}) collective-permute-start(bf16[128,1024]{1,0:T(8,128)(2,1)} %get-tuple-element.39), channel_id=1, source_target_pairs={{1,0},{2,1},{3,2},{4,3},{5,4},{6,5},{7,6},{8,7},{9,8},{10,9},{11,1... | collective-permute-start | bytes 786440 | tf_op jit(solution)/shard_map/ppermute | solution.py:36
  141.4 17.1 %collective-permute-start.16 = (bf16[128,1024]{1,0:T(8,128)(2,1)}, bf16[128,1024]{1,0:T(8,128)(2,1)}, u32[]{:S(2)}, u32[]{:S(2)}) collective-permute-start(bf16[128,1024]{1,0:T(8,128)(2,1)} %get-tuple-element.40), channel_id=1, source_target_pairs={{0,1},{1,2},{2,3},{3,4},{4,5},{5,6},{6,7},{7,8},{8,9},{9,10},{10,1... | collective-permute-start | bytes 786440 | tf_op jit(solution)/shard_map/ppermute | solution.py:36
  146.9 7.6 %collective-permute-start.10 = (bf16[304,256]{1,0:T(8,128)(2,1)S(1)}, bf16[304,256]{1,0:T(8,128)(2,1)S(1)}, u32[]{:S(2)}, u32[]{:S(2)}) collective-permute-start(bf16[304,256]{1,0:T(8,128)(2,1)S(1)} %collective-permute-done.9), channel_id=1, source_target_pairs={{0,8},{1,9},{2,10},{3,11},{4,12},{5,13},{6,14},{7,15},{8,16},{9,17... | collective-permute-start | bytes 466952 | tf_op jit(solution)/shard_map/ppermute | solution.py:23
  154.7 15.0 %collective-permute-start.11 = (bf16[4,304,256]{2,1,0:T(8,128)(2,1)S(1)}, bf16[4,304,256]{2,1,0:T(8,128)(2,1)S(1)}, u32[]{:S(2)}, u32[]{:S(2)}) collective-permute-start(bf16[4,304,256]{2,1,0:T(8,128)(2,1)S(1)} %pad_maximum_fusion.3.line), channel_id=1, source_target_pairs={{0,2},{1,3},{2,0},{3,1},{4,6},{5,7},{6,4},{7,5},{8,10},{9,11},{10,... | collective-permute-start | bytes 1867784 | tf_op jit(solution)/shard_map/ppermute | solution.py:23
  155.8 16.5 %collective-permute-start.12 = (bf16[4,304,256]{2,1,0:T(8,128)(2,1)S(1)}, bf16[4,304,256]{2,1,0:T(8,128)(2,1)}, u32[]{:S(2)}, u32[]{:S(2)}) collective-permute-start(bf16[4,304,256]{2,1,0:T(8,128)(2,1)S(1)} %pad_maximum_fusion.3.line), channel_id=1, source_target_pairs={{0,4},{1,5},{2,6},{3,7},{4,0},{5,1},{6,2},{7,3},{8,12},{9,13},{10,... | collective-permute-start | bytes 1867784 | tf_op jit(solution)/shard_map/ppermute | solution.py:23
  158.5 23.2 %copy-start = (bf16[256,4096]{1,0:T(8,128)(2,1)S(1)}, bf16[256,4096]{1,0:T(8,128)(2,1)}, u32[]{:S(2)}) copy-start(bf16[256,4096]{1,0:T(8,128)(2,1)} %get-tuple-element.16.tok) | copy-start | bytes 6291460
  158.5 16.7 %collective-permute-start.22 = (bf16[256,512]{1,0:T(8,128)(2,1)S(1)}, bf16[256,512]{1,0:T(8,128)(2,1)S(1)}, u32[]{:S(2)}, u32[]{:S(2)}) collective-permute-start(bf16[256,512]{1,0:T(8,128)(2,1)S(1)} %get-tuple-element.43), channel_id=1, source_target_pairs={{0,8},{1,9},{2,10},{3,11},{4,12},{5,13},{6,14},{7,15},{8,16},{9,17... | collective-permute-start | bytes 786440 | tf_op jit(solution)/shard_map/ppermute | solution.py:23
  169.7 9.4 %collective-permute-start.13 = (bf16[2,304,256]{2,1,0:T(8,128)(2,1)S(1)}, bf16[2,304,256]{2,1,0:T(8,128)(2,1)S(1)}, u32[]{:S(2)}, u32[]{:S(2)}) collective-permute-start(bf16[2,304,256]{2,1,0:T(8,128)(2,1)S(1)} %slice.65), channel_id=1, source_target_pairs={{0,4},{1,5},{2,6},{3,7},{4,0},{5,1},{6,2},{7,3},{8,12},{9,13},{10,... | collective-permute-start | bytes 933896 | tf_op jit(solution)/shard_map/ppermute | solution.py:23
  173.3 8.4 %collective-permute-start.14 = (bf16[2,304,256]{2,1,0:T(8,128)(2,1)S(1)}, bf16[2,304,256]{2,1,0:T(8,128)(2,1)S(1)}, u32[]{:S(2)}, u32[]{:S(2)}) collective-permute-start(bf16[2,304,256]{2,1,0:T(8,128)(2,1)S(1)} %slice.66), channel_id=1, source_target_pairs={{0,2},{1,3},{2,0},{3,1},{4,6},{5,7},{6,4},{7,5},{8,10},{9,11},{10,... | collective-permute-start | bytes 933896 | tf_op jit(solution)/shard_map/ppermute | solution.py:23
  175.1 1.6 collective-permute-start.17
  175.2 11.0 %collective-permute-start.1 = (bf16[256,512]{1,0:T(8,128)(2,1)S(1)}, bf16[256,512]{1,0:T(8,128)(2,1)S(1)}, u32[]{:S(2)}, u32[]{:S(2)}) collective-permute-start(bf16[256,512]{1,0:T(8,128)(2,1)S(1)} %get-tuple-element.44), channel_id=1, source_target_pairs={{0,8},{1,9},{2,10},{3,11},{4,12},{5,13},{6,14},{7,15},{8,16},{9,17... | collective-permute-start | bytes 786440 | tf_op jit(solution)/shard_map/ppermute | solution.py:23
  176.7 15.1 %collective-permute-start.23 = (bf16[256,512]{1,0:T(8,128)(2,1)S(1)}, bf16[256,512]{1,0:T(8,128)(2,1)S(1)}, u32[]{:S(2)}, u32[]{:S(2)}) collective-permute-start(bf16[256,512]{1,0:T(8,128)(2,1)S(1)} %collective-permute-done.22), channel_id=1, source_target_pairs={{0,8},{1,9},{2,10},{3,11},{4,12},{5,13},{6,14},{7,15},{8,16},{9,17... | collective-permute-start | bytes 786440 | tf_op jit(solution)/shard_map/ppermute | solution.py:23
  184.9 23.5 %copy-start.2 = (bf16[2,256,256]{2,1,0:T(8,128)(2,1)}, bf16[2,256,256]{2,1,0:T(8,128)(2,1)S(1)}, u32[]{:S(2)}) copy-start(bf16[2,256,256]{2,1,0:T(8,128)(2,1)S(1)} %get-tuple-element.20.table) | copy-start | bytes 786436
  184.9 25.3 %collective-permute-start.18 = (f32[1040,256]{1,0:T(8,128)S(1)}, f32[1040,256]{1,0:T(8,128)S(1)}, u32[]{:S(2)}, u32[]{:S(2)}) collective-permute-start(f32[1040,256]{1,0:T(8,128)S(1)} %get-tuple-element.18.own), channel_id=1, source_target_pairs={{0,1},{1,0},{2,3},{3,2},{4,5},{5,4},{6,7},{7,6},{8,9},{9,8},{10,11... | collective-permute-start | bytes 3194888 | tf_op jit(solution)/shard_map/ppermute | solution.py:23
  186.2 11.2 %collective-permute-start.2 = (bf16[256,512]{1,0:T(8,128)(2,1)S(1)}, bf16[256,512]{1,0:T(8,128)(2,1)S(1)}, u32[]{:S(2)}, u32[]{:S(2)}) collective-permute-start(bf16[256,512]{1,0:T(8,128)(2,1)S(1)} %collective-permute-done.1), channel_id=1, source_target_pairs={{0,8},{1,9},{2,10},{3,11},{4,12},{5,13},{6,14},{7,15},{8,16},{9,17... | collective-permute-start | bytes 786440 | tf_op jit(solution)/shard_map/ppermute | solution.py:23
  191.8 11.2 %collective-permute-start.24 = (bf16[256,512]{1,0:T(8,128)(2,1)S(1)}, bf16[256,512]{1,0:T(8,128)(2,1)S(1)}, u32[]{:S(2)}, u32[]{:S(2)}) collective-permute-start(bf16[256,512]{1,0:T(8,128)(2,1)S(1)} %collective-permute-done.23), channel_id=1, source_target_pairs={{0,8},{1,9},{2,10},{3,11},{4,12},{5,13},{6,14},{7,15},{8,16},{9,17... | collective-permute-start | bytes 786440 | tf_op jit(solution)/shard_map/ppermute | solution.py:23
  197.4 10.8 %collective-permute-start.3 = (bf16[256,512]{1,0:T(8,128)(2,1)S(1)}, bf16[256,512]{1,0:T(8,128)(2,1)S(1)}, u32[]{:S(2)}, u32[]{:S(2)}) collective-permute-start(bf16[256,512]{1,0:T(8,128)(2,1)S(1)} %collective-permute-done.2), channel_id=1, source_target_pairs={{0,8},{1,9},{2,10},{3,11},{4,12},{5,13},{6,14},{7,15},{8,16},{9,17... | collective-permute-start | bytes 786440 | tf_op jit(solution)/shard_map/ppermute | solution.py:23
  204.1 26.7 %collective-permute-start.25 = (bf16[4,256,512]{2,1,0:T(8,128)(2,1)}, bf16[4,256,512]{2,1,0:T(8,128)(2,1)}, u32[]{:S(2)}, u32[]{:S(2)}) collective-permute-start(bf16[4,256,512]{2,1,0:T(8,128)(2,1)} %pad_maximum_fusion.1.line), channel_id=1, source_target_pairs={{0,2},{1,3},{2,0},{3,1},{4,6},{5,7},{6,4},{7,5},{8,10},{9,11},{10,... | collective-permute-start | bytes 3145736 | tf_op jit(solution)/shard_map/ppermute | solution.py:23
  204.2 34.4 %collective-permute-start.26 = (bf16[4,256,512]{2,1,0:T(8,128)(2,1)}, bf16[4,256,512]{2,1,0:T(8,128)(2,1)}, u32[]{:S(2)}, u32[]{:S(2)}) collective-permute-start(bf16[4,256,512]{2,1,0:T(8,128)(2,1)} %pad_maximum_fusion.1.line), channel_id=1, source_target_pairs={{0,4},{1,5},{2,6},{3,7},{4,0},{5,1},{6,2},{7,3},{8,12},{9,13},{10,... | collective-permute-start | bytes 3145736 | tf_op jit(solution)/shard_map/ppermute | solution.py:23
  208.3 57.3 %collective-permute-start.4 = (bf16[4,256,512]{2,1,0:T(8,128)(2,1)S(1)}, bf16[4,256,512]{2,1,0:T(8,128)(2,1)}, u32[]{:S(2)}, u32[]{:S(2)}) collective-permute-start(bf16[4,256,512]{2,1,0:T(8,128)(2,1)S(1)} %pad_maximum_fusion.line), channel_id=1, source_target_pairs={{0,2},{1,3},{2,0},{3,1},{4,6},{5,7},{6,4},{7,5},{8,10},{9,11},{10,... | collective-permute-start | bytes 3145736 | tf_op jit(solution)/shard_map/ppermute | solution.py:23
  208.7 59.2 %collective-permute-start.5 = (bf16[4,256,512]{2,1,0:T(8,128)(2,1)S(1)}, bf16[4,256,512]{2,1,0:T(8,128)(2,1)}, u32[]{:S(2)}, u32[]{:S(2)}) collective-permute-start(bf16[4,256,512]{2,1,0:T(8,128)(2,1)S(1)} %pad_maximum_fusion.line), channel_id=1, source_target_pairs={{0,4},{1,5},{2,6},{3,7},{4,0},{5,1},{6,2},{7,3},{8,12},{9,13},{10,... | collective-permute-start | bytes 3145736 | tf_op jit(solution)/shard_map/ppermute | solution.py:23
  213.2 1.2 copy-start.1
  214.4 96.7 %all-to-all-start = ((f32[16,96,256]{2,1,0:T(8,128)}), f32[16,96,256]{2,1,0:T(8,128)}, u32[]{:S(2)}, u32[]{:S(2)}) async-start(f32[16,96,256]{2,1,0:T(8,128)} %copy-done.1), calls=%async_computation | async-start | bytes 3145728 | tf_op jit(solution)/shard_map/all_to_all | solution.py:356
  218.8 62.3 %copy-start.3 = (bf16[2,256,256]{2,1,0:T(8,128)(2,1)S(1)}, bf16[2,256,256]{2,1,0:T(8,128)(2,1)}, u32[]{:S(2)}) copy-start(bf16[2,256,256]{2,1,0:T(8,128)(2,1)} %copy-done.2) | copy-start | bytes 786436
  232.0 49.1 %collective-permute-start.27 = (bf16[2,256,512]{2,1,0:T(8,128)(2,1)S(1)}, bf16[2,256,512]{2,1,0:T(8,128)(2,1)S(1)}, u32[]{:S(2)}, u32[]{:S(2)}) collective-permute-start(bf16[2,256,512]{2,1,0:T(8,128)(2,1)S(1)} %slice.69), channel_id=1, source_target_pairs={{0,4},{1,5},{2,6},{3,7},{4,0},{5,1},{6,2},{7,3},{8,12},{9,13},{10,... | collective-permute-start | bytes 1572872 | tf_op jit(solution)/shard_map/ppermute | solution.py:23
  239.7 41.4 %collective-permute-start.28 = (bf16[2,256,512]{2,1,0:T(8,128)(2,1)S(1)}, bf16[2,256,512]{2,1,0:T(8,128)(2,1)S(1)}, u32[]{:S(2)}, u32[]{:S(2)}) collective-permute-start(bf16[2,256,512]{2,1,0:T(8,128)(2,1)S(1)} %slice.70), channel_id=1, source_target_pairs={{0,2},{1,3},{2,0},{3,1},{4,6},{5,7},{6,4},{7,5},{8,10},{9,11},{10,... | collective-permute-start | bytes 1572872 | tf_op jit(solution)/shard_map/ppermute | solution.py:23
  266.7 23.9 %collective-permute-start.6 = (bf16[2,256,512]{2,1,0:T(8,128)(2,1)S(1)}, bf16[2,256,512]{2,1,0:T(8,128)(2,1)S(1)}, u32[]{:S(2)}, u32[]{:S(2)}) collective-permute-start(bf16[2,256,512]{2,1,0:T(8,128)(2,1)S(1)} %slice.63), channel_id=1, source_target_pairs={{0,4},{1,5},{2,6},{3,7},{4,0},{5,1},{6,2},{7,3},{8,12},{9,13},{10,... | collective-permute-start | bytes 1572872 | tf_op jit(solution)/shard_map/ppermute | solution.py:23
  268.9 21.7 %collective-permute-start.7 = (bf16[2,256,512]{2,1,0:T(8,128)(2,1)S(1)}, bf16[2,256,512]{2,1,0:T(8,128)(2,1)S(1)}, u32[]{:S(2)}, u32[]{:S(2)}) collective-permute-start(bf16[2,256,512]{2,1,0:T(8,128)(2,1)S(1)} %slice.64), channel_id=1, source_target_pairs={{0,2},{1,3},{2,0},{3,1},{4,6},{5,7},{6,4},{7,5},{8,10},{9,11},{10,... | collective-permute-start | bytes 1572872 | tf_op jit(solution)/shard_map/ppermute | solution.py:23
  286.0 9.3 %collective-permute-start.29 = (f32[256,512]{1,0:T(8,128)S(1)}, f32[256,512]{1,0:T(8,128)S(1)}, u32[]{:S(2)}, u32[]{:S(2)}) collective-permute-start(f32[256,512]{1,0:T(8,128)S(1)} %get-tuple-element.24), channel_id=1, source_target_pairs={{0,1},{1,0},{2,3},{3,2},{4,5},{5,4},{6,7},{7,6},{8,9},{9,8},{10,11... | collective-permute-start | bytes 1572872 | tf_op jit(solution)/shard_map/ppermute | solution.py:23
  295.2 2.0 collective-permute-start.19
  298.0 8.7 %collective-permute-start.20 = (bf16[128,512]{1,0:T(8,128)(2,1)S(1)}, bf16[128,512]{1,0:T(8,128)(2,1)S(1)}, u32[]{:S(2)}, u32[]{:S(2)}) collective-permute-start(bf16[128,512]{1,0:T(8,128)(2,1)S(1)} %get-tuple-element.34), channel_id=1, source_target_pairs={{0,1},{1,2},{2,3},{3,4},{4,5},{5,6},{6,7},{7,8},{8,9},{9,10},{10,1... | collective-permute-start | bytes 393224 | tf_op jit(solution)/shard_map/ppermute | solution.py:36
  300.0 6.7 %collective-permute-start.21 = (bf16[128,512]{1,0:T(8,128)(2,1)S(1)}, bf16[128,512]{1,0:T(8,128)(2,1)S(1)}, u32[]{:S(2)}, u32[]{:S(2)}) collective-permute-start(bf16[128,512]{1,0:T(8,128)(2,1)S(1)} %get-tuple-element.33), channel_id=1, source_target_pairs={{1,0},{2,1},{3,2},{4,3},{5,4},{6,5},{7,6},{8,7},{9,8},{10,9},{11,1... | collective-permute-start | bytes 393224 | tf_op jit(solution)/shard_map/ppermute | solution.py:36
  301.3 5.5 %collective-permute-start.30 = (bf16[128,512]{1,0:T(8,128)(2,1)S(1)}, bf16[128,512]{1,0:T(8,128)(2,1)S(1)}, u32[]{:S(2)}, u32[]{:S(2)}) collective-permute-start(bf16[128,512]{1,0:T(8,128)(2,1)S(1)} %get-tuple-element.31), channel_id=1, source_target_pairs={{0,1},{1,2},{2,3},{3,4},{4,5},{5,6},{6,7},{7,8},{8,9},{9,10},{10,1... | collective-permute-start | bytes 393224 | tf_op jit(solution)/shard_map/ppermute | solution.py:36
  305.4 4.5 %collective-permute-start.31 = (bf16[128,512]{1,0:T(8,128)(2,1)S(1)}, bf16[128,512]{1,0:T(8,128)(2,1)S(1)}, u32[]{:S(2)}, u32[]{:S(2)}) collective-permute-start(bf16[128,512]{1,0:T(8,128)(2,1)S(1)} %get-tuple-element.32), channel_id=1, source_target_pairs={{1,0},{2,1},{3,2},{4,3},{5,4},{6,5},{7,6},{8,7},{9,8},{10,9},{11,1... | collective-permute-start | bytes 393224 | tf_op jit(solution)/shard_map/ppermute | solution.py:36

commit v2 on v1

--- a/solution.py
+++ b/solution.py
@@ -27,8 +27,8 @@
     return send_to(x, size, lambda i: i ^ bit)
 
 
-def ring(x, size):
-    return send_to(x, size, lambda i: (i + 8) % size)
+def turn(x, size, planes):
+    return send_to(x, size, lambda i: (i + 8 * planes) % size)
 
 
 def shift(x, size, step):
@@ -48,17 +48,64 @@
     return lax.rem(z + planes - step, planes) * 4 + y * 2 + x
 
 
-def gather_pieces(piece, size):
-    held = [piece]
-    for _ in range(size // 8 - 1):
-        held.append(ring(held[-1], size))
-    line = jnp.stack(held)
-    half = line.shape[0] // 2
-    across_x = swap(line, size, 2)
-    across_y = swap(line, size, 4)
-    first = swap(across_x[:half], size, 4)
-    last = swap(across_y[half:], size, 2)
-    return line, across_x, across_y, first, last
+def ordered(x, *before):
+    return lax.optimization_barrier((x, *before))[0]
+
+
+class Rows:
+    def __init__(self, array, parts):
+        self.array = array
+        self.parts = parts
+
+    def part(self, kind, begin, count):
+        if not count:
+            return None
+        parts, row, seen, first = [], 0, 0, None
+        for k, group, step, at, n in self.parts:
+            if k == kind and group in (1, 2):
+                low, high = max(begin, seen), min(begin + count, seen + n)
+                if low < high:
+                    parts.append((k, group, step, at + low - seen, high - low))
+                    first = row + low - seen if first is None else first
+                seen += n
+            row += n
+        return Rows(self.array[first : first + count], parts)
+
+    def count(self, kind):
+        return sum(n for k, group, _, _, n in self.parts if k == kind and group in (1, 2))
+
+    def swapped(self, size, group):
+        parts = [(k, g ^ group, s, at, n) for k, g, s, at, n in self.parts]
+        return Rows(swap(self.array, size, 2 * group), parts)
+
+    def turned(self, size, planes):
+        parts = [(k, g, s + planes, at, n) for k, g, s, at, n in self.parts]
+        return Rows(turn(self.array, size, planes), parts)
+
+
+def joined(rows):
+    rows = [r for r in rows if r is not None]
+    if len(rows) == 1:
+        return rows[0]
+    return Rows(jnp.concatenate([r.array for r in rows]), [p for r in rows for p in r.parts])
+
+
+def halves(rows, kind, unit):
+    total = rows.count(kind)
+    cut = total // 2 // unit * unit
+    return cut, total - cut
+
+
+def across(line, previous, kinds, size):
+    by_x, by_y = list(line), list(line)
+    if previous is not None:
+        over_x, over_y = previous
+        for kind, unit in kinds:
+            cut, rest = halves(over_x, kind, unit)
+            by_y.append(over_x.part(kind, 0, cut))
+            by_x.append(over_y.part(kind, cut, rest))
+    sent = [joined(rows) for rows in (by_x, by_y) if any(r is not None for r in rows)]
+    return sent, [rows.swapped(size, 1 + (i == len(sent) - 1)) for i, rows in enumerate(sent)]
 
 
 def split_tokens(tokens, size):
@@ -67,31 +114,23 @@
     chips = size // 2
     planes = size // 8
 
-    def kernel(tok, mine, other, sems):
+    def kernel(tok, mine, other):
         me = lax.axis_index("fsdp")
         core = lax.rem(me, 2)
-        copies = []
         for i in range(chips):
             chip = chip_at(me, planes, i // planes, i % planes)
-            for n, (ref, parity) in enumerate(((other, 1 - core), (mine, core))):
+            for ref, parity in ((other, 1 - core), (mine, core)):
                 start = pl.multiple_of((2 * chip + parity) * depth, depth)
-                copy = pltpu.make_async_copy(
-                    tok.at[:, pl.ds(start, depth)],
-                    ref.at[:, pl.ds(i * depth, depth)],
-                    sems.at[n, i],
-                )
-                copy.start()
-                copies.append(copy)
-        for copy in copies:
-            copy.wait()
+                ref[:, i * depth : (i + 1) * depth] = tok[:, pl.ds(start, depth)]
 
     half = jax.ShapeDtypeStruct((rows, width // 2), tokens.dtype)
     return pl.pallas_call(
         kernel,
         out_shape=(half, half),
-        in_specs=[ANY],
-        out_specs=(ANY, ANY),
-        scratch_shapes=[pltpu.SemaphoreType.DMA((2, chips))],
+        in_specs=[VMEM],
+        out_specs=(VMEM, VMEM),
+        compiler_params=pltpu.CompilerParams(vmem_limit_bytes=16 * MIB),
+        cost_estimate=pl.CostEstimate(flops=0, bytes_accessed=4 * rows * width, transcendentals=0),
         name="split_tokens",
     )(tokens)
 
@@ -108,36 +147,41 @@
     return lax.dot_general(a, b, (((0,), (0,)), ((), ())), preferred_element_type=F32)
 
 
-def low_rank_products(tok, tok_in, pieces, grad, grad_in, size):
+def low_rank_products(tok, tok_in, pieces, grad, grad_in, size, after):
     rows = tok.shape[0]
     depth = tok.shape[1] * 2 // size
     planes = size // 8
-    quarters = (pieces[0].shape[1] - depth - 16) // 16
-
-    def kernel(tok, tok_in, line, ax, ay, first, last, grad, grad_in, out, table):
+    deep = depth // 4
+    quarters = 2 * depth // 256
+    count = len(pieces)
+
+    def kernel(tok, tok_in, *refs):
+        refs, (grad, grad_in), (out, table, down) = refs[:count], refs[count : count + 2], refs[-3:]
         me = lax.axis_index("fsdp")
-
-        def piece(i):
-            group, step = i // planes, i % planes
-            if group < 3:
-                return (line, ax, ay)[group].at[step]
-            return first.at[step] if step < planes // 2 else last.at[step - planes // 2]
-
+        meta = jnp.zeros((16, WIDE), F32)
+        for ref, piece in zip(refs, pieces):
+            row = 0
+            for kind, group, step, at, n in piece.parts:
+                begin, row = row, row + n
+                if kind != "low":
+                    continue
+                spot = group * planes + step
+                n_down = min(n, deep - at)
+                if n_down > 0:
+                    for g in range(4):
+                        to = spot * depth + g * deep + at
+                        down[to : to + n_down] = ref[begin : begin + n_down, g * 256 : (g + 1) * 256]
+                if at + n <= deep:
+                    continue
+                last = slice(row - 16, row)
+                chip = chip_at(me, planes, group, step)
+                for q in range(quarters):
+                    flat = chip * quarters + q
+                    to = pl.multiple_of(flat // 2 * RANK, RANK)
+                    table[lax.rem(flat, 2), pl.ds(to, RANK), :] = ref[last, q * 256 : (q + 1) * 256]
+                meta += ref[last, 512 : 512 + WIDE].astype(F32)
         for half, source in enumerate((tok, tok_in)):
-            total = jnp.zeros((rows, WIDE), F32)
-            for i in range(4 * planes):
-                total += dot(source[:, i * depth : (i + 1) * depth], piece(i)[:depth])
-            out[half * rows : (half + 1) * rows] = total
-        meta = jnp.zeros((16, WIDE), F32)
-        for i in range(4 * planes):
-            chip = chip_at(me, planes, i // planes, i % planes)
-            for q in range(quarters):
-                flat = chip * quarters + q
-                spot = pl.multiple_of(flat // 2 * RANK, RANK)
-                table[lax.rem(flat, 2), pl.ds(spot, RANK), :] = piece(i)[
-                    depth + q * 16 : depth + (q + 1) * 16
-                ]
-            meta += piece(i)[depth + quarters * 16 :].astype(F32)
+            out[half * rows : (half + 1) * rows] = dot(source[...], down[...])
         for half, source in enumerate((grad, grad_in)):
             low = dot_nt(source[:, :256], table[0]) + dot_nt(source[:, 256:], table[1])
             out[(2 + half) * rows : (3 + half) * rows] = low
@@ -149,14 +193,15 @@
             jax.ShapeDtypeStruct((4 * rows + 16, WIDE), F32),
             jax.ShapeDtypeStruct((2, WIDE, 256), BF16),
         ),
-        in_specs=[VMEM] * 9,
+        in_specs=[VMEM] * (4 + count) + [ANY] * len(after),
         out_specs=(VMEM, VMEM),
-        compiler_params=pltpu.CompilerParams(vmem_limit_bytes=20 * MIB),
+        scratch_shapes=[pltpu.VMEM((tok.shape[1], WIDE), BF16)],
+        compiler_params=pltpu.CompilerParams(vmem_limit_bytes=24 * MIB),
         cost_estimate=pl.CostEstimate(
             flops=4 * rows * (tok.shape[1] + 512) * WIDE, bytes_accessed=9 * MIB, transcendentals=0
         ),
         name="low_rank_products",
-    )(tok, tok_in, *pieces, grad, grad_in)
+    )(tok, tok_in, *(p.array for p in pieces), grad, grad_in, *after)
 
 
 def adapter_terms(own, other, tok, tok_in, grad, grad_in, size, kind):
@@ -265,46 +310,53 @@
     )(terms, names)
 
 
-def value_products(tok, tok_in, pieces, hidden, table, start, size):
+def value_products(tok, tok_in, pieces, so_far, adapters, size, after):
     rows = tok.shape[0]
     depth = tok.shape[1] * 2 // size
     planes = size // 8
-    columns = pieces[0].shape[2]
     own_columns = 2 * depth
-
-    def kernel(tok, tok_in, line, ax, ay, first, last, hidden, table, keep, give):
+    width = pieces[0].array.shape[1]
+    count = len(pieces)
+    terms = []
+    for n, piece in enumerate(pieces):
+        row = 0
+        for kind, group, step, at, height in piece.parts:
+            if kind == "wide":
+                terms.append((n, row, (group * planes + step) * depth + at, height))
+            row += height
+    joint = so_far or adapters
+
+    def kernel(tok, tok_in, *refs):
+        refs, joint, (keep, give) = refs[:count], refs[count : count + 2], refs[-2:]
         core = lax.rem(lax.axis_index("fsdp"), 2)
         for half, (source, out) in enumerate(((tok, keep), (tok_in, give))):
-            for m in range(columns // 256):
-                here = slice(m * 256, (m + 1) * 256)
-                begin = 0
-                total = None
-                for ref in (line, ax, ay, first, last):
-                    deep = ref.shape[0] * depth
-                    part = dot(
-                        source[:, begin : begin + deep], ref[:, :, here].reshape(deep, 256)
-                    )
-                    total = part if total is None else total + part
-                    begin += deep
-                column = start + m * 256
-                owner = column // own_columns
-                q = (owner // 2 * own_columns + column % own_columns) // 256
-                scale = jnp.where(core == owner % 2, SCALE, 0.0).astype(F32)
-                extra = dot(hidden[half * rows : (half + 1) * rows], table[q])
-                out[:, here] = total + scale * extra
-
-    share = jax.ShapeDtypeStruct((rows, columns), F32)
+            for left in range(0, width, 256):
+                here = slice(left, left + 256)
+                if so_far:
+                    total = joint[half][:, here]
+                else:
+                    owner = left // own_columns
+                    place = (owner // 2 * own_columns + left % own_columns) // 256
+                    scale = jnp.where(core == owner % 2, SCALE, 0.0).astype(F32)
+                    total = scale * dot(joint[0][half * rows : (half + 1) * rows], joint[1][place])
+                for n, row, spot, height in terms:
+                    total += dot(source[:, spot : spot + height], refs[n][row : row + height, here])
+                out[:, here] = total
+
+    share = jax.ShapeDtypeStruct((rows, width), F32)
     return pl.pallas_call(
         kernel,
         out_shape=(share, share),
-        in_specs=[VMEM] * 9,
+        in_specs=[VMEM] * (4 + count) + [ANY] * len(after),
         out_specs=(VMEM, VMEM),
-        compiler_params=pltpu.CompilerParams(vmem_limit_bytes=20 * MIB),
+        compiler_params=pltpu.CompilerParams(vmem_limit_bytes=28 * MIB),
         cost_estimate=pl.CostEstimate(
-            flops=4 * rows * tok.shape[1] * columns, bytes_accessed=9 * MIB, transcendentals=0
+            flops=4 * rows * sum(t[3] for t in terms) * width,
+            bytes_accessed=4 * MIB,
+            transcendentals=0,
         ),
         name="value_products",
-    )(tok, tok_in, *pieces, hidden, table)
+    )(tok, tok_in, *(p.array for p in pieces), *joint, *after)
 
 
 def body(
@@ -328,12 +380,29 @@
     valid = (jnp.arange(BLOCK)[None, :] < block_valid_length[:, None])[..., None]
     zero = jnp.zeros((), BF16)
 
+    depth = adapter_down_weight.shape[0]
+    deep = depth // 4
+    planes = size // 8
     lane = jnp.arange(WIDE)[None, :]
     meta = jnp.where(lane == me, block_adapter_index[:, None], 0).astype(BF16)
-    meta = jnp.concatenate([meta, jnp.zeros((14, WIDE), BF16)])
-    ups = [adapter_up_weight[:, q * 256 : (q + 1) * 256] for q in range(own_columns // 256)]
-    piece = jnp.concatenate([adapter_down_weight, *ups, meta])
-    low_pieces = gather_pieces(piece, size)
+    meta = jnp.pad(meta, ((0, 14), (0, 0)))
+    downs = [adapter_down_weight[g * deep : (g + 1) * deep] for g in range(4)]
+    ups = jnp.pad(adapter_up_weight, ((0, 0), (0, 512 - own_columns)))
+    last_rows = jnp.concatenate([ups, meta, jnp.zeros_like(meta)], axis=1)
+    low_piece = jnp.concatenate([jnp.concatenate(downs, axis=1), last_rows])
+    low = [Rows(low_piece, [("low", 0, 0, 0, deep + 16)])]
+    wide = [Rows(frozen_value_weight, [("wide", 0, 0, 0, depth)])]
+    kinds = (("wide", 128), ("low", 16))
+
+    low += [low[0].turned(size, step) for step in range(1, planes)]
+    wide[0].array = ordered(wide[0].array, *(r.array for r in low[1:]))
+    for step in range(planes - 1):
+        wide.append(wide[-1].turned(size, 1))
+    _, stage0 = across([Rows(frozen_value_weight, wide[0].parts), low[0]], None, kinds, size)
+    _, stage1 = across(low[1:], stage0, kinds, size)
+    _, stage2 = across([wide[1]], stage1, kinds, size)
+    sent, stage = across([wide[2]], stage2, kinds, size)
+    stages = [stage0, stage1, stage2, stage]
 
     tok, tok_out = split_tokens(tokens, size)
     tok_in = swap(tok_out, size, 1)
@@ -348,26 +417,38 @@
     grad_mine = jnp.where(core == 0, even, odd)
     grad_in = swap(jnp.where(core == 0, odd, even), size, 1)
 
-    share, table = low_rank_products(tok, tok_in, low_pieces, grad_mine, grad_in, size)
+    share, table = low_rank_products(
+        tok, tok_in, [*low, *stage0, *stage1, *stage2], grad_mine, grad_in, size,
+        [r.array for r in sent],
+    )
     hidden, names, terms = adapter_terms(
-        share, swap(share, size, 1), tok, tok_in, grad_mine, grad_in, size, F32
+        share, swap(share, size, 1), tok, tok_in, grad_mine, grad_in, size, BF16
     )
+    terms_sent = terms
     groups = [list(range(core, size, 2)) for core in range(2)]
     terms = lax.all_to_all(terms, "fsdp", 0, 0, axis_index_groups=groups, tiled=True)
     down_gradient, up_gradient = sum_terms(terms, names, size)
 
-    outs = []
-    for start, stop in ((0, 512), (512, 1024)):
-        pieces = gather_pieces(frozen_value_weight[:, start:stop], size)
-        keep, give = value_products(tok, tok_in, pieces, hidden, table, start, size)
-        total = (keep + swap(give, size, 1)).reshape(-1, BLOCK, stop - start)
-        value = jnp.where(valid, total, 0.0).astype(BF16)
-        right = jnp.sum(jnp.where(goes_right, value, zero), axis=0)
-        left = jnp.sum(jnp.where(goes_left, value, zero), axis=0)
-        own = jnp.where(stays, value, zero)
-        lower, upper = shift(right, size, 1), shift(left, size, -1)
-        outs.append(jnp.concatenate([lower[None], own, upper[None]]).reshape(-1, stop - start))
-    return jnp.concatenate(outs, axis=1), down_gradient, up_gradient
+    early = [*wide[:3], *(r for stage in stages for r in stage)]
+    shares = value_products(tok, tok_in, early, (), (hidden, table), size, ())
+    wide[3].array = ordered(wide[3].array, terms_sent)
+    for step in range(3, planes):
+        _, stage = across([wide[step]], stages[-1], kinds, size)
+        stages.append(stage)
+    for rows in stages[-1]:
+        rows.array = ordered(rows.array, shares[0])
+    _, stage = across([], stages[-1], kinds, size)
+    late = [*wide[3:], *(r for s in stages[4:] for r in s)]
+    shares = value_products(tok, tok_in, late, shares, (), size, (down_gradient,))
+    keep, give = value_products(tok, tok_in, stage, shares, (), size, ())
+    total = (keep + swap(give, size, 1)).reshape(-1, BLOCK, width)
+    value = jnp.where(valid, total, 0.0).astype(BF16)
+    right = jnp.sum(jnp.where(goes_right, value, zero), axis=0)
+    left = jnp.sum(jnp.where(goes_left, value, zero), axis=0)
+    own = jnp.where(stays, value, zero)
+    lower, upper = shift(right, size, 1), shift(left, size, -1)
+    layer_out = jnp.concatenate([lower[None], own, upper[None]]).reshape(-1, width)
+    return layer_out, down_gradient, up_gradient
 
 
 def solution(mesh):

time: 319 us -> 166 us (0.52)
  the two profiles are of different devices: /device:TPU:0 before, /device:TPU:7 now
where the time goes in v2:
time: 166 us; the launch traced here: 165 us
  waiting for transfers between devices  59.5 us (36%)
  starting transfers between devices  43.9 us (26%)
  local copies, waits for them, and re-layouts  25.4 us (15%)
  Pallas kernels  23.9 us (14%)
  other arithmetic  10.9 us (7%)
    ppermute x22, waiting for transfers between devices, send_to(): return lax.ppermute(x, 'fsdp', [(i, target(i)) for i in range(size)])  51.9 us
    ppermute x22, starting transfers between devices, send_to(): return lax.ppermute(x, 'fsdp', [(i, target(i)) for i in range(size)])  24.1 us
    unnamed x71, local copies, waits for them, and re-layouts  16 us
    ppermute x4, starting transfers between devices, shift(): return lax.ppermute(x, 'fsdp', pairs)  14.6 us
    pallas_call x3, Pallas kernels, value_products(): pl.pallas_call(kernel, out_shape=(share, share), in_specs=[VMEM] * (4 + c...  12.5 us
    ppermute x4, waiting for transfers between devices, shift(): return lax.ppermute(x, 'fsdp', pairs)  7.57 us
    concatenate x5, other arithmetic, joined(): jnp.concatenate([r.array for r in rows])  6.67 us
    slice x8, local copies, waits for them, and re-layouts, part(): return Rows(self.array[first:first + count], parts)  6.41 us
  transfers between devices with their start and end apart: 27, of which 10 were waited for; matrix products, arithmetic and copies ran while one was open for 12% of the time, Pallas kernels for 11%

profile of v2, /device:TPU:7, one launch (start us, length us, event | category | flops | bytes accessed | tf_op | source)
XLA Modules:
  0.0 164.6 jit_solution(15866477297890541531)
XLA Ops:
  0.7 0.8 fusion.4
  2.2 1.1 maximum_maximum_fusion
  3.7 1.3 collective-permute-start.1
  5.0 2.3 %collective-permute-start.2 = (bf16[80,1024]{1,0:T(8,128)(2,1)S(1)}, bf16[80,1024]{1,0:T(8,128)(2,1)S(1)}, u32[]{:S(2)}, u32[]{:S(2)}) collective-permute-start(bf16[80,1024]{1,0:T(8,128)(2,1)S(1)} %maximum_maximum_fusion.1.refs_0_), channel_id=1, source_target_pairs={{0,16},{1,17},{2,18},{3,19},{4,20},{5,21},{6,22},{7,23},{8,24},{9,... | collective-permute-start | bytes 491528 | tf_op jit(solution)/shard_map/ppermute | solution.py:23
  7.4 1.1 collective-permute-start.3
  8.6 2.2 %copy-done.6 = bf16[256,8192]{1,0:T(8,128)(2,1)S(1)} copy-done((bf16[256,8192]{1,0:T(8,128)(2,1)S(1)}, bf16[256,8192]{1,0:T(8,128)(2,1)}, u32[]{:S(2)}) %copy-start.6) | copy-done | bytes 4194328
  10.8 1.9 %split_tokens.1 = (bf16[256,4096]{1,0:T(8,128)(2,1)S(1)}, bf16[256,4096]{1,0:T(8,128)(2,1)}) custom-call(bf16[256,8192]{1,0:T(8,128)(2,1)S(1)} %copy-done.6), custom_call_target="tpu_custom_call" | custom-call | bytes 8388608 | tf_op jit(solution)/shard_map/split_tokens/pallas_call | solution.py:127
  12.8 2.1 %collective-permute-start = (bf16[256,4096]{1,0:T(8,128)(2,1)}, bf16[256,4096]{1,0:T(8,128)(2,1)}, u32[]{:S(2)}, u32[]{:S(2)}) collective-permute-start(bf16[256,4096]{1,0:T(8,128)(2,1)} %get-tuple-element.23), channel_id=1, source_target_pairs={{0,1},{1,0},{2,3},{3,2},{4,5},{5,4},{6,7},{7,6},{8,9},{9,8},{10,11... | collective-permute-start | bytes 6291464 | tf_op jit(solution)/shard_map/ppermute | solution.py:23
  14.9 0.8 constant_dynamic-update-slice_fusion.5
  15.7 3.0 %collective-permute-done.2.refs_2_ = bf16[80,1024]{1,0:T(8,128)(2,1)S(1)} collective-permute-done((bf16[80,1024]{1,0:T(8,128)(2,1)S(1)}, bf16[80,1024]{1,0:T(8,128)(2,1)S(1)}, u32[]{:S(2)}, u32[]{:S(2)}) %collective-permute-start.2) | collective-permute-done | bytes 163872 | tf_op jit(solution)/shard_map/ppermute | solution.py:23
  18.8 0.8 constant_dynamic-update-slice_fusion.4
  19.5 0.8 constant_dynamic-update-slice_fusion.3
  22.0 1.6 collective-permute-done.8.refs_5_.refs_4_
  23.6 0.8 slice_dynamic-update-slice_fusion.1
  25.0 1.2 collective-permute-start.9
  26.2 1.4 collective-permute-start.4
  27.6 0.8 fusion.3
  28.4 4.7 %collective-permute-start.13 = (bf16[128,1024]{1,0:T(8,128)(2,1)}, bf16[128,1024]{1,0:T(8,128)(2,1)}, u32[]{:S(2)}, u32[]{:S(2)}) collective-permute-start(bf16[128,1024]{1,0:T(8,128)(2,1)} %get-tuple-element.45), channel_id=1, source_target_pairs={{1,0},{2,1},{3,2},{4,3},{5,4},{6,5},{7,6},{8,7},{9,8},{10,9},{11,1... | collective-permute-start | bytes 786440 | tf_op jit(solution)/shard_map/ppermute | solution.py:36
  33.1 12.1 %collective-permute-done.10.refs_7_.refs_6_ = bf16[400,1024]{1,0:T(8,128)(2,1)S(1)} collective-permute-done((bf16[400,1024]{1,0:T(8,128)(2,1)}, bf16[400,1024]{1,0:T(8,128)(2,1)S(1)}, u32[]{:S(2)}, u32[]{:S(2)}) %collective-permute-start.10) | collective-permute-done | bytes 819232 | tf_op jit(solution)/shard_map/ppermute | solution.py:23
  45.2 3.0 %collective-permute-start.14 = (bf16[128,1024]{1,0:T(8,128)(2,1)}, bf16[128,1024]{1,0:T(8,128)(2,1)}, u32[]{:S(2)}, u32[]{:S(2)}) collective-permute-start(bf16[128,1024]{1,0:T(8,128)(2,1)} %get-tuple-element.46), channel_id=1, source_target_pairs={{0,1},{1,2},{2,3},{3,4},{4,5},{5,6},{6,7},{7,8},{8,9},{9,10},{10,1... | collective-permute-start | bytes 786440 | tf_op jit(solution)/shard_map/ppermute | solution.py:36
  48.3 0.9 pad_maximum_fusion.5
  49.2 1.7 %collective-permute-start.11 = (bf16[384,1024]{1,0:T(8,128)(2,1)}, bf16[384,1024]{1,0:T(8,128)(2,1)}, u32[]{:S(2)}, u32[]{:S(2)}) collective-permute-start(bf16[384,1024]{1,0:T(8,128)(2,1)} %pad_maximum_fusion.5), channel_id=1, source_target_pairs={{0,2},{1,3},{2,0},{3,1},{4,6},{5,7},{6,4},{7,5},{8,10},{9,11},{10,... | collective-permute-start | bytes 2359304 | tf_op jit(solution)/shard_map/ppermute | solution.py:23
  50.9 1.0 slice.92
  51.8 0.9 pad_maximum_fusion.6
  52.8 1.8 %collective-permute-start.5 = (bf16[256,1024]{1,0:T(8,128)(2,1)S(1)}, bf16[256,1024]{1,0:T(8,128)(2,1)}, u32[]{:S(2)}, u32[]{:S(2)}) collective-permute-start(bf16[256,1024]{1,0:T(8,128)(2,1)S(1)} %collective-permute-done.4.refs_1_), channel_id=1, source_target_pairs={{0,8},{1,9},{2,10},{3,11},{4,12},{5,13},{6,14},{7,15},{8,16},{9,17... | collective-permute-start | bytes 1572872 | tf_op jit(solution)/shard_map/ppermute | solution.py:23
  54.7 1.4 fusion.1
  56.1 1.2 collective-permute-start.15
  57.3 13.5 %collective-permute-done.12.refs_9_.refs_8_ = bf16[368,1024]{1,0:T(8,128)(2,1)} collective-permute-done((bf16[368,1024]{1,0:T(8,128)(2,1)}, bf16[368,1024]{1,0:T(8,128)(2,1)}, u32[]{:S(2)}, u32[]{:S(2)}) %collective-permute-start.12) | collective-permute-done | bytes 753696 | tf_op jit(solution)/shard_map/ppermute | solution.py:23
  70.8 1.0 slice.95
  71.8 1.1 slice.96
  72.9 2.5 %pad_maximum_fusion.1 = (bf16[384,1024]{1,0:T(8,128)(2,1)}, bf16[384,1024]{1,0:T(8,128)(2,1)}) fusion(bf16[256,1024]{1,0:T(8,128)(2,1)} %collective-permute-done.5.refs_2_, bf16[128,1024]{1,0:T(8,128)(2,1)S(1)} %slice.96, bf16[128,1024]{1,0:T(8,128)(2,1)S(1)} %slice.95), kind=kLoop, calls=%fused_computation.2 | loop fusion | flops 2752512 | bytes 2621440 | tf_op jit(solution)/shard_map/concatenate | solution.py:90
  75.4 3.9 %low_rank_products.1 = (f32[1040,256]{1,0:T(8,128)S(1)}, bf16[2,256,256]{2,1,0:T(8,128)(2,1)S(1)}) custom-call(bf16[256,4096]{1,0:T(8,128)(2,1)S(1)} %get-tuple-element.22.tok, bf16[256,4096]{1,0:T(8,128)(2,1)} %collective-permute-done.tok_in, bf16[80,1024]{1,0:T(8,128)(2,1)S(1)} %copy-done.17, bf16[80,1024]{1,0:T(8,128)(2,1)S(1)} %copy-done.19, ...), custom_call_target="tpu_custom_call" | custom-call | flops 1207959552 | bytes 9437184 | tf_op jit(solution)/shard_map/low_rank_products/pallas_call | solution.py:190
  79.4 1.6 collective-permute-start.17
  81.0 1.8 %collective-permute-start.6 = (bf16[256,1024]{1,0:T(8,128)(2,1)}, bf16[256,1024]{1,0:T(8,128)(2,1)}, u32[]{:S(2)}, u32[]{:S(2)}) collective-permute-start(bf16[256,1024]{1,0:T(8,128)(2,1)} %collective-permute-done.5.refs_2_), channel_id=1, source_target_pairs={{0,8},{1,9},{2,10},{3,11},{4,12},{5,13},{6,14},{7,15},{8,16},{9,17... | collective-permute-start | bytes 1572872 | tf_op jit(solution)/shard_map/ppermute | solution.py:23
  82.7 3.1 %adapter_terms.1 = (bf16[512,256]{1,0:T(8,128)(2,1)S(1)}, f32[16,256]{1,0:T(8,128)S(1)}, bf16[16,96,256]{2,1,0:T(8,128)(2,1)S(1)}) custom-call(f32[1040,256]{1,0:T(8,128)S(1)} %get-tuple-element.25.own, f32[1040,256]{1,0:T(8,128)S(1)} %collective-permute-done.16.other, bf16[256,4096]{1,0:T(8,128)(2,1)S(1)} %get-tuple-element.22.tok, ...), custom_call_target="tpu_custom_call" | custom-call | flops 536870912 | bytes 9437184 | tf_op jit(solution)/shard_map/adapter_terms/pallas_call | solution.py:252
  85.8 0.9 copy-done.15
  87.4 5.2 %all-to-all-start = ((bf16[16,96,256]{2,1,0:T(8,128)(2,1)}), bf16[16,96,256]{2,1,0:T(8,128)(2,1)}, u32[]{:S(2)}, u32[]{:S(2)}) async-start(bf16[16,96,256]{2,1,0:T(8,128)(2,1)} %copy-done.15), calls=%async_computation | async-start | bytes 1572864 | tf_op jit(solution)/shard_map/all_to_all | solution.py:429
  92.6 6.0 %collective-permute-done.17.refs_9_ = bf16[384,1024]{1,0:T(8,128)(2,1)} collective-permute-done((bf16[384,1024]{1,0:T(8,128)(2,1)}, bf16[384,1024]{1,0:T(8,128)(2,1)}, u32[]{:S(2)}, u32[]{:S(2)}) %collective-permute-start.17) | collective-permute-done | bytes 786464 | tf_op jit(solution)/shard_map/ppermute | solution.py:23
  98.5 1.0 slice.97
  99.5 3.5 %collective-permute-done.19.refs_10_ = bf16[384,1024]{1,0:T(8,128)(2,1)} collective-permute-done((bf16[384,1024]{1,0:T(8,128)(2,1)}, bf16[384,1024]{1,0:T(8,128)(2,1)}, u32[]{:S(2)}, u32[]{:S(2)}) %collective-permute-start.19) | collective-permute-done | bytes 786464 | tf_op jit(solution)/shard_map/ppermute | solution.py:23
  103.1 1.0 slice.98
  104.0 1.2 pad_maximum_fusion.3
  105.4 0.9 collective-permute-start.18
  106.3 7.0 %value_products.3 = (f32[256,1024]{1,0:T(8,128)S(1)}, f32[256,1024]{1,0:T(8,128)S(1)}) custom-call(bf16[256,4096]{1,0:T(8,128)(2,1)S(1)} %get-tuple-element.22.tok, bf16[256,4096]{1,0:T(8,128)(2,1)} %collective-permute-done.tok_in, bf16[256,1024]{1,0:T(8,128)(2,1)} %refs_0_, bf16[256,1024]{1,0:T(8,128)(2,1)S(1)} %collective-permute-done.4.refs_1_, ...), custom_call_target="tpu_custom_call" | custom-call | flops 2952790016 | bytes 4194304 | tf_op jit(solution)/shard_map/value_products/pallas_call | solution.py:347
  113.3 1.0 copy-done.11
  114.2 1.0 copy-done.13
  115.2 10.0 %collective-permute-done.21.refs_1_ = bf16[384,1024]{1,0:T(8,128)(2,1)S(1)} collective-permute-done((bf16[384,1024]{1,0:T(8,128)(2,1)S(1)}, bf16[384,1024]{1,0:T(8,128)(2,1)S(1)}, u32[]{:S(2)}, u32[]{:S(2)}) %collective-permute-start.21) | collective-permute-done | bytes 786464 | tf_op jit(solution)/shard_map/ppermute | solution.py:23
  125.9 0.9 copy-done.7
  128.1 0.9 copy-done.9
  129.0 1.1 collective-permute-start.20
  130.1 2.5 %sum_terms.1 = (f32[256,256]{1,0:T(8,128)}, f32[16,512]{1,0:T(8,128)}) custom-call(bf16[16,96,256]{2,1,0:T(8,128)(2,1)} %all-to-all-done.terms, f32[16,256]{1,0:T(8,128)S(1)} %get-tuple-element.34.names), custom_call_target="tpu_custom_call" | custom-call | flops 134217728 | bytes 2097152 | tf_op jit(solution)/shard_map/sum_terms/pallas_call | solution.py:297
  132.6 1.1 copy-done.10
  133.8 1.2 copy-done.12
  135.0 1.2 copy-done.14
  136.2 0.9 copy-done.24
  137.2 3.2 %value_products.4 = (f32[256,1024]{1,0:T(8,128)S(1)}, f32[256,1024]{1,0:T(8,128)S(1)}) custom-call(bf16[256,4096]{1,0:T(8,128)(2,1)S(1)} %get-tuple-element.22.tok, bf16[256,4096]{1,0:T(8,128)(2,1)} %collective-permute-done.tok_in, bf16[256,1024]{1,0:T(8,128)(2,1)} %collective-permute-done.6.refs_0_, bf16[384,1024]{1,0:T(8,128)(2,1)S(1)} %copy-done.8, ...), custom_call_target="tpu_custom_call" | custom-call | flops 1073741824 | bytes 4194304 | tf_op jit(solution)/shard_map/value_products/pallas_call | solution.py:347
  140.4 2.3 %value_products.5 = (f32[256,1024]{1,0:T(8,128)S(1)}, f32[256,1024]{1,0:T(8,128)S(1)}) custom-call(bf16[256,4096]{1,0:T(8,128)(2,1)S(1)} %get-tuple-element.22.tok, bf16[256,4096]{1,0:T(8,128)(2,1)} %collective-permute-done.tok_in, bf16[128,1024]{1,0:T(8,128)(2,1)S(1)} %collective-permute-done.20.refs_0_, ...), custom_call_target="tpu_custom_call" | custom-call | flops 268435456 | bytes 4194304 | tf_op jit(solution)/shard_map/value_products/pallas_call | solution.py:347
  142.7 3.2 %collective-permute-start.23 = (f32[256,1024]{1,0:T(8,128)S(1)}, f32[256,1024]{1,0:T(8,128)S(1)}, u32[]{:S(2)}, u32[]{:S(2)}) collective-permute-start(f32[256,1024]{1,0:T(8,128)S(1)} %get-tuple-element.39), channel_id=1, source_target_pairs={{0,1},{1,0},{2,3},{3,2},{4,5},{5,4},{6,7},{7,6},{8,9},{9,8},{10,11... | collective-permute-start | bytes 3145736 | tf_op jit(solution)/shard_map/ppermute | solution.py:23
  145.9 2.3 %collective-permute-done.23 = f32[256,1024]{1,0:T(8,128)S(1)} collective-permute-done((f32[256,1024]{1,0:T(8,128)S(1)}, f32[256,1024]{1,0:T(8,128)S(1)}, u32[]{:S(2)}, u32[]{:S(2)}) %collective-permute-start.23) | collective-permute-done | bytes 1048608 | tf_op jit(solution)/shard_map/ppermute | solution.py:23
  149.1 5.0 %collective-permute-start.24 = (bf16[128,1024]{1,0:T(8,128)(2,1)S(1)}, bf16[128,1024]{1,0:T(8,128)(2,1)S(1)}, u32[]{:S(2)}, u32[]{:S(2)}) collective-permute-start(bf16[128,1024]{1,0:T(8,128)(2,1)S(1)} %get-tuple-element.41), channel_id=1, source_target_pairs={{0,1},{1,2},{2,3},{3,4},{4,5},{5,6},{6,7},{7,8},{8,9},{9,10},{10,1... | collective-permute-start | bytes 786440 | tf_op jit(solution)/shard_map/ppermute | solution.py:36
  154.0 1.9 %collective-permute-start.25 = (bf16[128,1024]{1,0:T(8,128)(2,1)S(1)}, bf16[128,1024]{1,0:T(8,128)(2,1)S(1)}, u32[]{:S(2)}, u32[]{:S(2)}) collective-permute-start(bf16[128,1024]{1,0:T(8,128)(2,1)S(1)} %get-tuple-element.42), channel_id=1, source_target_pairs={{1,0},{2,1},{3,2},{4,3},{5,4},{6,5},{7,6},{8,7},{9,8},{10,9},{11,1... | collective-permute-start | bytes 786440 | tf_op jit(solution)/shard_map/ppermute | solution.py:36
  156.0 1.4 collective-permute-done.24
  157.4 6.2 %collective-permute-done.25 = bf16[128,1024]{1,0:T(8,128)(2,1)S(1)} collective-permute-done((bf16[128,1024]{1,0:T(8,128)(2,1)S(1)}, bf16[128,1024]{1,0:T(8,128)(2,1)S(1)}, u32[]{:S(2)}, u32[]{:S(2)}) %collective-permute-start.25) | collective-permute-done | bytes 262176 | tf_op jit(solution)/shard_map/ppermute | solution.py:36
  163.5 1.1 pad_maximum_fusion
  (99 shorter events, 7.6 us)
Async XLA Ops:
  0.6 3.0 %copy-start.30 = (bf16[16,512]{1,0:T(8,128)(2,1)S(1)}, bf16[16,512]{1,0:T(8,128)(2,1)}, u32[]{:S(2)}) copy-start(bf16[16,512]{1,0:T(8,128)(2,1)} %param.11) | copy-start | bytes 49156
  3.3 17.0 %collective-permute-start.7 = (bf16[336,1024]{1,0:T(8,128)(2,1)S(1)}, bf16[336,1024]{1,0:T(8,128)(2,1)S(1)}, u32[]{:S(2)}, u32[]{:S(2)}) collective-permute-start(bf16[336,1024]{1,0:T(8,128)(2,1)S(1)} %maximum_maximum_fusion), channel_id=1, source_target_pairs={{0,2},{1,3},{2,0},{3,1},{4,6},{5,7},{6,4},{7,5},{8,10},{9,11},{10,... | collective-permute-start | bytes 2064392 | tf_op jit(solution)/shard_map/ppermute | solution.py:23
  3.7 9.1 %copy-start.16 = (bf16[80,1024]{1,0:T(8,128)(2,1)}, bf16[80,1024]{1,0:T(8,128)(2,1)S(1)}, u32[]{:S(2)}) copy-start(bf16[80,1024]{1,0:T(8,128)(2,1)S(1)} %maximum_maximum_fusion.1.refs_0_) | copy-start | bytes 491524
  3.7 9.1 %collective-permute-start.1 = (bf16[80,1024]{1,0:T(8,128)(2,1)S(1)}, bf16[80,1024]{1,0:T(8,128)(2,1)S(1)}, u32[]{:S(2)}, u32[]{:S(2)}) collective-permute-start(bf16[80,1024]{1,0:T(8,128)(2,1)S(1)} %maximum_maximum_fusion.1.refs_0_), channel_id=1, source_target_pairs={{0,8},{1,9},{2,10},{3,11},{4,12},{5,13},{6,14},{7,15},{8,16},{9,17... | collective-permute-start | bytes 491528 | tf_op jit(solution)/shard_map/ppermute | solution.py:23
  5.0 13.7 %collective-permute-start.2 = (bf16[80,1024]{1,0:T(8,128)(2,1)S(1)}, bf16[80,1024]{1,0:T(8,128)(2,1)S(1)}, u32[]{:S(2)}, u32[]{:S(2)}) collective-permute-start(bf16[80,1024]{1,0:T(8,128)(2,1)S(1)} %maximum_maximum_fusion.1.refs_0_), channel_id=1, source_target_pairs={{0,16},{1,17},{2,18},{3,19},{4,20},{5,21},{6,22},{7,23},{8,24},{9,... | collective-permute-start | bytes 491528 | tf_op jit(solution)/shard_map/ppermute | solution.py:23
  7.4 12.2 %collective-permute-start.3 = (bf16[80,1024]{1,0:T(8,128)(2,1)S(1)}, bf16[80,1024]{1,0:T(8,128)(2,1)S(1)}, u32[]{:S(2)}, u32[]{:S(2)}) collective-permute-start(bf16[80,1024]{1,0:T(8,128)(2,1)S(1)} %maximum_maximum_fusion.1.refs_0_), channel_id=1, source_target_pairs={{0,24},{1,25},{2,26},{3,27},{4,28},{5,29},{6,30},{7,31},{8,0},{9,1... | collective-permute-start | bytes 491528 | tf_op jit(solution)/shard_map/ppermute | solution.py:23
  8.4 15.1 %collective-permute-start.8 = (bf16[336,1024]{1,0:T(8,128)(2,1)S(1)}, bf16[336,1024]{1,0:T(8,128)(2,1)S(1)}, u32[]{:S(2)}, u32[]{:S(2)}) collective-permute-start(bf16[336,1024]{1,0:T(8,128)(2,1)S(1)} %maximum_maximum_fusion), channel_id=1, source_target_pairs={{0,4},{1,5},{2,6},{3,7},{4,0},{5,1},{6,2},{7,3},{8,12},{9,13},{10,... | collective-permute-start | bytes 2064392 | tf_op jit(solution)/shard_map/ppermute | solution.py:23
  8.6 2.2 %copy-start.6 = (bf16[256,8192]{1,0:T(8,128)(2,1)S(1)}, bf16[256,8192]{1,0:T(8,128)(2,1)}, u32[]{:S(2)}) copy-start(bf16[256,8192]{1,0:T(8,128)(2,1)} %tok.1) | copy-start | bytes 12582916
  12.8 14.8 %copy-start.29 = (bf16[512,1024]{1,0:T(8,128)(2,1)S(1)}, bf16[512,1024]{1,0:T(8,128)(2,1)}, u32[]{:S(2)}) copy-start(bf16[512,1024]{1,0:T(8,128)(2,1)} %param.15) | copy-start | bytes 3145732
  12.8 15.6 %copy-start.18 = (bf16[80,1024]{1,0:T(8,128)(2,1)}, bf16[80,1024]{1,0:T(8,128)(2,1)S(1)}, u32[]{:S(2)}) copy-start(bf16[80,1024]{1,0:T(8,128)(2,1)S(1)} %collective-permute-done.1.refs_1_) | copy-start | bytes 491524
  12.8 62.6 %collective-permute-start = (bf16[256,4096]{1,0:T(8,128)(2,1)}, bf16[256,4096]{1,0:T(8,128)(2,1)}, u32[]{:S(2)}, u32[]{:S(2)}) collective-permute-start(bf16[256,4096]{1,0:T(8,128)(2,1)} %get-tuple-element.23), channel_id=1, source_target_pairs={{0,1},{1,0},{2,3},{3,2},{4,5},{5,4},{6,7},{7,6},{8,9},{9,8},{10,11... | collective-permute-start | bytes 6291464 | tf_op jit(solution)/shard_map/ppermute | solution.py:23
  18.7 9.6 %copy-start.20 = (bf16[80,1024]{1,0:T(8,128)(2,1)}, bf16[80,1024]{1,0:T(8,128)(2,1)S(1)}, u32[]{:S(2)}) copy-start(bf16[80,1024]{1,0:T(8,128)(2,1)S(1)} %collective-permute-done.2.refs_2_) | copy-start | bytes 491524
  19.5 13.6 %copy-start.31 = (s32[2]{0:T(128)S(1)}, s32[2]{0:T(128)}, u32[]{:S(2)}) copy-start(s32[2]{0:T(128)} %param.14) | copy-start | bytes 28
  19.5 8.9 %copy-start.22 = (bf16[80,1024]{1,0:T(8,128)(2,1)}, bf16[80,1024]{1,0:T(8,128)(2,1)S(1)}, u32[]{:S(2)}) copy-start(bf16[80,1024]{1,0:T(8,128)(2,1)S(1)} %collective-permute-done.3.refs_3_) | copy-start | bytes 491524
  20.3 5.8 %copy-start.3 = (bf16[336,1024]{1,0:T(8,128)(2,1)}, bf16[336,1024]{1,0:T(8,128)(2,1)S(1)}, u32[]{:S(2)}) copy-start(bf16[336,1024]{1,0:T(8,128)(2,1)S(1)} %collective-permute-done.7.refs_4_.refs_3_) | copy-start | bytes 2064388
  21.7 23.4 %collective-permute-start.10 = (bf16[400,1024]{1,0:T(8,128)(2,1)}, bf16[400,1024]{1,0:T(8,128)(2,1)S(1)}, u32[]{:S(2)}, u32[]{:S(2)}) collective-permute-start(bf16[400,1024]{1,0:T(8,128)(2,1)} %slice_dynamic-update-slice_fusion.3), channel_id=1, source_target_pairs={{0,4},{1,5},{2,6},{3,7},{4,0},{5,1},{6,2},{7,3},{8,12},{9,13},{10,... | collective-permute-start | bytes 2457608 | tf_op jit(solution)/shard_map/ppermute | solution.py:23
  23.5 1.4 copy-start
  25.0 25.9 %collective-permute-start.9 = (bf16[416,1024]{1,0:T(8,128)(2,1)}, bf16[416,1024]{1,0:T(8,128)(2,1)}, u32[]{:S(2)}, u32[]{:S(2)}) collective-permute-start(bf16[416,1024]{1,0:T(8,128)(2,1)} %slice_dynamic-update-slice_fusion.2), channel_id=1, source_target_pairs={{0,2},{1,3},{2,0},{3,1},{4,6},{5,7},{6,4},{7,5},{8,10},{9,11},{10,... | collective-permute-start | bytes 2555912 | tf_op jit(solution)/shard_map/ppermute | solution.py:23
  26.2 22.1 %collective-permute-start.4 = (bf16[256,1024]{1,0:T(8,128)(2,1)}, bf16[256,1024]{1,0:T(8,128)(2,1)S(1)}, u32[]{:S(2)}, u32[]{:S(2)}) collective-permute-start(bf16[256,1024]{1,0:T(8,128)(2,1)} %refs_0_), channel_id=1, source_target_pairs={{0,8},{1,9},{2,10},{3,11},{4,12},{5,13},{6,14},{7,15},{8,16},{9,17... | collective-permute-start | bytes 1572872 | tf_op jit(solution)/shard_map/ppermute | solution.py:23
  28.4 24.4 %collective-permute-start.13 = (bf16[128,1024]{1,0:T(8,128)(2,1)}, bf16[128,1024]{1,0:T(8,128)(2,1)}, u32[]{:S(2)}, u32[]{:S(2)}) collective-permute-start(bf16[128,1024]{1,0:T(8,128)(2,1)} %get-tuple-element.45), channel_id=1, source_target_pairs={{1,0},{2,1},{3,2},{4,3},{5,4},{6,5},{7,6},{8,7},{9,8},{10,9},{11,1... | collective-permute-start | bytes 786440 | tf_op jit(solution)/shard_map/ppermute | solution.py:36
  45.2 9.5 %collective-permute-start.14 = (bf16[128,1024]{1,0:T(8,128)(2,1)}, bf16[128,1024]{1,0:T(8,128)(2,1)}, u32[]{:S(2)}, u32[]{:S(2)}) collective-permute-start(bf16[128,1024]{1,0:T(8,128)(2,1)} %get-tuple-element.46), channel_id=1, source_target_pairs={{0,1},{1,2},{2,3},{3,4},{4,5},{5,6},{6,7},{7,8},{8,9},{9,10},{10,1... | collective-permute-start | bytes 786440 | tf_op jit(solution)/shard_map/ppermute | solution.py:36
  48.3 6.3 %copy-start.32 = (s32[2]{0:T(128)S(1)}, s32[2]{0:T(128)}, u32[]{:S(2)}) copy-start(s32[2]{0:T(128)} %param.13) | copy-start | bytes 28
  49.2 22.6 %collective-permute-start.11 = (bf16[384,1024]{1,0:T(8,128)(2,1)}, bf16[384,1024]{1,0:T(8,128)(2,1)}, u32[]{:S(2)}, u32[]{:S(2)}) collective-permute-start(bf16[384,1024]{1,0:T(8,128)(2,1)} %pad_maximum_fusion.5), channel_id=1, source_target_pairs={{0,2},{1,3},{2,0},{3,1},{4,6},{5,7},{6,4},{7,5},{8,10},{9,11},{10,... | collective-permute-start | bytes 2359304 | tf_op jit(solution)/shard_map/ppermute | solution.py:23
  52.7 18.0 %collective-permute-start.12 = (bf16[368,1024]{1,0:T(8,128)(2,1)}, bf16[368,1024]{1,0:T(8,128)(2,1)}, u32[]{:S(2)}, u32[]{:S(2)}) collective-permute-start(bf16[368,1024]{1,0:T(8,128)(2,1)} %pad_maximum_fusion.6), channel_id=1, source_target_pairs={{0,4},{1,5},{2,6},{3,7},{4,0},{5,1},{6,2},{7,3},{8,12},{9,13},{10,... | collective-permute-start | bytes 2261000 | tf_op jit(solution)/shard_map/ppermute | solution.py:23
  52.8 20.1 %collective-permute-start.5 = (bf16[256,1024]{1,0:T(8,128)(2,1)S(1)}, bf16[256,1024]{1,0:T(8,128)(2,1)}, u32[]{:S(2)}, u32[]{:S(2)}) collective-permute-start(bf16[256,1024]{1,0:T(8,128)(2,1)S(1)} %collective-permute-done.4.refs_1_), channel_id=1, source_target_pairs={{0,8},{1,9},{2,10},{3,11},{4,12},{5,13},{6,14},{7,15},{8,16},{9,17... | collective-permute-start | bytes 1572872 | tf_op jit(solution)/shard_map/ppermute | solution.py:23
  56.1 19.3 %collective-permute-start.15 = (bf16[256,512]{1,0:T(8,128)(2,1)S(1)}, bf16[256,512]{1,0:T(8,128)(2,1)S(1)}, u32[]{:S(2)}, u32[]{:S(2)}) collective-permute-start(bf16[256,512]{1,0:T(8,128)(2,1)S(1)} %get-tuple-element.51), channel_id=1, source_target_pairs={{0,1},{1,0},{2,3},{3,2},{4,5},{5,4},{6,7},{7,6},{8,9},{9,8},{10,11... | collective-permute-start | bytes 786440 | tf_op jit(solution)/shard_map/ppermute | solution.py:23
  71.7 3.7 %copy-start.1 = (bf16[336,1024]{1,0:T(8,128)(2,1)S(1)}, bf16[336,1024]{1,0:T(8,128)(2,1)}, u32[]{:S(2)}) copy-start(bf16[336,1024]{1,0:T(8,128)(2,1)} %copy-done) | copy-start | bytes 2064388
  71.7 3.7 %copy-start.4 = (bf16[336,1024]{1,0:T(8,128)(2,1)S(1)}, bf16[336,1024]{1,0:T(8,128)(2,1)}, u32[]{:S(2)}) copy-start(bf16[336,1024]{1,0:T(8,128)(2,1)} %copy-done.3) | copy-start | bytes 2064388
  71.7 3.7 %copy-start.17 = (bf16[80,1024]{1,0:T(8,128)(2,1)S(1)}, bf16[80,1024]{1,0:T(8,128)(2,1)}, u32[]{:S(2)}) copy-start(bf16[80,1024]{1,0:T(8,128)(2,1)} %copy-done.16) | copy-start | bytes 491524
  71.8 3.7 %copy-start.19 = (bf16[80,1024]{1,0:T(8,128)(2,1)S(1)}, bf16[80,1024]{1,0:T(8,128)(2,1)}, u32[]{:S(2)}) copy-start(bf16[80,1024]{1,0:T(8,128)(2,1)} %copy-done.18) | copy-start | bytes 491524
  71.8 3.7 %copy-start.21 = (bf16[80,1024]{1,0:T(8,128)(2,1)S(1)}, bf16[80,1024]{1,0:T(8,128)(2,1)}, u32[]{:S(2)}) copy-start(bf16[80,1024]{1,0:T(8,128)(2,1)} %copy-done.20) | copy-start | bytes 491524
  71.8 3.7 %copy-start.23 = (bf16[80,1024]{1,0:T(8,128)(2,1)S(1)}, bf16[80,1024]{1,0:T(8,128)(2,1)}, u32[]{:S(2)}) copy-start(bf16[80,1024]{1,0:T(8,128)(2,1)} %copy-done.22) | copy-start | bytes 491524
  79.3 6.5 %copy-start.25 = (bf16[2,256,256]{2,1,0:T(8,128)(2,1)}, bf16[2,256,256]{2,1,0:T(8,128)(2,1)S(1)}, u32[]{:S(2)}) copy-start(bf16[2,256,256]{2,1,0:T(8,128)(2,1)S(1)} %get-tuple-element.29.refs_12_) | copy-start | bytes 786436
  79.3 3.4 %collective-permute-start.16 = (f32[1040,256]{1,0:T(8,128)S(1)}, f32[1040,256]{1,0:T(8,128)S(1)}, u32[]{:S(2)}, u32[]{:S(2)}) collective-permute-start(f32[1040,256]{1,0:T(8,128)S(1)} %get-tuple-element.25.own), channel_id=1, source_target_pairs={{0,1},{1,0},{2,3},{3,2},{4,5},{5,4},{6,7},{7,6},{8,9},{9,8},{10,11... | collective-permute-start | bytes 3194888 | tf_op jit(solution)/shard_map/ppermute | solution.py:23
  79.4 19.1 %collective-permute-start.17 = (bf16[384,1024]{1,0:T(8,128)(2,1)}, bf16[384,1024]{1,0:T(8,128)(2,1)}, u32[]{:S(2)}, u32[]{:S(2)}) collective-permute-start(bf16[384,1024]{1,0:T(8,128)(2,1)} %get-tuple-element.50.refs_12_), channel_id=1, source_target_pairs={{0,2},{1,3},{2,0},{3,1},{4,6},{5,7},{6,4},{7,5},{8,10},{9,11},{10,... | collective-permute-start | bytes 2359304 | tf_op jit(solution)/shard_map/ppermute | solution.py:23
  81.0 22.1 %collective-permute-start.19 = (bf16[384,1024]{1,0:T(8,128)(2,1)}, bf16[384,1024]{1,0:T(8,128)(2,1)}, u32[]{:S(2)}, u32[]{:S(2)}) collective-permute-start(bf16[384,1024]{1,0:T(8,128)(2,1)} %get-tuple-element.49.refs_13_), channel_id=1, source_target_pairs={{0,4},{1,5},{2,6},{3,7},{4,0},{5,1},{6,2},{7,3},{8,12},{9,13},{10,... | collective-permute-start | bytes 2359304 | tf_op jit(solution)/shard_map/ppermute | solution.py:23
  81.0 23.1 %collective-permute-start.6 = (bf16[256,1024]{1,0:T(8,128)(2,1)}, bf16[256,1024]{1,0:T(8,128)(2,1)}, u32[]{:S(2)}, u32[]{:S(2)}) collective-permute-start(bf16[256,1024]{1,0:T(8,128)(2,1)} %collective-permute-done.5.refs_2_), channel_id=1, source_target_pairs={{0,8},{1,9},{2,10},{3,11},{4,12},{5,13},{6,14},{7,15},{8,16},{9,17... | collective-permute-start | bytes 1572872 | tf_op jit(solution)/shard_map/ppermute | solution.py:23
  85.8 0.9 copy-start.15
  86.7 0.7 copy-start.27
  87.4 42.7 %all-to-all-start = ((bf16[16,96,256]{2,1,0:T(8,128)(2,1)}), bf16[16,96,256]{2,1,0:T(8,128)(2,1)}, u32[]{:S(2)}, u32[]{:S(2)}) async-start(bf16[16,96,256]{2,1,0:T(8,128)(2,1)} %copy-done.15), calls=%async_computation | async-start | bytes 1572864 | tf_op jit(solution)/shard_map/all_to_all | solution.py:429
  99.5 6.7 %copy-start.2 = (bf16[336,1024]{1,0:T(8,128)(2,1)S(1)}, bf16[336,1024]{1,0:T(8,128)(2,1)}, u32[]{:S(2)}) copy-start(bf16[336,1024]{1,0:T(8,128)(2,1)} %copy-done) | copy-start | bytes 2064388
  99.5 6.7 %copy-start.5 = (bf16[336,1024]{1,0:T(8,128)(2,1)S(1)}, bf16[336,1024]{1,0:T(8,128)(2,1)}, u32[]{:S(2)}) copy-start(bf16[336,1024]{1,0:T(8,128)(2,1)} %copy-done.3) | copy-start | bytes 2064388
  99.5 6.7 %copy-start.26 = (bf16[2,256,256]{2,1,0:T(8,128)(2,1)S(1)}, bf16[2,256,256]{2,1,0:T(8,128)(2,1)}, u32[]{:S(2)}) copy-start(bf16[2,256,256]{2,1,0:T(8,128)(2,1)} %copy-done.25) | copy-start | bytes 786436
  99.5 6.7 %copy-start.28 = (bf16[512,256]{1,0:T(8,128)(2,1)S(1)}, bf16[512,256]{1,0:T(8,128)(2,1)}, u32[]{:S(2)}) copy-start(bf16[512,256]{1,0:T(8,128)(2,1)} %copy-done.27) | copy-start | bytes 786436
  105.3 19.9 %collective-permute-start.21 = (bf16[384,1024]{1,0:T(8,128)(2,1)S(1)}, bf16[384,1024]{1,0:T(8,128)(2,1)S(1)}, u32[]{:S(2)}, u32[]{:S(2)}) collective-permute-start(bf16[384,1024]{1,0:T(8,128)(2,1)S(1)} %get-tuple-element.47), channel_id=1, source_target_pairs={{0,2},{1,3},{2,0},{3,1},{4,6},{5,7},{6,4},{7,5},{8,10},{9,11},{10,... | collective-permute-start | bytes 2359304 | tf_op jit(solution)/shard_map/ppermute | solution.py:23
  105.4 19.8 %collective-permute-start.18 = (bf16[384,1024]{1,0:T(8,128)(2,1)S(1)}, bf16[384,1024]{1,0:T(8,128)(2,1)S(1)}, u32[]{:S(2)}, u32[]{:S(2)}) collective-permute-start(bf16[384,1024]{1,0:T(8,128)(2,1)S(1)} %get-tuple-element.48), channel_id=1, source_target_pairs={{0,4},{1,5},{2,6},{3,7},{4,0},{5,1},{6,2},{7,3},{8,12},{9,13},{10,... | collective-permute-start | bytes 2359304 | tf_op jit(solution)/shard_map/ppermute | solution.py:23
  113.3 1.0 copy-start.11
  114.2 1.0 copy-start.13
  125.9 0.9 copy-start.7
  126.8 13.6 %collective-permute-start.22 = (bf16[128,1024]{1,0:T(8,128)(2,1)}, bf16[128,1024]{1,0:T(8,128)(2,1)S(1)}, u32[]{:S(2)}, u32[]{:S(2)}) collective-permute-start(bf16[128,1024]{1,0:T(8,128)(2,1)} %slice.86), channel_id=1, source_target_pairs={{0,4},{1,5},{2,6},{3,7},{4,0},{5,1},{6,2},{7,3},{8,12},{9,13},{10,... | collective-permute-start | bytes 786440 | tf_op jit(solution)/shard_map/ppermute | solution.py:23
  127.4 5.3 %copy-start.8 = (bf16[384,1024]{1,0:T(8,128)(2,1)S(1)}, bf16[384,1024]{1,0:T(8,128)(2,1)}, u32[]{:S(2)}) copy-start(bf16[384,1024]{1,0:T(8,128)(2,1)} %copy-done.7) | copy-start | bytes 2359300
  128.1 0.9 copy-start.9
  129.0 11.4 %collective-permute-start.20 = (bf16[128,1024]{1,0:T(8,128)(2,1)}, bf16[128,1024]{1,0:T(8,128)(2,1)S(1)}, u32[]{:S(2)}, u32[]{:S(2)}) collective-permute-start(bf16[128,1024]{1,0:T(8,128)(2,1)} %slice.84), channel_id=1, source_target_pairs={{0,2},{1,3},{2,0},{3,1},{4,6},{5,7},{6,4},{7,5},{8,10},{9,11},{10,... | collective-permute-start | bytes 786440 | tf_op jit(solution)/shard_map/ppermute | solution.py:23
  132.6 1.1 copy-start.10
  133.8 1.2 copy-start.12
  135.0 1.2 copy-start.14
  136.2 0.9 copy-start.24
  142.7 5.5 %collective-permute-start.23 = (f32[256,1024]{1,0:T(8,128)S(1)}, f32[256,1024]{1,0:T(8,128)S(1)}, u32[]{:S(2)}, u32[]{:S(2)}) collective-permute-start(f32[256,1024]{1,0:T(8,128)S(1)} %get-tuple-element.39), channel_id=1, source_target_pairs={{0,1},{1,0},{2,3},{3,2},{4,5},{5,4},{6,7},{7,6},{8,9},{9,8},{10,11... | collective-permute-start | bytes 3145736 | tf_op jit(solution)/shard_map/ppermute | solution.py:23
  149.1 8.3 %collective-permute-start.24 = (bf16[128,1024]{1,0:T(8,128)(2,1)S(1)}, bf16[128,1024]{1,0:T(8,128)(2,1)S(1)}, u32[]{:S(2)}, u32[]{:S(2)}) collective-permute-start(bf16[128,1024]{1,0:T(8,128)(2,1)S(1)} %get-tuple-element.41), channel_id=1, source_target_pairs={{0,1},{1,2},{2,3},{3,4},{4,5},{5,6},{6,7},{7,8},{8,9},{9,10},{10,1... | collective-permute-start | bytes 786440 | tf_op jit(solution)/shard_map/ppermute | solution.py:36
  154.0 9.5 %collective-permute-start.25 = (bf16[128,1024]{1,0:T(8,128)(2,1)S(1)}, bf16[128,1024]{1,0:T(8,128)(2,1)S(1)}, u32[]{:S(2)}, u32[]{:S(2)}) collective-permute-start(bf16[128,1024]{1,0:T(8,128)(2,1)S(1)} %get-tuple-element.42), channel_id=1, source_target_pairs={{1,0},{2,1},{3,2},{4,3},{5,4},{6,5},{7,6},{8,7},{9,8},{10,9},{11,1... | collective-permute-start | bytes 786440 | tf_op jit(solution)/shard_map/ppermute | solution.py:36

commit v3 on v2

--- a/solution.py
+++ b/solution.py
@@ -42,9 +42,9 @@
     y = (chip // 2) % 2
     x = chip % 2
     if group & 1:
+        y = 1 - y
+    if group & 2:
         x = 1 - x
-    if group & 2:
-        y = 1 - y
     return lax.rem(z + planes - step, planes) * 4 + y * 2 + x
 
 
@@ -58,8 +58,6 @@
         self.parts = parts
 
     def part(self, kind, begin, count):
-        if not count:
-            return None
         parts, row, seen, first = [], 0, 0, None
         for k, group, step, at, n in self.parts:
             if k == kind and group in (1, 2):
@@ -69,43 +67,65 @@
                     first = row + low - seen if first is None else first
                 seen += n
             row += n
-        return Rows(self.array[first : first + count], parts)
+        return first, count, parts
 
     def count(self, kind):
         return sum(n for k, group, _, _, n in self.parts if k == kind and group in (1, 2))
 
     def swapped(self, size, group):
         parts = [(k, g ^ group, s, at, n) for k, g, s, at, n in self.parts]
-        return Rows(swap(self.array, size, 2 * group), parts)
+        return Rows(swap(self.array, size, 4 // group), parts)
 
     def turned(self, size, planes):
         parts = [(k, g, s + planes, at, n) for k, g, s, at, n in self.parts]
         return Rows(turn(self.array, size, planes), parts)
 
 
-def joined(rows):
-    rows = [r for r in rows if r is not None]
-    if len(rows) == 1:
-        return rows[0]
-    return Rows(jnp.concatenate([r.array for r in rows]), [p for r in rows for p in r.parts])
-
-
-def halves(rows, kind, unit):
-    total = rows.count(kind)
-    cut = total // 2 // unit * unit
-    return cut, total - cut
+def packed(takes, sources):
+    takes = [take for take in takes if take]
+    counts = [sum(n for _, _, n in take) for take in takes]
+
+    def kernel(*refs):
+        for take, out in zip(takes, refs[len(sources) :]):
+            row = 0
+            for source, first, n in take:
+                out[row : row + n] = refs[source][first : first + n]
+                row += n
+
+    return pl.pallas_call(
+        kernel,
+        out_shape=[jax.ShapeDtypeStruct((n, sources[0].shape[1]), BF16) for n in counts],
+        in_specs=[VMEM] * len(sources),
+        out_specs=[VMEM] * len(takes),
+        compiler_params=pltpu.CompilerParams(vmem_limit_bytes=12 * MIB),
+        cost_estimate=pl.CostEstimate(flops=0, bytes_accessed=4 * MIB, transcendentals=0),
+        name="packed",
+    )(*sources)
 
 
 def across(line, previous, kinds, size):
-    by_x, by_y = list(line), list(line)
-    if previous is not None:
-        over_x, over_y = previous
+    rows = [*line, *(previous or ())]
+    takes, parts = ([], []), ([], [])
+    for n, r in enumerate(line):
+        for way in range(2):
+            takes[way].append((n, 0, r.array.shape[0]))
+            parts[way].extend(r.parts)
+    if previous:
         for kind, unit in kinds:
-            cut, rest = halves(over_x, kind, unit)
-            by_y.append(over_x.part(kind, 0, cut))
-            by_x.append(over_y.part(kind, cut, rest))
-    sent = [joined(rows) for rows in (by_x, by_y) if any(r is not None for r in rows)]
-    return sent, [rows.swapped(size, 1 + (i == len(sent) - 1)) for i, rows in enumerate(sent)]
+            total = previous[0].count(kind)
+            cut = total // 2 // unit * unit
+            for way, begin, count in ((1, 0, cut), (0, cut, total - cut)):
+                if count:
+                    first, n, what = previous[1 - way].part(kind, begin, count)
+                    takes[way].append((len(line) + 1 - way, first, n))
+                    parts[way].extend(what)
+    if previous:
+        arrays = packed(takes, [r.array for r in rows])
+    else:
+        arrays = [jnp.concatenate([r.array for r in line])] * 2
+    ways = [way for way in range(2) if takes[way]]
+    sent = [Rows(array, parts[way]) for way, array in zip(ways, arrays)]
+    return sent, [r.swapped(size, 1 + way) for way, r in zip(ways, sent)]
 
 
 def split_tokens(tokens, size):
@@ -114,7 +134,7 @@
     chips = size // 2
     planes = size // 8
 
-    def kernel(tok, mine, other):
+    def kernel(tok, mine, other, far):
         me = lax.axis_index("fsdp")
         core = lax.rem(me, 2)
         for i in range(chips):
@@ -122,13 +142,14 @@
             for ref, parity in ((other, 1 - core), (mine, core)):
                 start = pl.multiple_of((2 * chip + parity) * depth, depth)
                 ref[:, i * depth : (i + 1) * depth] = tok[:, pl.ds(start, depth)]
+        far[...] = mine[:, chips * depth // 2 :]
 
     half = jax.ShapeDtypeStruct((rows, width // 2), tokens.dtype)
     return pl.pallas_call(
         kernel,
-        out_shape=(half, half),
+        out_shape=(half, half, jax.ShapeDtypeStruct((rows, width // 4), tokens.dtype)),
         in_specs=[VMEM],
-        out_specs=(VMEM, VMEM),
+        out_specs=(VMEM, VMEM, VMEM),
         compiler_params=pltpu.CompilerParams(vmem_limit_bytes=16 * MIB),
         cost_estimate=pl.CostEstimate(flops=0, bytes_accessed=4 * rows * width, transcendentals=0),
         name="split_tokens",
@@ -204,13 +225,14 @@
     )(tok, tok_in, *(p.array for p in pieces), grad, grad_in, *after)
 
 
-def adapter_terms(own, other, tok, tok_in, grad, grad_in, size, kind):
+def adapter_terms(own, other, tok, tok_in, grad, grad_in, size, kind, after):
     rows = tok.shape[0]
     depth = tok.shape[1] * 2 // size
     planes = size // 8
     slices = 512 // depth
 
-    def kernel(own, other, tok, tok_in, grad, grad_in, hidden, names, terms):
+    def kernel(own, other, tok, tok_in, grad, grad_in, *refs):
+        hidden, names, terms = refs[-3:]
         me = lax.axis_index("fsdp")
         table = own[4 * rows :] + other[4 * rows :]
         names[...] = table
@@ -256,14 +278,14 @@
             jax.ShapeDtypeStruct((16, WIDE), F32),
             jax.ShapeDtypeStruct((size // 2, 96, depth), kind),
         ),
-        in_specs=[VMEM] * 6,
+        in_specs=[VMEM] * 6 + [ANY] * len(after),
         out_specs=(VMEM, VMEM, VMEM),
         compiler_params=pltpu.CompilerParams(vmem_limit_bytes=24 * MIB),
         cost_estimate=pl.CostEstimate(
             flops=4 * rows * tok.shape[1] * 128, bytes_accessed=9 * MIB, transcendentals=0
         ),
         name="adapter_terms",
-    )(own, other, tok, tok_in, grad, grad_in)
+    )(own, other, tok, tok_in, grad, grad_in, *after)
 
 
 def sum_terms(terms, names, size):
@@ -310,7 +332,7 @@
     )(terms, names)
 
 
-def value_products(tok, tok_in, pieces, so_far, adapters, size, after):
+def value_products(tok, tok_in, tok_far, pieces, so_far, adapters, size, after):
     rows = tok.shape[0]
     depth = tok.shape[1] * 2 // size
     planes = size // 8
@@ -321,42 +343,49 @@
     for n, piece in enumerate(pieces):
         row = 0
         for kind, group, step, at, height in piece.parts:
-            if kind == "wide":
-                terms.append((n, row, (group * planes + step) * depth + at, height))
+            terms.append((n, row, (group * planes + step) * depth + at, height))
             row += height
-    joint = so_far or adapters
-
-    def kernel(tok, tok_in, *refs):
-        refs, joint, (keep, give) = refs[:count], refs[count : count + 2], refs[-2:]
+    joint = (*so_far, *adapters)
+    n_joint = len(joint)
+
+    def kernel(tok, tok_in, far, far_in, *refs):
+        refs, joint, (keep, give) = refs[:count], refs[count : count + n_joint], refs[-2:]
         core = lax.rem(lax.axis_index("fsdp"), 2)
-        for half, (source, out) in enumerate(((tok, keep), (tok_in, give))):
-            for left in range(0, width, 256):
-                here = slice(left, left + 256)
-                if so_far:
-                    total = joint[half][:, here]
-                else:
-                    owner = left // own_columns
-                    place = (owner // 2 * own_columns + left % own_columns) // 256
-                    scale = jnp.where(core == owner % 2, SCALE, 0.0).astype(F32)
-                    total = scale * dot(joint[0][half * rows : (half + 1) * rows], joint[1][place])
-                for n, row, spot, height in terms:
-                    total += dot(source[:, spot : spot + height], refs[n][row : row + height, here])
-                out[:, here] = total
-
-    share = jax.ShapeDtypeStruct((rows, width), F32)
+        for chip in range(2):
+            for half, out in enumerate((keep, give)):
+                to = slice(chip * rows, (chip + 1) * rows)
+                for left in range(0, width, 256):
+                    here = slice(left, left + 256)
+                    total = joint[half][to, here] if so_far else jnp.zeros((rows, 256), F32)
+                    if adapters and not chip:
+                        hidden, table = joint[-2:]
+                        owner = left // own_columns
+                        place = (owner // 2 * own_columns + left % own_columns) // 256
+                        scale = jnp.where(core == owner % 2, SCALE, 0.0).astype(F32)
+                        total += scale * dot(hidden[half * rows : (half + 1) * rows], table[place])
+                    for n, row, spot, height in terms:
+                        columns = slice(spot, spot + height)
+                        if chip:
+                            left_side = (far, far_in)[half][:, columns]
+                        else:
+                            left_side = (tok, tok_in)[half][:, columns]
+                        total += dot(left_side, refs[n][row : row + height, here])
+                    out[to, here] = total
+
+    share = jax.ShapeDtypeStruct((2 * rows, width), F32)
     return pl.pallas_call(
         kernel,
         out_shape=(share, share),
-        in_specs=[VMEM] * (4 + count) + [ANY] * len(after),
+        in_specs=[VMEM] * (4 + count + n_joint) + [ANY] * len(after),
         out_specs=(VMEM, VMEM),
-        compiler_params=pltpu.CompilerParams(vmem_limit_bytes=28 * MIB),
+        compiler_params=pltpu.CompilerParams(vmem_limit_bytes=40 * MIB),
         cost_estimate=pl.CostEstimate(
-            flops=4 * rows * sum(t[3] for t in terms) * width,
+            flops=8 * rows * sum(t[3] for t in terms) * width,
             bytes_accessed=4 * MIB,
             transcendentals=0,
         ),
         name="value_products",
-    )(tok, tok_in, *(p.array for p in pieces), *joint, *after)
+    )(tok, tok_in, *tok_far, *(p.array for p in pieces), *joint, *after)
 
 
 def body(
@@ -392,20 +421,21 @@
     low_piece = jnp.concatenate([jnp.concatenate(downs, axis=1), last_rows])
     low = [Rows(low_piece, [("low", 0, 0, 0, deep + 16)])]
     wide = [Rows(frozen_value_weight, [("wide", 0, 0, 0, depth)])]
-    kinds = (("wide", 128), ("low", 16))
+    kinds = (("low", 16),)
 
     low += [low[0].turned(size, step) for step in range(1, planes)]
     wide[0].array = ordered(wide[0].array, *(r.array for r in low[1:]))
     for step in range(planes - 1):
         wide.append(wide[-1].turned(size, 1))
-    _, stage0 = across([Rows(frozen_value_weight, wide[0].parts), low[0]], None, kinds, size)
-    _, stage1 = across(low[1:], stage0, kinds, size)
-    _, stage2 = across([wide[1]], stage1, kinds, size)
-    sent, stage = across([wide[2]], stage2, kinds, size)
-    stages = [stage0, stage1, stage2, stage]
-
-    tok, tok_out = split_tokens(tokens, size)
+    wide[0].array = frozen_value_weight
+    wide_y = [r.swapped(size, 1) for r in wide]
+    _, stage0 = across(low[:1], None, kinds, size)
+    wide_y[0] = Rows(ordered(frozen_value_weight, *(r.array for r in stage0)), wide[0].parts).swapped(size, 1)
+
+    tok, tok_out, far_out = split_tokens(tokens, size)
+    far_own = swap(far_out, size, 2)
     tok_in = swap(tok_out, size, 1)
+    near = tok.shape[1] // 2
 
     slots = cotangent.reshape(-1, BLOCK, width)
     from_upper = shift(slots[0], size, -1)
@@ -417,36 +447,38 @@
     grad_mine = jnp.where(core == 0, even, odd)
     grad_in = swap(jnp.where(core == 0, odd, even), size, 1)
 
+    _, stage1 = across(low[1:], stage0, kinds, size)
+    _, stage2 = across([], stage1, kinds, size)
+    far_columns = ordered(tok_in[:, near:], *(r.array for r in stage1))
+    tok_far = (far_own, swap(far_columns, size, 2))
     share, table = low_rank_products(
         tok, tok_in, [*low, *stage0, *stage1, *stage2], grad_mine, grad_in, size,
-        [r.array for r in sent],
+        (wide[1].array, far_columns, ),
     )
     hidden, names, terms = adapter_terms(
-        share, swap(share, size, 1), tok, tok_in, grad_mine, grad_in, size, BF16
+        share, swap(share, size, 1), tok, tok_in, grad_mine, grad_in, size, BF16, ()
     )
     terms_sent = terms
     groups = [list(range(core, size, 2)) for core in range(2)]
     terms = lax.all_to_all(terms, "fsdp", 0, 0, axis_index_groups=groups, tiled=True)
     down_gradient, up_gradient = sum_terms(terms, names, size)
 
-    early = [*wide[:3], *(r for stage in stages for r in stage)]
-    shares = value_products(tok, tok_in, early, (), (hidden, table), size, ())
-    wide[3].array = ordered(wide[3].array, terms_sent)
-    for step in range(3, planes):
-        _, stage = across([wide[step]], stages[-1], kinds, size)
-        stages.append(stage)
-    for rows in stages[-1]:
-        rows.array = ordered(rows.array, shares[0])
-    _, stage = across([], stages[-1], kinds, size)
-    late = [*wide[3:], *(r for s in stages[4:] for r in s)]
-    shares = value_products(tok, tok_in, late, shares, (), size, (down_gradient,))
-    keep, give = value_products(tok, tok_in, stage, shares, (), size, ())
-    total = (keep + swap(give, size, 1)).reshape(-1, BLOCK, width)
+    early = [*wide, *wide_y[:-2]]
+    late = wide_y[-2:]
+    shares = value_products(tok, tok_in, tok_far, early, (), (), size, ())
+    keep, give = value_products(
+        tok, tok_in, tok_far, late, shares, (hidden, table), size, ()
+    )
+    both = keep + swap(give, size, 1)
+    rows = both.shape[0] // 2
+    far = swap(both[rows:].astype(BF16), size, 2)
+    total = (both[:rows] + far.astype(F32)).reshape(-1, BLOCK, width)
     value = jnp.where(valid, total, 0.0).astype(BF16)
     right = jnp.sum(jnp.where(goes_right, value, zero), axis=0)
     left = jnp.sum(jnp.where(goes_left, value, zero), axis=0)
     own = jnp.where(stays, value, zero)
     lower, upper = shift(right, size, 1), shift(left, size, -1)
+    own = ordered(own, down_gradient)
     layer_out = jnp.concatenate([lower[None], own, upper[None]]).reshape(-1, width)
     return layer_out, down_gradient, up_gradient
 

time: 166 us -> 142 us (0.86)
  the two profiles are of different devices: /device:TPU:7 before, /device:TPU:0 now
where the time goes in v3:
time: 142 us; the launch traced here: 140 us
  waiting for transfers between devices  76.3 us (54%)
  starting transfers between devices  35.3 us (25%)
  Pallas kernels  15.1 us (11%)
  local copies, waits for them, and re-layouts  6.71 us (5%)
  other arithmetic  5.3 us (4%)
    ppermute x23, waiting for transfers between devices, send_to(): return lax.ppermute(x, 'fsdp', [(i, target(i)) for i in range(size)])  69.9 us
    ppermute x23, starting transfers between devices, send_to(): return lax.ppermute(x, 'fsdp', [(i, target(i)) for i in range(size)])  23.1 us
    ppermute x4, starting transfers between devices, shift(): return lax.ppermute(x, 'fsdp', pairs)  7.25 us
    pallas_call x2, Pallas kernels, value_products(): pl.pallas_call(kernel, out_shape=(share, share), in_specs=[VMEM] * (4 + c...  6.55 us
    all_to_all x1, waiting for transfers between devices, body(): lax.all_to_all(terms, 'fsdp', 0, 0, axis_index_groups=groups, tiled=True)  6.38 us
    all_to_all x1, starting transfers between devices, body(): lax.all_to_all(terms, 'fsdp', 0, 0, axis_index_groups=groups, tiled=True)  4.92 us
    unnamed x46, local copies, waits for them, and re-layouts  4.6 us
  transfers between devices with their start and end apart: 28, of which 13 were waited for; matrix products, arithmetic and copies ran while one was open for 4% of the time, Pallas kernels for 7%

profile of v3, /device:TPU:0, one launch (start us, length us, event | category | flops | bytes accessed | tf_op | source)
XLA Modules:
  0.0 139.7 jit_solution(13924585568505435331)
XLA Ops:
  0.6 2.2 %copy-done.2 = bf16[256,8192]{1,0:T(8,128)(2,1)S(1)} copy-done((bf16[256,8192]{1,0:T(8,128)(2,1)S(1)}, bf16[256,8192]{1,0:T(8,128)(2,1)}, u32[]{:S(2)}) %copy-start.2) | copy-done | bytes 4194328
  2.8 2.1 %split_tokens.1 = (bf16[256,4096]{1,0:T(8,128)(2,1)S(1)}, bf16[256,4096]{1,0:T(8,128)(2,1)}, bf16[256,2048]{1,0:T(8,128)(2,1)S(1)}) custom-call(bf16[256,8192]{1,0:T(8,128)(2,1)S(1)} %copy-done.2), custom_call_target="tpu_custom_call" | custom-call | bytes 8388608 | tf_op jit(solution)/shard_map/split_tokens/pallas_call | solution.py:148
  5.0 1.4 copy-done
  6.3 1.0 copy-done.14
  7.3 0.5 collective-permute-start
  7.8 0.1 select_convert_fusion.1
  7.9 2.6 %collective-permute-start.6 = (bf16[80,1024]{1,0:T(8,128)(2,1)S(1)}, bf16[80,1024]{1,0:T(8,128)(2,1)S(1)}, u32[]{:S(2)}, u32[]{:S(2)}) collective-permute-start(bf16[80,1024]{1,0:T(8,128)(2,1)S(1)} %fusion.8.refs_0_), channel_id=1, source_target_pairs={{0,2},{1,3},{2,0},{3,1},{4,6},{5,7},{6,4},{7,5},{8,10},{9,11},{10,... | collective-permute-start | bytes 491528 | tf_op jit(solution)/shard_map/ppermute | solution.py:23
  10.5 1.4 %collective-permute-start.5 = (bf16[80,1024]{1,0:T(8,128)(2,1)S(1)}, bf16[80,1024]{1,0:T(8,128)(2,1)S(1)}, u32[]{:S(2)}, u32[]{:S(2)}) collective-permute-start(bf16[80,1024]{1,0:T(8,128)(2,1)S(1)} %fusion.8.refs_0_), channel_id=1, source_target_pairs={{0,4},{1,5},{2,6},{3,7},{4,0},{5,1},{6,2},{7,3},{8,12},{9,13},{10,... | collective-permute-start | bytes 491528 | tf_op jit(solution)/shard_map/ppermute | solution.py:23
  11.9 3.6 %collective-permute-start.4 = (bf16[80,1024]{1,0:T(8,128)(2,1)S(1)}, bf16[80,1024]{1,0:T(8,128)(2,1)S(1)}, u32[]{:S(2)}, u32[]{:S(2)}) collective-permute-start(bf16[80,1024]{1,0:T(8,128)(2,1)S(1)} %fusion.8.refs_0_), channel_id=1, source_target_pairs={{0,24},{1,25},{2,26},{3,27},{4,28},{5,29},{6,30},{7,31},{8,0},{9,1... | collective-permute-start | bytes 491528 | tf_op jit(solution)/shard_map/ppermute | solution.py:23
  15.5 1.9 %fusion.10 = (bf16[128,1024]{1,0:T(8,128)(2,1)}, bf16[128,1024]{1,0:T(8,128)(2,1)}) fusion(bf16[512,1024]{1,0:T(8,128)(2,1)} %param.15), kind=kLoop, calls=%fused_computation.31 | loop fusion | bytes 1048576 | tf_op jit(solution)/shard_map/slice | solution.py:441
  17.3 0.0 collective-permute-done.6.refs_4_.refs_5_
  17.4 1.0 collective-permute-start.2
  18.4 1.3 collective-permute-start.19
  19.7 0.4 collective-permute-done.4.refs_2_.refs_3_
  20.1 3.4 %collective-permute-start.20 = (bf16[128,1024]{1,0:T(8,128)(2,1)}, bf16[128,1024]{1,0:T(8,128)(2,1)}, u32[]{:S(2)}, u32[]{:S(2)}) collective-permute-start(bf16[128,1024]{1,0:T(8,128)(2,1)} %get-tuple-element.52), channel_id=1, source_target_pairs={{0,1},{1,2},{2,3},{3,4},{4,5},{5,6},{6,7},{7,8},{8,9},{9,10},{10,1... | collective-permute-start | bytes 786440 | tf_op jit(solution)/shard_map/ppermute | solution.py:36
  23.5 6.1 %collective-permute-done.3.refs_1_.refs_2_ = bf16[80,1024]{1,0:T(8,128)(2,1)S(1)} collective-permute-done((bf16[80,1024]{1,0:T(8,128)(2,1)S(1)}, bf16[80,1024]{1,0:T(8,128)(2,1)S(1)}, u32[]{:S(2)}, u32[]{:S(2)}) %collective-permute-start.3) | collective-permute-done | bytes 163872 | tf_op jit(solution)/shard_map/ppermute | solution.py:23
  29.6 1.1 packed.2
  30.7 0.4 collective-permute-start.8
  31.2 0.7 collective-permute-start.7
  31.8 0.1 broadcast_bitcast_fusion
  31.9 1.7 %collective-permute-start.10 = (bf16[256,1024]{1,0:T(8,128)(2,1)}, bf16[256,1024]{1,0:T(8,128)(2,1)S(1)}, u32[]{:S(2)}, u32[]{:S(2)}) collective-permute-start(bf16[256,1024]{1,0:T(8,128)(2,1)} %refs_0_.1), channel_id=1, source_target_pairs={{0,8},{1,9},{2,10},{3,11},{4,12},{5,13},{6,14},{7,15},{8,16},{9,17... | collective-permute-start | bytes 1572872 | tf_op jit(solution)/shard_map/ppermute | solution.py:23
  33.6 0.1 iota_compare_fusion.4
  33.7 1.4 fusion.1
  35.1 0.0 copy-start.16
  35.2 0.1 collective-permute-start.21
  35.3 9.7 %collective-permute-done.8.refs_1_.refs_7_ = bf16[272,1024]{1,0:T(8,128)(2,1)S(1)} collective-permute-done((bf16[272,1024]{1,0:T(8,128)(2,1)}, bf16[272,1024]{1,0:T(8,128)(2,1)S(1)}, u32[]{:S(2)}, u32[]{:S(2)}) %collective-permute-start.8) | collective-permute-done | bytes 557088 | tf_op jit(solution)/shard_map/ppermute | solution.py:23
  45.0 1.0 collective-permute-done.7.refs_0_.refs_6_
  46.0 1.6 %collective-permute-start.18 = (bf16[112,1024]{1,0:T(8,128)(2,1)S(1)}, bf16[112,1024]{1,0:T(8,128)(2,1)S(1)}, u32[]{:S(2)}, u32[]{:S(2)}) collective-permute-start(bf16[112,1024]{1,0:T(8,128)(2,1)S(1)} %get-tuple-element.36), channel_id=1, source_target_pairs={{0,2},{1,3},{2,0},{3,1},{4,6},{5,7},{6,4},{7,5},{8,10},{9,11},{10,... | collective-permute-start | bytes 688136 | tf_op jit(solution)/shard_map/ppermute | solution.py:23
  47.6 0.5 collective-permute-start.1
  48.1 0.5 collective-permute-start.11
  48.6 0.6 collective-permute-start.17
  49.2 0.1 slice.52.refs_13_
  49.3 1.5 %collective-permute-start.15 = (bf16[256,1024]{1,0:T(8,128)(2,1)S(1)}, bf16[256,1024]{1,0:T(8,128)(2,1)S(1)}, u32[]{:S(2)}, u32[]{:S(2)}) collective-permute-start(bf16[256,1024]{1,0:T(8,128)(2,1)S(1)} %copy-done.16), channel_id=1, source_target_pairs={{0,4},{1,5},{2,6},{3,7},{4,0},{5,1},{6,2},{7,3},{8,12},{9,13},{10,... | collective-permute-start | bytes 1572872 | tf_op jit(solution)/shard_map/ppermute | solution.py:23
  50.8 3.8 %collective-permute-done.18.refs_9_ = bf16[112,1024]{1,0:T(8,128)(2,1)S(1)} collective-permute-done((bf16[112,1024]{1,0:T(8,128)(2,1)S(1)}, bf16[112,1024]{1,0:T(8,128)(2,1)S(1)}, u32[]{:S(2)}, u32[]{:S(2)}) %collective-permute-start.18) | collective-permute-done | bytes 229408 | tf_op jit(solution)/shard_map/ppermute | solution.py:23
  54.6 1.5 %collective-permute-start.9 = (bf16[256,2048]{1,0:T(8,128)(2,1)S(1)}, bf16[256,2048]{1,0:T(8,128)(2,1)S(1)}, u32[]{:S(2)}, u32[]{:S(2)}) collective-permute-start(bf16[256,2048]{1,0:T(8,128)(2,1)S(1)} %slice.52.refs_13_), channel_id=1, source_target_pairs={{0,2},{1,3},{2,0},{3,1},{4,6},{5,7},{6,4},{7,5},{8,10},{9,11},{10,... | collective-permute-start | bytes 3145736 | tf_op jit(solution)/shard_map/ppermute | solution.py:23
  56.1 1.7 %collective-permute-done.17.refs_8_ = bf16[128,1024]{1,0:T(8,128)(2,1)S(1)} collective-permute-done((bf16[128,1024]{1,0:T(8,128)(2,1)S(1)}, bf16[128,1024]{1,0:T(8,128)(2,1)S(1)}, u32[]{:S(2)}, u32[]{:S(2)}) %collective-permute-start.17) | collective-permute-done | bytes 262176 | tf_op jit(solution)/shard_map/ppermute | solution.py:23
  57.9 1.5 %low_rank_products.1 = (f32[1040,256]{1,0:T(8,128)S(1)}, bf16[2,256,256]{2,1,0:T(8,128)(2,1)S(1)}) custom-call(bf16[256,4096]{1,0:T(8,128)(2,1)S(1)} %copy-done.1, bf16[256,4096]{1,0:T(8,128)(2,1)S(1)} %collective-permute-done.tok_in, bf16[80,1024]{1,0:T(8,128)(2,1)S(1)} %fusion.8.refs_0_, bf16[80,1024]{1,0:T(8,128)(2,1)S(1)} %copy-done.13, ...), custom_call_target="tpu_custom_call" | custom-call | flops 1207959552 | bytes 9437184 | tf_op jit(solution)/shard_map/low_rank_products/pallas_call | solution.py:211
  59.4 0.1 collective-permute-start.22
  59.5 2.1 %collective-permute-done.11.refs_2_ = bf16[256,1024]{1,0:T(8,128)(2,1)S(1)} collective-permute-done((bf16[256,1024]{1,0:T(8,128)(2,1)S(1)}, bf16[256,1024]{1,0:T(8,128)(2,1)S(1)}, u32[]{:S(2)}, u32[]{:S(2)}) %collective-permute-start.11) | collective-permute-done | bytes 524320 | tf_op jit(solution)/shard_map/ppermute | solution.py:23
  61.5 0.6 collective-permute-start.13
  62.1 3.8 %collective-permute-done.15.refs_4_ = bf16[256,1024]{1,0:T(8,128)(2,1)S(1)} collective-permute-done((bf16[256,1024]{1,0:T(8,128)(2,1)S(1)}, bf16[256,1024]{1,0:T(8,128)(2,1)S(1)}, u32[]{:S(2)}, u32[]{:S(2)}) %collective-permute-start.15) | collective-permute-done | bytes 524320 | tf_op jit(solution)/shard_map/ppermute | solution.py:23
  65.9 0.7 collective-permute-start.16
  66.6 10.5 %collective-permute-done.1.far = bf16[256,2048]{1,0:T(8,128)(2,1)S(1)} collective-permute-done((bf16[256,2048]{1,0:T(8,128)(2,1)S(1)}, bf16[256,2048]{1,0:T(8,128)(2,1)S(1)}, u32[]{:S(2)}, u32[]{:S(2)}) %collective-permute-start.1) | collective-permute-done | bytes 1048608 | tf_op jit(solution)/shard_map/ppermute | solution.py:23
  77.1 0.6 collective-permute-start.12
  77.7 1.4 %collective-permute-start.14 = (bf16[256,1024]{1,0:T(8,128)(2,1)S(1)}, bf16[256,1024]{1,0:T(8,128)(2,1)S(1)}, u32[]{:S(2)}, u32[]{:S(2)}) collective-permute-start(bf16[256,1024]{1,0:T(8,128)(2,1)S(1)} %collective-permute-done.13.refs_3_), channel_id=1, source_target_pairs={{0,4},{1,5},{2,6},{3,7},{4,0},{5,1},{6,2},{7,3},{8,12},{9,13},{10,... | collective-permute-start | bytes 1572872 | tf_op jit(solution)/shard_map/ppermute | solution.py:23
  79.1 17.8 %collective-permute-done.9.far_in = bf16[256,2048]{1,0:T(8,128)(2,1)S(1)} collective-permute-done((bf16[256,2048]{1,0:T(8,128)(2,1)S(1)}, bf16[256,2048]{1,0:T(8,128)(2,1)S(1)}, u32[]{:S(2)}, u32[]{:S(2)}) %collective-permute-start.9) | collective-permute-done | bytes 1048608 | tf_op jit(solution)/shard_map/ppermute | solution.py:23
  96.9 3.4 %value_products.2 = (f32[512,1024]{1,0:T(8,128)S(1)}, f32[512,1024]{1,0:T(8,128)S(1)}) custom-call(bf16[256,4096]{1,0:T(8,128)(2,1)S(1)} %copy-done.1, bf16[256,4096]{1,0:T(8,128)(2,1)S(1)} %collective-permute-done.tok_in, bf16[256,2048]{1,0:T(8,128)(2,1)S(1)} %collective-permute-done.1.far, bf16[256,2048]{1,0:T(8,128)(2,1)S(1)} %collective-permute-done.9.far_in, ...), custom_call_target="tpu_custom_call" | custom-call | flops 3221225472 | bytes 4194304 | tf_op jit(solution)/shard_map/value_products/pallas_call | solution.py:376
  100.3 2.3 %adapter_terms.1 = (bf16[512,256]{1,0:T(8,128)(2,1)S(1)}, f32[16,256]{1,0:T(8,128)S(1)}, bf16[16,96,256]{2,1,0:T(8,128)(2,1)}) custom-call(f32[1040,256]{1,0:T(8,128)S(1)} %get-tuple-element.37.own, f32[1040,256]{1,0:T(8,128)S(1)} %collective-permute-done.22.other, bf16[256,4096]{1,0:T(8,128)(2,1)S(1)} %copy-done.1, ...), custom_call_target="tpu_custom_call" | custom-call | flops 536870912 | bytes 9437184 | tf_op jit(solution)/shard_map/adapter_terms/pallas_call | solution.py:274
  102.7 3.1 %value_products.3 = (f32[512,1024]{1,0:T(8,128)S(1)}, f32[512,1024]{1,0:T(8,128)S(1)}) custom-call(bf16[256,4096]{1,0:T(8,128)(2,1)S(1)} %copy-done.1, bf16[256,4096]{1,0:T(8,128)(2,1)S(1)} %collective-permute-done.tok_in, bf16[256,2048]{1,0:T(8,128)(2,1)S(1)} %collective-permute-done.1.far, bf16[256,2048]{1,0:T(8,128)(2,1)S(1)} %collective-permute-done.9.far_in, ...), custom_call_target="tpu_custom_call" | custom-call | flops 1073741824 | bytes 4194304 | tf_op jit(solution)/shard_map/value_products/pallas_call | solution.py:376
  105.8 0.1 collective-permute-start.23
  105.9 4.1 %collective-permute-done.23 = f32[512,1024]{1,0:T(8,128)S(1)} collective-permute-done((f32[512,1024]{1,0:T(8,128)S(1)}, f32[512,1024]{1,0:T(8,128)S(1)}, u32[]{:S(2)}, u32[]{:S(2)}) %collective-permute-start.23) | collective-permute-done | bytes 2097184 | tf_op jit(solution)/shard_map/ppermute | solution.py:23
  110.1 0.6 add.18
  110.6 0.1 slice.64
  110.7 1.5 %collective-permute-start.24 = (bf16[256,1024]{1,0:T(8,128)(2,1)S(1)}, bf16[256,1024]{1,0:T(8,128)(2,1)S(1)}, u32[]{:S(2)}, u32[]{:S(2)}) collective-permute-start(bf16[256,1024]{1,0:T(8,128)(2,1)S(1)} %slice.64), channel_id=1, source_target_pairs={{0,2},{1,3},{2,0},{3,1},{4,6},{5,7},{6,4},{7,5},{8,10},{9,11},{10,... | collective-permute-start | bytes 1572872 | tf_op jit(solution)/shard_map/ppermute | solution.py:23
  112.3 4.9 %all-to-all-start = ((bf16[16,96,256]{2,1,0:T(8,128)(2,1)}), bf16[16,96,256]{2,1,0:T(8,128)(2,1)S(1)}, u32[]{:S(2)}, u32[]{:S(2)}) async-start(bf16[16,96,256]{2,1,0:T(8,128)(2,1)} %get-tuple-element.42), calls=%async_computation | async-start | bytes 1572864 | tf_op jit(solution)/shard_map/all_to_all | solution.py:463
  117.2 8.9 %collective-permute-done.24 = bf16[256,1024]{1,0:T(8,128)(2,1)S(1)} collective-permute-done((bf16[256,1024]{1,0:T(8,128)(2,1)S(1)}, bf16[256,1024]{1,0:T(8,128)(2,1)S(1)}, u32[]{:S(2)}, u32[]{:S(2)}) %collective-permute-start.24) | collective-permute-done | bytes 524320 | tf_op jit(solution)/shard_map/ppermute | solution.py:23
  126.1 1.4 slice_add_fusion
  127.5 0.3 broadcast_select_fusion
  127.8 0.4 select_reduce_fusion.1
  128.2 1.3 collective-permute-start.25
  129.5 1.3 collective-permute-start.26
  130.8 6.4 %all-to-all-done.terms = bf16[16,96,256]{2,1,0:T(8,128)(2,1)S(1)} async-done(((bf16[16,96,256]{2,1,0:T(8,128)(2,1)}), bf16[16,96,256]{2,1,0:T(8,128)(2,1)S(1)}, u32[]{:S(2)}, u32[]{:S(2)}) %all-to-all-start) | async-done | bytes 786464 | tf_op jit(solution)/shard_map/all_to_all | solution.py:463
  137.2 1.4 sum_terms.1
  138.6 1.1 pad_maximum_fusion
  (64 shorter events, 0.2 us)
Async XLA Ops:
  0.6 2.2 %copy-start.2 = (bf16[256,8192]{1,0:T(8,128)(2,1)S(1)}, bf16[256,8192]{1,0:T(8,128)(2,1)}, u32[]{:S(2)}) copy-start(bf16[256,8192]{1,0:T(8,128)(2,1)} %tok.1) | copy-start | bytes 12582916
  2.8 5.0 %copy-start.21 = (s32[2]{0:T(128)S(1)}, s32[2]{0:T(128)}, u32[]{:S(2)}) copy-start(s32[2]{0:T(128)} %param.12) | copy-start | bytes 28
  2.8 5.0 %copy-start.18 = (bf16[256,256]{1,0:T(8,128)(2,1)S(1)}, bf16[256,256]{1,0:T(8,128)(2,1)}, u32[]{:S(2)}) copy-start(bf16[256,256]{1,0:T(8,128)(2,1)} %param.10) | copy-start | bytes 393220
  2.8 5.1 %copy-start.19 = (bf16[16,512]{1,0:T(8,128)(2,1)S(1)}, bf16[16,512]{1,0:T(8,128)(2,1)}, u32[]{:S(2)}) copy-start(bf16[16,512]{1,0:T(8,128)(2,1)} %param.11) | copy-start | bytes 49156
  2.8 16.8 %copy-start.20 = (s32[2]{0:T(128)S(1)}, s32[2]{0:T(128)}, u32[]{:S(2)}) copy-start(s32[2]{0:T(128)} %param.14) | copy-start | bytes 28
  5.0 1.4 copy-start
  6.3 1.0 copy-start.14
  7.3 26.3 %copy-start.22 = (s32[2]{0:T(128)S(1)}, s32[2]{0:T(128)}, u32[]{:S(2)}) copy-start(s32[2]{0:T(128)} %param.13) | copy-start | bytes 28
  7.3 41.3 %collective-permute-start = (bf16[256,4096]{1,0:T(8,128)(2,1)}, bf16[256,4096]{1,0:T(8,128)(2,1)S(1)}, u32[]{:S(2)}, u32[]{:S(2)}) collective-permute-start(bf16[256,4096]{1,0:T(8,128)(2,1)} %get-tuple-element.26), channel_id=1, source_target_pairs={{0,1},{1,0},{2,3},{3,2},{4,5},{5,4},{6,7},{7,6},{8,9},{9,8},{10,11... | collective-permute-start | bytes 6291464 | tf_op jit(solution)/shard_map/ppermute | solution.py:23
  7.9 9.4 %collective-permute-start.6 = (bf16[80,1024]{1,0:T(8,128)(2,1)S(1)}, bf16[80,1024]{1,0:T(8,128)(2,1)S(1)}, u32[]{:S(2)}, u32[]{:S(2)}) collective-permute-start(bf16[80,1024]{1,0:T(8,128)(2,1)S(1)} %fusion.8.refs_0_), channel_id=1, source_target_pairs={{0,2},{1,3},{2,0},{3,1},{4,6},{5,7},{6,4},{7,5},{8,10},{9,11},{10,... | collective-permute-start | bytes 491528 | tf_op jit(solution)/shard_map/ppermute | solution.py:23
  10.5 7.9 %collective-permute-start.5 = (bf16[80,1024]{1,0:T(8,128)(2,1)S(1)}, bf16[80,1024]{1,0:T(8,128)(2,1)S(1)}, u32[]{:S(2)}, u32[]{:S(2)}) collective-permute-start(bf16[80,1024]{1,0:T(8,128)(2,1)S(1)} %fusion.8.refs_0_), channel_id=1, source_target_pairs={{0,4},{1,5},{2,6},{3,7},{4,0},{5,1},{6,2},{7,3},{8,12},{9,13},{10,... | collective-permute-start | bytes 491528 | tf_op jit(solution)/shard_map/ppermute | solution.py:23
  11.9 8.2 %collective-permute-start.4 = (bf16[80,1024]{1,0:T(8,128)(2,1)S(1)}, bf16[80,1024]{1,0:T(8,128)(2,1)S(1)}, u32[]{:S(2)}, u32[]{:S(2)}) collective-permute-start(bf16[80,1024]{1,0:T(8,128)(2,1)S(1)} %fusion.8.refs_0_), channel_id=1, source_target_pairs={{0,24},{1,25},{2,26},{3,27},{4,28},{5,29},{6,30},{7,31},{8,0},{9,1... | collective-permute-start | bytes 491528 | tf_op jit(solution)/shard_map/ppermute | solution.py:23
  15.5 14.1 %collective-permute-start.3 = (bf16[80,1024]{1,0:T(8,128)(2,1)S(1)}, bf16[80,1024]{1,0:T(8,128)(2,1)S(1)}, u32[]{:S(2)}, u32[]{:S(2)}) collective-permute-start(bf16[80,1024]{1,0:T(8,128)(2,1)S(1)} %fusion.8.refs_0_), channel_id=1, source_target_pairs={{0,16},{1,17},{2,18},{3,19},{4,20},{5,21},{6,22},{7,23},{8,24},{9,... | collective-permute-start | bytes 491528 | tf_op jit(solution)/shard_map/ppermute | solution.py:23
  17.4 13.8 %copy-start.4 = (bf16[80,1024]{1,0:T(8,128)(2,1)}, bf16[80,1024]{1,0:T(8,128)(2,1)S(1)}, u32[]{:S(2)}) copy-start(bf16[80,1024]{1,0:T(8,128)(2,1)S(1)} %collective-permute-done.6.refs_4_.refs_5_) | copy-start | bytes 491524
  17.4 12.2 %collective-permute-start.2 = (bf16[80,1024]{1,0:T(8,128)(2,1)S(1)}, bf16[80,1024]{1,0:T(8,128)(2,1)S(1)}, u32[]{:S(2)}, u32[]{:S(2)}) collective-permute-start(bf16[80,1024]{1,0:T(8,128)(2,1)S(1)} %fusion.8.refs_0_), channel_id=1, source_target_pairs={{0,8},{1,9},{2,10},{3,11},{4,12},{5,13},{6,14},{7,15},{8,16},{9,17... | collective-permute-start | bytes 491528 | tf_op jit(solution)/shard_map/ppermute | solution.py:23
  18.4 12.8 %copy-start.6 = (bf16[80,1024]{1,0:T(8,128)(2,1)}, bf16[80,1024]{1,0:T(8,128)(2,1)S(1)}, u32[]{:S(2)}) copy-start(bf16[80,1024]{1,0:T(8,128)(2,1)S(1)} %collective-permute-done.5.refs_3_.refs_4_) | copy-start | bytes 491524
  18.4 13.5 %collective-permute-start.19 = (bf16[128,1024]{1,0:T(8,128)(2,1)}, bf16[128,1024]{1,0:T(8,128)(2,1)}, u32[]{:S(2)}, u32[]{:S(2)}) collective-permute-start(bf16[128,1024]{1,0:T(8,128)(2,1)} %get-tuple-element.51), channel_id=1, source_target_pairs={{1,0},{2,1},{3,2},{4,3},{5,4},{6,5},{7,6},{8,7},{9,8},{10,9},{11,1... | collective-permute-start | bytes 786440 | tf_op jit(solution)/shard_map/ppermute | solution.py:36
  20.1 11.1 %copy-start.8 = (bf16[80,1024]{1,0:T(8,128)(2,1)}, bf16[80,1024]{1,0:T(8,128)(2,1)S(1)}, u32[]{:S(2)}) copy-start(bf16[80,1024]{1,0:T(8,128)(2,1)S(1)} %collective-permute-done.4.refs_2_.refs_3_) | copy-start | bytes 491524
  20.1 13.6 %collective-permute-start.20 = (bf16[128,1024]{1,0:T(8,128)(2,1)}, bf16[128,1024]{1,0:T(8,128)(2,1)}, u32[]{:S(2)}, u32[]{:S(2)}) collective-permute-start(bf16[128,1024]{1,0:T(8,128)(2,1)} %get-tuple-element.52), channel_id=1, source_target_pairs={{0,1},{1,2},{2,3},{3,4},{4,5},{5,6},{6,7},{7,8},{8,9},{9,10},{10,1... | collective-permute-start | bytes 786440 | tf_op jit(solution)/shard_map/ppermute | solution.py:36
  29.6 1.1 copy-start.10
  29.6 1.1 copy-start.12
  30.7 14.3 %collective-permute-start.8 = (bf16[272,1024]{1,0:T(8,128)(2,1)}, bf16[272,1024]{1,0:T(8,128)(2,1)S(1)}, u32[]{:S(2)}, u32[]{:S(2)}) collective-permute-start(bf16[272,1024]{1,0:T(8,128)(2,1)} %get-tuple-element.29), channel_id=1, source_target_pairs={{0,2},{1,3},{2,0},{3,1},{4,6},{5,7},{6,4},{7,5},{8,10},{9,11},{10,... | collective-permute-start | bytes 1671176 | tf_op jit(solution)/shard_map/ppermute | solution.py:23
  31.2 14.8 %collective-permute-start.7 = (bf16[288,1024]{1,0:T(8,128)(2,1)}, bf16[288,1024]{1,0:T(8,128)(2,1)S(1)}, u32[]{:S(2)}, u32[]{:S(2)}) collective-permute-start(bf16[288,1024]{1,0:T(8,128)(2,1)} %get-tuple-element.28), channel_id=1, source_target_pairs={{0,4},{1,5},{2,6},{3,7},{4,0},{5,1},{6,2},{7,3},{8,12},{9,13},{10,... | collective-permute-start | bytes 1769480 | tf_op jit(solution)/shard_map/ppermute | solution.py:23
  31.9 15.7 %copy-start.15 = (bf16[256,2048]{1,0:T(8,128)(2,1)S(1)}, bf16[256,2048]{1,0:T(8,128)(2,1)}, u32[]{:S(2)}) copy-start(bf16[256,2048]{1,0:T(8,128)(2,1)} %copy-done.14) | copy-start | bytes 3145732
  31.9 16.2 %collective-permute-start.10 = (bf16[256,1024]{1,0:T(8,128)(2,1)}, bf16[256,1024]{1,0:T(8,128)(2,1)S(1)}, u32[]{:S(2)}, u32[]{:S(2)}) collective-permute-start(bf16[256,1024]{1,0:T(8,128)(2,1)} %refs_0_.1), channel_id=1, source_target_pairs={{0,8},{1,9},{2,10},{3,11},{4,12},{5,13},{6,14},{7,15},{8,16},{9,17... | collective-permute-start | bytes 1572872 | tf_op jit(solution)/shard_map/ppermute | solution.py:23
  35.1 14.2 %copy-start.16 = (bf16[256,1024]{1,0:T(8,128)(2,1)S(1)}, bf16[256,1024]{1,0:T(8,128)(2,1)}, u32[]{:S(2)}) copy-start(bf16[256,1024]{1,0:T(8,128)(2,1)} %refs_0_.1) | copy-start | bytes 1572868
  35.1 22.7 %copy-start.1 = (bf16[256,4096]{1,0:T(8,128)(2,1)S(1)}, bf16[256,4096]{1,0:T(8,128)(2,1)}, u32[]{:S(2)}) copy-start(bf16[256,4096]{1,0:T(8,128)(2,1)} %copy-done) | copy-start | bytes 6291460
  35.1 22.7 %copy-start.5 = (bf16[80,1024]{1,0:T(8,128)(2,1)S(1)}, bf16[80,1024]{1,0:T(8,128)(2,1)}, u32[]{:S(2)}) copy-start(bf16[80,1024]{1,0:T(8,128)(2,1)} %copy-done.4) | copy-start | bytes 491524
  35.1 22.7 %copy-start.7 = (bf16[80,1024]{1,0:T(8,128)(2,1)S(1)}, bf16[80,1024]{1,0:T(8,128)(2,1)}, u32[]{:S(2)}) copy-start(bf16[80,1024]{1,0:T(8,128)(2,1)} %copy-done.6) | copy-start | bytes 491524
  35.1 22.7 %copy-start.9 = (bf16[80,1024]{1,0:T(8,128)(2,1)S(1)}, bf16[80,1024]{1,0:T(8,128)(2,1)}, u32[]{:S(2)}) copy-start(bf16[80,1024]{1,0:T(8,128)(2,1)} %copy-done.8) | copy-start | bytes 491524
  35.1 22.7 %copy-start.11 = (bf16[80,1024]{1,0:T(8,128)(2,1)S(1)}, bf16[80,1024]{1,0:T(8,128)(2,1)}, u32[]{:S(2)}) copy-start(bf16[80,1024]{1,0:T(8,128)(2,1)} %copy-done.10) | copy-start | bytes 491524
  35.1 22.7 %copy-start.13 = (bf16[80,1024]{1,0:T(8,128)(2,1)S(1)}, bf16[80,1024]{1,0:T(8,128)(2,1)}, u32[]{:S(2)}) copy-start(bf16[80,1024]{1,0:T(8,128)(2,1)} %copy-done.12) | copy-start | bytes 491524
  35.2 14.1 %collective-permute-start.21 = (bf16[256,512]{1,0:T(8,128)(2,1)S(1)}, bf16[256,512]{1,0:T(8,128)(2,1)S(1)}, u32[]{:S(2)}, u32[]{:S(2)}) collective-permute-start(bf16[256,512]{1,0:T(8,128)(2,1)S(1)} %get-tuple-element.53), channel_id=1, source_target_pairs={{0,1},{1,0},{2,3},{3,2},{4,5},{5,4},{6,7},{7,6},{8,9},{9,8},{10,11... | collective-permute-start | bytes 786440 | tf_op jit(solution)/shard_map/ppermute | solution.py:23
  46.0 8.6 %collective-permute-start.18 = (bf16[112,1024]{1,0:T(8,128)(2,1)S(1)}, bf16[112,1024]{1,0:T(8,128)(2,1)S(1)}, u32[]{:S(2)}, u32[]{:S(2)}) collective-permute-start(bf16[112,1024]{1,0:T(8,128)(2,1)S(1)} %get-tuple-element.36), channel_id=1, source_target_pairs={{0,2},{1,3},{2,0},{3,1},{4,6},{5,7},{6,4},{7,5},{8,10},{9,11},{10,... | collective-permute-start | bytes 688136 | tf_op jit(solution)/shard_map/ppermute | solution.py:23
  47.6 29.5 %collective-permute-start.1 = (bf16[256,2048]{1,0:T(8,128)(2,1)S(1)}, bf16[256,2048]{1,0:T(8,128)(2,1)S(1)}, u32[]{:S(2)}, u32[]{:S(2)}) collective-permute-start(bf16[256,2048]{1,0:T(8,128)(2,1)S(1)} %copy-done.15), channel_id=1, source_target_pairs={{0,2},{1,3},{2,0},{3,1},{4,6},{5,7},{6,4},{7,5},{8,10},{9,11},{10,... | collective-permute-start | bytes 3145736 | tf_op jit(solution)/shard_map/ppermute | solution.py:23
  48.1 13.4 %collective-permute-start.11 = (bf16[256,1024]{1,0:T(8,128)(2,1)S(1)}, bf16[256,1024]{1,0:T(8,128)(2,1)S(1)}, u32[]{:S(2)}, u32[]{:S(2)}) collective-permute-start(bf16[256,1024]{1,0:T(8,128)(2,1)S(1)} %collective-permute-done.10.refs_1_.refs_12_), channel_id=1, source_target_pairs={{0,8},{1,9},{2,10},{3,11},{4,12},{5,13},{6,14},{7,15},{8,16},{9,17... | collective-permute-start | bytes 1572872 | tf_op jit(solution)/shard_map/ppermute | solution.py:23
  48.6 9.2 %collective-permute-start.17 = (bf16[128,1024]{1,0:T(8,128)(2,1)S(1)}, bf16[128,1024]{1,0:T(8,128)(2,1)S(1)}, u32[]{:S(2)}, u32[]{:S(2)}) collective-permute-start(bf16[128,1024]{1,0:T(8,128)(2,1)S(1)} %get-tuple-element.35), channel_id=1, source_target_pairs={{0,4},{1,5},{2,6},{3,7},{4,0},{5,1},{6,2},{7,3},{8,12},{9,13},{10,... | collective-permute-start | bytes 786440 | tf_op jit(solution)/shard_map/ppermute | solution.py:23
  49.3 16.6 %collective-permute-start.15 = (bf16[256,1024]{1,0:T(8,128)(2,1)S(1)}, bf16[256,1024]{1,0:T(8,128)(2,1)S(1)}, u32[]{:S(2)}, u32[]{:S(2)}) collective-permute-start(bf16[256,1024]{1,0:T(8,128)(2,1)S(1)} %copy-done.16), channel_id=1, source_target_pairs={{0,4},{1,5},{2,6},{3,7},{4,0},{5,1},{6,2},{7,3},{8,12},{9,13},{10,... | collective-permute-start | bytes 1572872 | tf_op jit(solution)/shard_map/ppermute | solution.py:23
  54.6 42.3 %collective-permute-start.9 = (bf16[256,2048]{1,0:T(8,128)(2,1)S(1)}, bf16[256,2048]{1,0:T(8,128)(2,1)S(1)}, u32[]{:S(2)}, u32[]{:S(2)}) collective-permute-start(bf16[256,2048]{1,0:T(8,128)(2,1)S(1)} %slice.52.refs_13_), channel_id=1, source_target_pairs={{0,2},{1,3},{2,0},{3,1},{4,6},{5,7},{6,4},{7,5},{8,10},{9,11},{10,... | collective-permute-start | bytes 3145736 | tf_op jit(solution)/shard_map/ppermute | solution.py:23
  59.4 40.9 %collective-permute-start.22 = (f32[1040,256]{1,0:T(8,128)S(1)}, f32[1040,256]{1,0:T(8,128)S(1)}, u32[]{:S(2)}, u32[]{:S(2)}) collective-permute-start(f32[1040,256]{1,0:T(8,128)S(1)} %get-tuple-element.37.own), channel_id=1, source_target_pairs={{0,1},{1,0},{2,3},{3,2},{4,5},{5,4},{6,7},{7,6},{8,9},{9,8},{10,11... | collective-permute-start | bytes 3194888 | tf_op jit(solution)/shard_map/ppermute | solution.py:23
  61.5 16.1 %collective-permute-start.13 = (bf16[256,1024]{1,0:T(8,128)(2,1)S(1)}, bf16[256,1024]{1,0:T(8,128)(2,1)S(1)}, u32[]{:S(2)}, u32[]{:S(2)}) collective-permute-start(bf16[256,1024]{1,0:T(8,128)(2,1)S(1)} %collective-permute-done.11.refs_2_), channel_id=1, source_target_pairs={{0,8},{1,9},{2,10},{3,11},{4,12},{5,13},{6,14},{7,15},{8,16},{9,17... | collective-permute-start | bytes 1572872 | tf_op jit(solution)/shard_map/ppermute | solution.py:23
  65.9 13.2 %collective-permute-start.16 = (bf16[256,1024]{1,0:T(8,128)(2,1)S(1)}, bf16[256,1024]{1,0:T(8,128)(2,1)S(1)}, u32[]{:S(2)}, u32[]{:S(2)}) collective-permute-start(bf16[256,1024]{1,0:T(8,128)(2,1)S(1)} %collective-permute-done.10.refs_1_.refs_12_), channel_id=1, source_target_pairs={{0,4},{1,5},{2,6},{3,7},{4,0},{5,1},{6,2},{7,3},{8,12},{9,13},{10,... | collective-permute-start | bytes 1572872 | tf_op jit(solution)/shard_map/ppermute | solution.py:23
  77.1 25.6 %collective-permute-start.12 = (bf16[256,1024]{1,0:T(8,128)(2,1)S(1)}, bf16[256,1024]{1,0:T(8,128)(2,1)S(1)}, u32[]{:S(2)}, u32[]{:S(2)}) collective-permute-start(bf16[256,1024]{1,0:T(8,128)(2,1)S(1)} %collective-permute-done.11.refs_2_), channel_id=1, source_target_pairs={{0,4},{1,5},{2,6},{3,7},{4,0},{5,1},{6,2},{7,3},{8,12},{9,13},{10,... | collective-permute-start | bytes 1572872 | tf_op jit(solution)/shard_map/ppermute | solution.py:23
  77.7 25.0 %collective-permute-start.14 = (bf16[256,1024]{1,0:T(8,128)(2,1)S(1)}, bf16[256,1024]{1,0:T(8,128)(2,1)S(1)}, u32[]{:S(2)}, u32[]{:S(2)}) collective-permute-start(bf16[256,1024]{1,0:T(8,128)(2,1)S(1)} %collective-permute-done.13.refs_3_), channel_id=1, source_target_pairs={{0,4},{1,5},{2,6},{3,7},{4,0},{5,1},{6,2},{7,3},{8,12},{9,13},{10,... | collective-permute-start | bytes 1572872 | tf_op jit(solution)/shard_map/ppermute | solution.py:23
  100.3 2.4 %copy-start.3 = (f32[512,1024]{1,0:T(8,128)}, f32[512,1024]{1,0:T(8,128)S(1)}, u32[]{:S(2)}) copy-start(f32[512,1024]{1,0:T(8,128)S(1)} %get-tuple-element.34.refs_3_) | copy-start | bytes 6291460
  105.8 4.2 %collective-permute-start.23 = (f32[512,1024]{1,0:T(8,128)S(1)}, f32[512,1024]{1,0:T(8,128)S(1)}, u32[]{:S(2)}, u32[]{:S(2)}) collective-permute-start(f32[512,1024]{1,0:T(8,128)S(1)} %get-tuple-element.41), channel_id=1, source_target_pairs={{0,1},{1,0},{2,3},{3,2},{4,5},{5,4},{6,7},{7,6},{8,9},{9,8},{10,11... | collective-permute-start | bytes 6291464 | tf_op jit(solution)/shard_map/ppermute | solution.py:23
  110.6 1.6 %copy-start.17 = (f32[512,1024]{1,0:T(8,128)}, f32[512,1024]{1,0:T(8,128)S(1)}, u32[]{:S(2)}) copy-start(f32[512,1024]{1,0:T(8,128)S(1)} %add.18) | copy-start | bytes 6291460
  110.7 15.4 %collective-permute-start.24 = (bf16[256,1024]{1,0:T(8,128)(2,1)S(1)}, bf16[256,1024]{1,0:T(8,128)(2,1)S(1)}, u32[]{:S(2)}, u32[]{:S(2)}) collective-permute-start(bf16[256,1024]{1,0:T(8,128)(2,1)S(1)} %slice.64), channel_id=1, source_target_pairs={{0,2},{1,3},{2,0},{3,1},{4,6},{5,7},{6,4},{7,5},{8,10},{9,11},{10,... | collective-permute-start | bytes 1572872 | tf_op jit(solution)/shard_map/ppermute | solution.py:23
  112.3 24.9 %all-to-all-start = ((bf16[16,96,256]{2,1,0:T(8,128)(2,1)}), bf16[16,96,256]{2,1,0:T(8,128)(2,1)S(1)}, u32[]{:S(2)}, u32[]{:S(2)}) async-start(bf16[16,96,256]{2,1,0:T(8,128)(2,1)} %get-tuple-element.42), calls=%async_computation | async-start | bytes 1572864 | tf_op jit(solution)/shard_map/all_to_all | solution.py:463
  128.2 10.4 %collective-permute-start.25 = (bf16[128,1024]{1,0:T(8,128)(2,1)S(1)}, bf16[128,1024]{1,0:T(8,128)(2,1)S(1)}, u32[]{:S(2)}, u32[]{:S(2)}) collective-permute-start(bf16[128,1024]{1,0:T(8,128)(2,1)S(1)} %get-tuple-element.47), channel_id=1, source_target_pairs={{0,1},{1,2},{2,3},{3,4},{4,5},{5,6},{6,7},{7,8},{8,9},{9,10},{10,1... | collective-permute-start | bytes 786440 | tf_op jit(solution)/shard_map/ppermute | solution.py:36
  129.5 9.1 %collective-permute-start.26 = (bf16[128,1024]{1,0:T(8,128)(2,1)S(1)}, bf16[128,1024]{1,0:T(8,128)(2,1)S(1)}, u32[]{:S(2)}, u32[]{:S(2)}) collective-permute-start(bf16[128,1024]{1,0:T(8,128)(2,1)S(1)} %get-tuple-element.48), channel_id=1, source_target_pairs={{1,0},{2,1},{3,2},{4,3},{5,4},{6,5},{7,6},{8,7},{9,8},{10,9},{11,1... | collective-permute-start | bytes 786440 | tf_op jit(solution)/shard_map/ppermute | solution.py:36

commit v4 on v3

--- a/solution.py
+++ b/solution.py
@@ -370,12 +370,12 @@
                         else:
                             left_side = (tok, tok_in)[half][:, columns]
                         total += dot(left_side, refs[n][row : row + height, here])
-                    out[to, here] = total
+                    out[to, here] = total.astype(out.dtype)
 
     share = jax.ShapeDtypeStruct((2 * rows, width), F32)
     return pl.pallas_call(
         kernel,
-        out_shape=(share, share),
+        out_shape=(share, jax.ShapeDtypeStruct(share.shape, BF16) if adapters else share),
         in_specs=[VMEM] * (4 + count + n_joint) + [ANY] * len(after),
         out_specs=(VMEM, VMEM),
         compiler_params=pltpu.CompilerParams(vmem_limit_bytes=40 * MIB),
@@ -453,10 +453,10 @@
     tok_far = (far_own, swap(far_columns, size, 2))
     share, table = low_rank_products(
         tok, tok_in, [*low, *stage0, *stage1, *stage2], grad_mine, grad_in, size,
-        (wide[1].array, far_columns, ),
+        (far_columns, ),
     )
     hidden, names, terms = adapter_terms(
-        share, swap(share, size, 1), tok, tok_in, grad_mine, grad_in, size, BF16, ()
+        share, swap(share, size, 1), tok, tok_in, grad_mine, grad_in, size, BF16, (wide[2].array, )
     )
     terms_sent = terms
     groups = [list(range(core, size, 2)) for core in range(2)]
@@ -469,7 +469,7 @@
     keep, give = value_products(
         tok, tok_in, tok_far, late, shares, (hidden, table), size, ()
     )
-    both = keep + swap(give, size, 1)
+    both = keep + swap(give, size, 1).astype(F32)
     rows = both.shape[0] // 2
     far = swap(both[rows:].astype(BF16), size, 2)
     total = (both[:rows] + far.astype(F32)).reshape(-1, BLOCK, width)

time: 142 us -> 141 us (level)
  waiting for transfers between devices: 76.3 us -> 74.8 us
    ppermute x23, waiting for transfers between devices: 69.9 us -> 68.4 us  [send_to(): return lax.ppermute(x, 'fsdp', [(i, target(i)) for i in range(size)])]
where the time goes in v4:
time: 141 us; the launch traced here: 138 us
  waiting for transfers between devices  74.8 us (53%)
  starting transfers between devices  35.3 us (25%)
  Pallas kernels  15.1 us (11%)
  local copies, waits for them, and re-layouts  6.71 us (5%)
  other arithmetic  5.18 us (4%)
    ppermute x23, waiting for transfers between devices, send_to(): return lax.ppermute(x, 'fsdp', [(i, target(i)) for i in range(size)])  68.4 us
    ppermute x23, starting transfers between devices, send_to(): return lax.ppermute(x, 'fsdp', [(i, target(i)) for i in range(size)])  23.1 us
    ppermute x4, starting transfers between devices, shift(): return lax.ppermute(x, 'fsdp', pairs)  7.25 us
    pallas_call x2, Pallas kernels, value_products(): pl.pallas_call(kernel, out_shape=(share, jax.ShapeDtypeStruct(share.shape...  6.55 us
    all_to_all x1, waiting for transfers between devices, body(): lax.all_to_all(terms, 'fsdp', 0, 0, axis_index_groups=groups, tiled=True)  6.38 us
    all_to_all x1, starting transfers between devices, body(): lax.all_to_all(terms, 'fsdp', 0, 0, axis_index_groups=groups, tiled=True)  4.92 us
    unnamed x46, local copies, waits for them, and re-layouts  4.6 us
  transfers between devices with their start and end apart: 28, of which 13 were waited for; matrix products, arithmetic and copies ran while one was open for 4% of the time, Pallas kernels for 7%

profile of v4, /device:TPU:0, one launch (start us, length us, event | category | flops | bytes accessed | tf_op | source)
XLA Modules:
  0.0 138.1 jit_solution(17827790124333583787)
XLA Ops:
  0.6 2.2 %copy-done.2 = bf16[256,8192]{1,0:T(8,128)(2,1)S(1)} copy-done((bf16[256,8192]{1,0:T(8,128)(2,1)S(1)}, bf16[256,8192]{1,0:T(8,128)(2,1)}, u32[]{:S(2)}) %copy-start.2) | copy-done | bytes 4194328
  2.8 2.1 %split_tokens.1 = (bf16[256,4096]{1,0:T(8,128)(2,1)S(1)}, bf16[256,4096]{1,0:T(8,128)(2,1)}, bf16[256,2048]{1,0:T(8,128)(2,1)S(1)}) custom-call(bf16[256,8192]{1,0:T(8,128)(2,1)S(1)} %copy-done.2), custom_call_target="tpu_custom_call" | custom-call | bytes 8388608 | tf_op jit(solution)/shard_map/split_tokens/pallas_call | solution.py:148
  5.0 1.4 copy-done
  6.3 1.0 copy-done.14
  7.3 0.5 collective-permute-start
  7.8 0.1 select_convert_fusion.1
  7.9 2.6 %collective-permute-start.6 = (bf16[80,1024]{1,0:T(8,128)(2,1)S(1)}, bf16[80,1024]{1,0:T(8,128)(2,1)S(1)}, u32[]{:S(2)}, u32[]{:S(2)}) collective-permute-start(bf16[80,1024]{1,0:T(8,128)(2,1)S(1)} %fusion.8.refs_0_), channel_id=1, source_target_pairs={{0,2},{1,3},{2,0},{3,1},{4,6},{5,7},{6,4},{7,5},{8,10},{9,11},{10,... | collective-permute-start | bytes 491528 | tf_op jit(solution)/shard_map/ppermute | solution.py:23
  10.5 1.4 %collective-permute-start.5 = (bf16[80,1024]{1,0:T(8,128)(2,1)S(1)}, bf16[80,1024]{1,0:T(8,128)(2,1)S(1)}, u32[]{:S(2)}, u32[]{:S(2)}) collective-permute-start(bf16[80,1024]{1,0:T(8,128)(2,1)S(1)} %fusion.8.refs_0_), channel_id=1, source_target_pairs={{0,4},{1,5},{2,6},{3,7},{4,0},{5,1},{6,2},{7,3},{8,12},{9,13},{10,... | collective-permute-start | bytes 491528 | tf_op jit(solution)/shard_map/ppermute | solution.py:23
  11.9 3.6 %collective-permute-start.4 = (bf16[80,1024]{1,0:T(8,128)(2,1)S(1)}, bf16[80,1024]{1,0:T(8,128)(2,1)S(1)}, u32[]{:S(2)}, u32[]{:S(2)}) collective-permute-start(bf16[80,1024]{1,0:T(8,128)(2,1)S(1)} %fusion.8.refs_0_), channel_id=1, source_target_pairs={{0,24},{1,25},{2,26},{3,27},{4,28},{5,29},{6,30},{7,31},{8,0},{9,1... | collective-permute-start | bytes 491528 | tf_op jit(solution)/shard_map/ppermute | solution.py:23
  15.5 0.0 collective-permute-start.3
  15.5 1.9 %fusion.10 = (bf16[128,1024]{1,0:T(8,128)(2,1)}, bf16[128,1024]{1,0:T(8,128)(2,1)}) fusion(bf16[512,1024]{1,0:T(8,128)(2,1)} %param.15), kind=kLoop, calls=%fused_computation.32 | loop fusion | bytes 1048576 | tf_op jit(solution)/shard_map/slice | solution.py:441
  17.4 1.0 collective-permute-start.2
  18.4 1.3 collective-permute-start.19
  19.7 0.4 collective-permute-done.4.refs_2_.refs_3_
  20.1 3.4 %collective-permute-start.20 = (bf16[128,1024]{1,0:T(8,128)(2,1)}, bf16[128,1024]{1,0:T(8,128)(2,1)}, u32[]{:S(2)}, u32[]{:S(2)}) collective-permute-start(bf16[128,1024]{1,0:T(8,128)(2,1)} %get-tuple-element.52), channel_id=1, source_target_pairs={{0,1},{1,2},{2,3},{3,4},{4,5},{5,6},{6,7},{7,8},{8,9},{9,10},{10,1... | collective-permute-start | bytes 786440 | tf_op jit(solution)/shard_map/ppermute | solution.py:36
  23.5 6.1 %collective-permute-done.3.refs_1_.refs_2_ = bf16[80,1024]{1,0:T(8,128)(2,1)S(1)} collective-permute-done((bf16[80,1024]{1,0:T(8,128)(2,1)S(1)}, bf16[80,1024]{1,0:T(8,128)(2,1)S(1)}, u32[]{:S(2)}, u32[]{:S(2)}) %collective-permute-start.3) | collective-permute-done | bytes 163872 | tf_op jit(solution)/shard_map/ppermute | solution.py:23
  29.6 1.1 packed.2
  30.7 0.4 collective-permute-start.8
  31.2 0.7 collective-permute-start.7
  31.8 0.1 broadcast_bitcast_fusion
  31.9 1.7 %collective-permute-start.10 = (bf16[256,1024]{1,0:T(8,128)(2,1)}, bf16[256,1024]{1,0:T(8,128)(2,1)S(1)}, u32[]{:S(2)}, u32[]{:S(2)}) collective-permute-start(bf16[256,1024]{1,0:T(8,128)(2,1)} %refs_0_.1), channel_id=1, source_target_pairs={{0,8},{1,9},{2,10},{3,11},{4,12},{5,13},{6,14},{7,15},{8,16},{9,17... | collective-permute-start | bytes 1572872 | tf_op jit(solution)/shard_map/ppermute | solution.py:23
  33.6 0.1 iota_compare_fusion.4
  33.7 1.4 fusion.1
  35.1 0.0 copy-start.16
  35.2 0.1 collective-permute-start.21
  35.3 9.7 %collective-permute-done.8.refs_1_.refs_7_ = bf16[272,1024]{1,0:T(8,128)(2,1)S(1)} collective-permute-done((bf16[272,1024]{1,0:T(8,128)(2,1)}, bf16[272,1024]{1,0:T(8,128)(2,1)S(1)}, u32[]{:S(2)}, u32[]{:S(2)}) %collective-permute-start.8) | collective-permute-done | bytes 557088 | tf_op jit(solution)/shard_map/ppermute | solution.py:23
  45.0 1.0 collective-permute-done.7.refs_0_.refs_6_
  46.0 1.6 %collective-permute-start.18 = (bf16[112,1024]{1,0:T(8,128)(2,1)S(1)}, bf16[112,1024]{1,0:T(8,128)(2,1)S(1)}, u32[]{:S(2)}, u32[]{:S(2)}) collective-permute-start(bf16[112,1024]{1,0:T(8,128)(2,1)S(1)} %get-tuple-element.36), channel_id=1, source_target_pairs={{0,2},{1,3},{2,0},{3,1},{4,6},{5,7},{6,4},{7,5},{8,10},{9,11},{10,... | collective-permute-start | bytes 688136 | tf_op jit(solution)/shard_map/ppermute | solution.py:23
  47.6 0.5 collective-permute-start.1
  48.1 0.5 collective-permute-start.11
  48.6 0.6 collective-permute-start.17
  49.2 0.1 slice.52.refs_12_
  49.3 1.5 %collective-permute-start.15 = (bf16[256,1024]{1,0:T(8,128)(2,1)S(1)}, bf16[256,1024]{1,0:T(8,128)(2,1)S(1)}, u32[]{:S(2)}, u32[]{:S(2)}) collective-permute-start(bf16[256,1024]{1,0:T(8,128)(2,1)S(1)} %copy-done.16), channel_id=1, source_target_pairs={{0,4},{1,5},{2,6},{3,7},{4,0},{5,1},{6,2},{7,3},{8,12},{9,13},{10,... | collective-permute-start | bytes 1572872 | tf_op jit(solution)/shard_map/ppermute | solution.py:23
  50.8 3.8 %collective-permute-done.18.refs_9_ = bf16[112,1024]{1,0:T(8,128)(2,1)S(1)} collective-permute-done((bf16[112,1024]{1,0:T(8,128)(2,1)S(1)}, bf16[112,1024]{1,0:T(8,128)(2,1)S(1)}, u32[]{:S(2)}, u32[]{:S(2)}) %collective-permute-start.18) | collective-permute-done | bytes 229408 | tf_op jit(solution)/shard_map/ppermute | solution.py:23
  54.6 1.5 %collective-permute-start.9 = (bf16[256,2048]{1,0:T(8,128)(2,1)S(1)}, bf16[256,2048]{1,0:T(8,128)(2,1)S(1)}, u32[]{:S(2)}, u32[]{:S(2)}) collective-permute-start(bf16[256,2048]{1,0:T(8,128)(2,1)S(1)} %slice.52.refs_12_), channel_id=1, source_target_pairs={{0,2},{1,3},{2,0},{3,1},{4,6},{5,7},{6,4},{7,5},{8,10},{9,11},{10,... | collective-permute-start | bytes 3145736 | tf_op jit(solution)/shard_map/ppermute | solution.py:23
  56.1 1.7 %collective-permute-done.17.refs_8_ = bf16[128,1024]{1,0:T(8,128)(2,1)S(1)} collective-permute-done((bf16[128,1024]{1,0:T(8,128)(2,1)S(1)}, bf16[128,1024]{1,0:T(8,128)(2,1)S(1)}, u32[]{:S(2)}, u32[]{:S(2)}) %collective-permute-start.17) | collective-permute-done | bytes 262176 | tf_op jit(solution)/shard_map/ppermute | solution.py:23
  57.9 1.5 %low_rank_products.1 = (f32[1040,256]{1,0:T(8,128)S(1)}, bf16[2,256,256]{2,1,0:T(8,128)(2,1)S(1)}) custom-call(bf16[256,4096]{1,0:T(8,128)(2,1)S(1)} %copy-done.1, bf16[256,4096]{1,0:T(8,128)(2,1)S(1)} %collective-permute-done.tok_in, bf16[80,1024]{1,0:T(8,128)(2,1)S(1)} %fusion.8.refs_0_, bf16[80,1024]{1,0:T(8,128)(2,1)S(1)} %copy-done.13, ...), custom_call_target="tpu_custom_call" | custom-call | flops 1207959552 | bytes 9437184 | tf_op jit(solution)/shard_map/low_rank_products/pallas_call | solution.py:211
  59.4 0.1 collective-permute-start.22
  59.5 2.1 %collective-permute-done.11.refs_2_.refs_0_ = bf16[256,1024]{1,0:T(8,128)(2,1)S(1)} collective-permute-done((bf16[256,1024]{1,0:T(8,128)(2,1)S(1)}, bf16[256,1024]{1,0:T(8,128)(2,1)S(1)}, u32[]{:S(2)}, u32[]{:S(2)}) %collective-permute-start.11) | collective-permute-done | bytes 524320 | tf_op jit(solution)/shard_map/ppermute | solution.py:23
  61.5 0.6 collective-permute-start.13
  62.1 3.8 %collective-permute-done.15.refs_4_ = bf16[256,1024]{1,0:T(8,128)(2,1)S(1)} collective-permute-done((bf16[256,1024]{1,0:T(8,128)(2,1)S(1)}, bf16[256,1024]{1,0:T(8,128)(2,1)S(1)}, u32[]{:S(2)}, u32[]{:S(2)}) %collective-permute-start.15) | collective-permute-done | bytes 524320 | tf_op jit(solution)/shard_map/ppermute | solution.py:23
  65.9 0.7 collective-permute-start.16
  66.6 10.5 %collective-permute-done.1.far = bf16[256,2048]{1,0:T(8,128)(2,1)S(1)} collective-permute-done((bf16[256,2048]{1,0:T(8,128)(2,1)S(1)}, bf16[256,2048]{1,0:T(8,128)(2,1)S(1)}, u32[]{:S(2)}, u32[]{:S(2)}) %collective-permute-start.1) | collective-permute-done | bytes 1048608 | tf_op jit(solution)/shard_map/ppermute | solution.py:23
  77.1 0.6 collective-permute-start.12
  77.7 1.4 %collective-permute-start.14 = (bf16[256,1024]{1,0:T(8,128)(2,1)S(1)}, bf16[256,1024]{1,0:T(8,128)(2,1)S(1)}, u32[]{:S(2)}, u32[]{:S(2)}) collective-permute-start(bf16[256,1024]{1,0:T(8,128)(2,1)S(1)} %collective-permute-done.13.refs_3_), channel_id=1, source_target_pairs={{0,4},{1,5},{2,6},{3,7},{4,0},{5,1},{6,2},{7,3},{8,12},{9,13},{10,... | collective-permute-start | bytes 1572872 | tf_op jit(solution)/shard_map/ppermute | solution.py:23
  79.1 17.8 %collective-permute-done.9.far_in = bf16[256,2048]{1,0:T(8,128)(2,1)S(1)} collective-permute-done((bf16[256,2048]{1,0:T(8,128)(2,1)S(1)}, bf16[256,2048]{1,0:T(8,128)(2,1)S(1)}, u32[]{:S(2)}, u32[]{:S(2)}) %collective-permute-start.9) | collective-permute-done | bytes 1048608 | tf_op jit(solution)/shard_map/ppermute | solution.py:23
  96.9 3.4 %value_products.2 = (f32[512,1024]{1,0:T(8,128)S(1)}, f32[512,1024]{1,0:T(8,128)S(1)}) custom-call(bf16[256,4096]{1,0:T(8,128)(2,1)S(1)} %copy-done.1, bf16[256,4096]{1,0:T(8,128)(2,1)S(1)} %collective-permute-done.tok_in, bf16[256,2048]{1,0:T(8,128)(2,1)S(1)} %collective-permute-done.1.far, bf16[256,2048]{1,0:T(8,128)(2,1)S(1)} %collective-permute-done.9.far_in, ...), custom_call_target="tpu_custom_call" | custom-call | flops 3221225472 | bytes 4194304 | tf_op jit(solution)/shard_map/value_products/pallas_call | solution.py:376
  100.3 2.3 %adapter_terms.1 = (bf16[512,256]{1,0:T(8,128)(2,1)S(1)}, f32[16,256]{1,0:T(8,128)S(1)}, bf16[16,96,256]{2,1,0:T(8,128)(2,1)}) custom-call(f32[1040,256]{1,0:T(8,128)S(1)} %get-tuple-element.37.own, f32[1040,256]{1,0:T(8,128)S(1)} %collective-permute-done.22.other, bf16[256,4096]{1,0:T(8,128)(2,1)S(1)} %copy-done.1, ...), custom_call_target="tpu_custom_call" | custom-call | flops 536870912 | bytes 9437184 | tf_op jit(solution)/shard_map/adapter_terms/pallas_call | solution.py:274
  102.7 3.1 %value_products.3 = (f32[512,1024]{1,0:T(8,128)S(1)}, bf16[512,1024]{1,0:T(8,128)(2,1)S(1)}) custom-call(bf16[256,4096]{1,0:T(8,128)(2,1)S(1)} %copy-done.1, bf16[256,4096]{1,0:T(8,128)(2,1)S(1)} %collective-permute-done.tok_in, bf16[256,2048]{1,0:T(8,128)(2,1)S(1)} %collective-permute-done.1.far, bf16[256,2048]{1,0:T(8,128)(2,1)S(1)} %collective-permute-done.9.far_in, ...), custom_call_target="tpu_custom_call" | custom-call | flops 1073741824 | bytes 4194304 | tf_op jit(solution)/shard_map/value_products/pallas_call | solution.py:376
  105.8 0.1 collective-permute-start.23
  105.9 2.6 %collective-permute-done.23 = bf16[512,1024]{1,0:T(8,128)(2,1)S(1)} collective-permute-done((bf16[512,1024]{1,0:T(8,128)(2,1)S(1)}, bf16[512,1024]{1,0:T(8,128)(2,1)S(1)}, u32[]{:S(2)}, u32[]{:S(2)}) %collective-permute-start.23) | collective-permute-done | bytes 1048608 | tf_op jit(solution)/shard_map/ppermute | solution.py:23
  108.6 0.4 convert_add_fusion
  109.0 0.1 slice.64
  109.1 1.5 %collective-permute-start.24 = (bf16[256,1024]{1,0:T(8,128)(2,1)S(1)}, bf16[256,1024]{1,0:T(8,128)(2,1)S(1)}, u32[]{:S(2)}, u32[]{:S(2)}) collective-permute-start(bf16[256,1024]{1,0:T(8,128)(2,1)S(1)} %slice.64), channel_id=1, source_target_pairs={{0,2},{1,3},{2,0},{3,1},{4,6},{5,7},{6,4},{7,5},{8,10},{9,11},{10,... | collective-permute-start | bytes 1572872 | tf_op jit(solution)/shard_map/ppermute | solution.py:23
  110.6 4.9 %all-to-all-start = ((bf16[16,96,256]{2,1,0:T(8,128)(2,1)}), bf16[16,96,256]{2,1,0:T(8,128)(2,1)S(1)}, u32[]{:S(2)}, u32[]{:S(2)}) async-start(bf16[16,96,256]{2,1,0:T(8,128)(2,1)} %get-tuple-element.42), calls=%async_computation | async-start | bytes 1572864 | tf_op jit(solution)/shard_map/all_to_all | solution.py:463
  115.6 8.9 %collective-permute-done.24 = bf16[256,1024]{1,0:T(8,128)(2,1)S(1)} collective-permute-done((bf16[256,1024]{1,0:T(8,128)(2,1)S(1)}, bf16[256,1024]{1,0:T(8,128)(2,1)S(1)}, u32[]{:S(2)}, u32[]{:S(2)}) %collective-permute-start.24) | collective-permute-done | bytes 524320 | tf_op jit(solution)/shard_map/ppermute | solution.py:23
  124.5 1.4 slice_add_fusion
  125.9 0.3 broadcast_select_fusion
  126.2 0.4 select_reduce_fusion.1
  126.6 1.3 collective-permute-start.25
  127.9 1.3 collective-permute-start.26
  129.2 6.4 %all-to-all-done.terms = bf16[16,96,256]{2,1,0:T(8,128)(2,1)S(1)} async-done(((bf16[16,96,256]{2,1,0:T(8,128)(2,1)}), bf16[16,96,256]{2,1,0:T(8,128)(2,1)S(1)}, u32[]{:S(2)}, u32[]{:S(2)}) %all-to-all-start) | async-done | bytes 786464 | tf_op jit(solution)/shard_map/all_to_all | solution.py:463
  135.6 1.4 %sum_terms.1 = (f32[256,256]{1,0:T(8,128)}, f32[16,512]{1,0:T(8,128)}) custom-call(bf16[16,96,256]{2,1,0:T(8,128)(2,1)S(1)} %all-to-all-done.terms, f32[16,256]{1,0:T(8,128)S(1)} %get-tuple-element.43.names), custom_call_target="tpu_custom_call" | custom-call | flops 134217728 | bytes 2097152 | tf_op jit(solution)/shard_map/sum_terms/pallas_call | solution.py:319
  137.0 1.1 pad_maximum_fusion
  (64 shorter events, 0.2 us)
Async XLA Ops:
  0.6 2.2 %copy-start.2 = (bf16[256,8192]{1,0:T(8,128)(2,1)S(1)}, bf16[256,8192]{1,0:T(8,128)(2,1)}, u32[]{:S(2)}) copy-start(bf16[256,8192]{1,0:T(8,128)(2,1)} %tok.1) | copy-start | bytes 12582916
  2.8 5.0 %copy-start.21 = (s32[2]{0:T(128)S(1)}, s32[2]{0:T(128)}, u32[]{:S(2)}) copy-start(s32[2]{0:T(128)} %param.12) | copy-start | bytes 28
  2.8 5.0 %copy-start.18 = (bf16[256,256]{1,0:T(8,128)(2,1)S(1)}, bf16[256,256]{1,0:T(8,128)(2,1)}, u32[]{:S(2)}) copy-start(bf16[256,256]{1,0:T(8,128)(2,1)} %param.10) | copy-start | bytes 393220
  2.8 5.1 %copy-start.19 = (bf16[16,512]{1,0:T(8,128)(2,1)S(1)}, bf16[16,512]{1,0:T(8,128)(2,1)}, u32[]{:S(2)}) copy-start(bf16[16,512]{1,0:T(8,128)(2,1)} %param.11) | copy-start | bytes 49156
  2.8 16.8 %copy-start.20 = (s32[2]{0:T(128)S(1)}, s32[2]{0:T(128)}, u32[]{:S(2)}) copy-start(s32[2]{0:T(128)} %param.14) | copy-start | bytes 28
  5.0 1.4 copy-start
  6.3 1.0 copy-start.14
  7.3 26.3 %copy-start.22 = (s32[2]{0:T(128)S(1)}, s32[2]{0:T(128)}, u32[]{:S(2)}) copy-start(s32[2]{0:T(128)} %param.13) | copy-start | bytes 28
  7.3 41.3 %collective-permute-start = (bf16[256,4096]{1,0:T(8,128)(2,1)}, bf16[256,4096]{1,0:T(8,128)(2,1)S(1)}, u32[]{:S(2)}, u32[]{:S(2)}) collective-permute-start(bf16[256,4096]{1,0:T(8,128)(2,1)} %get-tuple-element.26), channel_id=1, source_target_pairs={{0,1},{1,0},{2,3},{3,2},{4,5},{5,4},{6,7},{7,6},{8,9},{9,8},{10,11... | collective-permute-start | bytes 6291464 | tf_op jit(solution)/shard_map/ppermute | solution.py:23
  7.9 9.4 %collective-permute-start.6 = (bf16[80,1024]{1,0:T(8,128)(2,1)S(1)}, bf16[80,1024]{1,0:T(8,128)(2,1)S(1)}, u32[]{:S(2)}, u32[]{:S(2)}) collective-permute-start(bf16[80,1024]{1,0:T(8,128)(2,1)S(1)} %fusion.8.refs_0_), channel_id=1, source_target_pairs={{0,2},{1,3},{2,0},{3,1},{4,6},{5,7},{6,4},{7,5},{8,10},{9,11},{10,... | collective-permute-start | bytes 491528 | tf_op jit(solution)/shard_map/ppermute | solution.py:23
  10.5 7.9 %collective-permute-start.5 = (bf16[80,1024]{1,0:T(8,128)(2,1)S(1)}, bf16[80,1024]{1,0:T(8,128)(2,1)S(1)}, u32[]{:S(2)}, u32[]{:S(2)}) collective-permute-start(bf16[80,1024]{1,0:T(8,128)(2,1)S(1)} %fusion.8.refs_0_), channel_id=1, source_target_pairs={{0,4},{1,5},{2,6},{3,7},{4,0},{5,1},{6,2},{7,3},{8,12},{9,13},{10,... | collective-permute-start | bytes 491528 | tf_op jit(solution)/shard_map/ppermute | solution.py:23
  11.9 8.2 %collective-permute-start.4 = (bf16[80,1024]{1,0:T(8,128)(2,1)S(1)}, bf16[80,1024]{1,0:T(8,128)(2,1)S(1)}, u32[]{:S(2)}, u32[]{:S(2)}) collective-permute-start(bf16[80,1024]{1,0:T(8,128)(2,1)S(1)} %fusion.8.refs_0_), channel_id=1, source_target_pairs={{0,24},{1,25},{2,26},{3,27},{4,28},{5,29},{6,30},{7,31},{8,0},{9,1... | collective-permute-start | bytes 491528 | tf_op jit(solution)/shard_map/ppermute | solution.py:23
  15.5 14.1 %collective-permute-start.3 = (bf16[80,1024]{1,0:T(8,128)(2,1)S(1)}, bf16[80,1024]{1,0:T(8,128)(2,1)S(1)}, u32[]{:S(2)}, u32[]{:S(2)}) collective-permute-start(bf16[80,1024]{1,0:T(8,128)(2,1)S(1)} %fusion.8.refs_0_), channel_id=1, source_target_pairs={{0,16},{1,17},{2,18},{3,19},{4,20},{5,21},{6,22},{7,23},{8,24},{9,... | collective-permute-start | bytes 491528 | tf_op jit(solution)/shard_map/ppermute | solution.py:23
  17.4 13.8 %copy-start.4 = (bf16[80,1024]{1,0:T(8,128)(2,1)}, bf16[80,1024]{1,0:T(8,128)(2,1)S(1)}, u32[]{:S(2)}) copy-start(bf16[80,1024]{1,0:T(8,128)(2,1)S(1)} %collective-permute-done.6.refs_4_.refs_5_) | copy-start | bytes 491524
  17.4 12.2 %collective-permute-start.2 = (bf16[80,1024]{1,0:T(8,128)(2,1)S(1)}, bf16[80,1024]{1,0:T(8,128)(2,1)S(1)}, u32[]{:S(2)}, u32[]{:S(2)}) collective-permute-start(bf16[80,1024]{1,0:T(8,128)(2,1)S(1)} %fusion.8.refs_0_), channel_id=1, source_target_pairs={{0,8},{1,9},{2,10},{3,11},{4,12},{5,13},{6,14},{7,15},{8,16},{9,17... | collective-permute-start | bytes 491528 | tf_op jit(solution)/shard_map/ppermute | solution.py:23
  18.4 12.8 %copy-start.6 = (bf16[80,1024]{1,0:T(8,128)(2,1)}, bf16[80,1024]{1,0:T(8,128)(2,1)S(1)}, u32[]{:S(2)}) copy-start(bf16[80,1024]{1,0:T(8,128)(2,1)S(1)} %collective-permute-done.5.refs_3_.refs_4_) | copy-start | bytes 491524
  18.4 13.5 %collective-permute-start.19 = (bf16[128,1024]{1,0:T(8,128)(2,1)}, bf16[128,1024]{1,0:T(8,128)(2,1)}, u32[]{:S(2)}, u32[]{:S(2)}) collective-permute-start(bf16[128,1024]{1,0:T(8,128)(2,1)} %get-tuple-element.51), channel_id=1, source_target_pairs={{1,0},{2,1},{3,2},{4,3},{5,4},{6,5},{7,6},{8,7},{9,8},{10,9},{11,1... | collective-permute-start | bytes 786440 | tf_op jit(solution)/shard_map/ppermute | solution.py:36
  20.1 11.1 %copy-start.8 = (bf16[80,1024]{1,0:T(8,128)(2,1)}, bf16[80,1024]{1,0:T(8,128)(2,1)S(1)}, u32[]{:S(2)}) copy-start(bf16[80,1024]{1,0:T(8,128)(2,1)S(1)} %collective-permute-done.4.refs_2_.refs_3_) | copy-start | bytes 491524
  20.1 13.6 %collective-permute-start.20 = (bf16[128,1024]{1,0:T(8,128)(2,1)}, bf16[128,1024]{1,0:T(8,128)(2,1)}, u32[]{:S(2)}, u32[]{:S(2)}) collective-permute-start(bf16[128,1024]{1,0:T(8,128)(2,1)} %get-tuple-element.52), channel_id=1, source_target_pairs={{0,1},{1,2},{2,3},{3,4},{4,5},{5,6},{6,7},{7,8},{8,9},{9,10},{10,1... | collective-permute-start | bytes 786440 | tf_op jit(solution)/shard_map/ppermute | solution.py:36
  29.6 1.1 copy-start.10
  29.6 1.1 copy-start.12
  30.7 14.3 %collective-permute-start.8 = (bf16[272,1024]{1,0:T(8,128)(2,1)}, bf16[272,1024]{1,0:T(8,128)(2,1)S(1)}, u32[]{:S(2)}, u32[]{:S(2)}) collective-permute-start(bf16[272,1024]{1,0:T(8,128)(2,1)} %get-tuple-element.29), channel_id=1, source_target_pairs={{0,2},{1,3},{2,0},{3,1},{4,6},{5,7},{6,4},{7,5},{8,10},{9,11},{10,... | collective-permute-start | bytes 1671176 | tf_op jit(solution)/shard_map/ppermute | solution.py:23
  31.2 14.8 %collective-permute-start.7 = (bf16[288,1024]{1,0:T(8,128)(2,1)}, bf16[288,1024]{1,0:T(8,128)(2,1)S(1)}, u32[]{:S(2)}, u32[]{:S(2)}) collective-permute-start(bf16[288,1024]{1,0:T(8,128)(2,1)} %get-tuple-element.28), channel_id=1, source_target_pairs={{0,4},{1,5},{2,6},{3,7},{4,0},{5,1},{6,2},{7,3},{8,12},{9,13},{10,... | collective-permute-start | bytes 1769480 | tf_op jit(solution)/shard_map/ppermute | solution.py:23
  31.9 15.7 %copy-start.15 = (bf16[256,2048]{1,0:T(8,128)(2,1)S(1)}, bf16[256,2048]{1,0:T(8,128)(2,1)}, u32[]{:S(2)}) copy-start(bf16[256,2048]{1,0:T(8,128)(2,1)} %copy-done.14) | copy-start | bytes 3145732
  31.9 16.2 %collective-permute-start.10 = (bf16[256,1024]{1,0:T(8,128)(2,1)}, bf16[256,1024]{1,0:T(8,128)(2,1)S(1)}, u32[]{:S(2)}, u32[]{:S(2)}) collective-permute-start(bf16[256,1024]{1,0:T(8,128)(2,1)} %refs_0_.1), channel_id=1, source_target_pairs={{0,8},{1,9},{2,10},{3,11},{4,12},{5,13},{6,14},{7,15},{8,16},{9,17... | collective-permute-start | bytes 1572872 | tf_op jit(solution)/shard_map/ppermute | solution.py:23
  35.1 14.2 %copy-start.16 = (bf16[256,1024]{1,0:T(8,128)(2,1)S(1)}, bf16[256,1024]{1,0:T(8,128)(2,1)}, u32[]{:S(2)}) copy-start(bf16[256,1024]{1,0:T(8,128)(2,1)} %refs_0_.1) | copy-start | bytes 1572868
  35.1 22.7 %copy-start.1 = (bf16[256,4096]{1,0:T(8,128)(2,1)S(1)}, bf16[256,4096]{1,0:T(8,128)(2,1)}, u32[]{:S(2)}) copy-start(bf16[256,4096]{1,0:T(8,128)(2,1)} %copy-done) | copy-start | bytes 6291460
  35.1 22.7 %copy-start.5 = (bf16[80,1024]{1,0:T(8,128)(2,1)S(1)}, bf16[80,1024]{1,0:T(8,128)(2,1)}, u32[]{:S(2)}) copy-start(bf16[80,1024]{1,0:T(8,128)(2,1)} %copy-done.4) | copy-start | bytes 491524
  35.1 22.7 %copy-start.7 = (bf16[80,1024]{1,0:T(8,128)(2,1)S(1)}, bf16[80,1024]{1,0:T(8,128)(2,1)}, u32[]{:S(2)}) copy-start(bf16[80,1024]{1,0:T(8,128)(2,1)} %copy-done.6) | copy-start | bytes 491524
  35.1 22.7 %copy-start.9 = (bf16[80,1024]{1,0:T(8,128)(2,1)S(1)}, bf16[80,1024]{1,0:T(8,128)(2,1)}, u32[]{:S(2)}) copy-start(bf16[80,1024]{1,0:T(8,128)(2,1)} %copy-done.8) | copy-start | bytes 491524
  35.1 22.7 %copy-start.11 = (bf16[80,1024]{1,0:T(8,128)(2,1)S(1)}, bf16[80,1024]{1,0:T(8,128)(2,1)}, u32[]{:S(2)}) copy-start(bf16[80,1024]{1,0:T(8,128)(2,1)} %copy-done.10) | copy-start | bytes 491524
  35.1 22.7 %copy-start.13 = (bf16[80,1024]{1,0:T(8,128)(2,1)S(1)}, bf16[80,1024]{1,0:T(8,128)(2,1)}, u32[]{:S(2)}) copy-start(bf16[80,1024]{1,0:T(8,128)(2,1)} %copy-done.12) | copy-start | bytes 491524
  35.2 14.1 %collective-permute-start.21 = (bf16[256,512]{1,0:T(8,128)(2,1)S(1)}, bf16[256,512]{1,0:T(8,128)(2,1)S(1)}, u32[]{:S(2)}, u32[]{:S(2)}) collective-permute-start(bf16[256,512]{1,0:T(8,128)(2,1)S(1)} %get-tuple-element.53), channel_id=1, source_target_pairs={{0,1},{1,0},{2,3},{3,2},{4,5},{5,4},{6,7},{7,6},{8,9},{9,8},{10,11... | collective-permute-start | bytes 786440 | tf_op jit(solution)/shard_map/ppermute | solution.py:23
  46.0 8.6 %collective-permute-start.18 = (bf16[112,1024]{1,0:T(8,128)(2,1)S(1)}, bf16[112,1024]{1,0:T(8,128)(2,1)S(1)}, u32[]{:S(2)}, u32[]{:S(2)}) collective-permute-start(bf16[112,1024]{1,0:T(8,128)(2,1)S(1)} %get-tuple-element.36), channel_id=1, source_target_pairs={{0,2},{1,3},{2,0},{3,1},{4,6},{5,7},{6,4},{7,5},{8,10},{9,11},{10,... | collective-permute-start | bytes 688136 | tf_op jit(solution)/shard_map/ppermute | solution.py:23
  47.6 29.5 %collective-permute-start.1 = (bf16[256,2048]{1,0:T(8,128)(2,1)S(1)}, bf16[256,2048]{1,0:T(8,128)(2,1)S(1)}, u32[]{:S(2)}, u32[]{:S(2)}) collective-permute-start(bf16[256,2048]{1,0:T(8,128)(2,1)S(1)} %copy-done.15), channel_id=1, source_target_pairs={{0,2},{1,3},{2,0},{3,1},{4,6},{5,7},{6,4},{7,5},{8,10},{9,11},{10,... | collective-permute-start | bytes 3145736 | tf_op jit(solution)/shard_map/ppermute | solution.py:23
  48.1 13.4 %collective-permute-start.11 = (bf16[256,1024]{1,0:T(8,128)(2,1)S(1)}, bf16[256,1024]{1,0:T(8,128)(2,1)S(1)}, u32[]{:S(2)}, u32[]{:S(2)}) collective-permute-start(bf16[256,1024]{1,0:T(8,128)(2,1)S(1)} %collective-permute-done.10.refs_1_), channel_id=1, source_target_pairs={{0,8},{1,9},{2,10},{3,11},{4,12},{5,13},{6,14},{7,15},{8,16},{9,17... | collective-permute-start | bytes 1572872 | tf_op jit(solution)/shard_map/ppermute | solution.py:23
  48.6 9.2 %collective-permute-start.17 = (bf16[128,1024]{1,0:T(8,128)(2,1)S(1)}, bf16[128,1024]{1,0:T(8,128)(2,1)S(1)}, u32[]{:S(2)}, u32[]{:S(2)}) collective-permute-start(bf16[128,1024]{1,0:T(8,128)(2,1)S(1)} %get-tuple-element.35), channel_id=1, source_target_pairs={{0,4},{1,5},{2,6},{3,7},{4,0},{5,1},{6,2},{7,3},{8,12},{9,13},{10,... | collective-permute-start | bytes 786440 | tf_op jit(solution)/shard_map/ppermute | solution.py:23
  49.3 16.6 %collective-permute-start.15 = (bf16[256,1024]{1,0:T(8,128)(2,1)S(1)}, bf16[256,1024]{1,0:T(8,128)(2,1)S(1)}, u32[]{:S(2)}, u32[]{:S(2)}) collective-permute-start(bf16[256,1024]{1,0:T(8,128)(2,1)S(1)} %copy-done.16), channel_id=1, source_target_pairs={{0,4},{1,5},{2,6},{3,7},{4,0},{5,1},{6,2},{7,3},{8,12},{9,13},{10,... | collective-permute-start | bytes 1572872 | tf_op jit(solution)/shard_map/ppermute | solution.py:23
  54.6 42.3 %collective-permute-start.9 = (bf16[256,2048]{1,0:T(8,128)(2,1)S(1)}, bf16[256,2048]{1,0:T(8,128)(2,1)S(1)}, u32[]{:S(2)}, u32[]{:S(2)}) collective-permute-start(bf16[256,2048]{1,0:T(8,128)(2,1)S(1)} %slice.52.refs_12_), channel_id=1, source_target_pairs={{0,2},{1,3},{2,0},{3,1},{4,6},{5,7},{6,4},{7,5},{8,10},{9,11},{10,... | collective-permute-start | bytes 3145736 | tf_op jit(solution)/shard_map/ppermute | solution.py:23
  59.4 40.9 %collective-permute-start.22 = (f32[1040,256]{1,0:T(8,128)S(1)}, f32[1040,256]{1,0:T(8,128)S(1)}, u32[]{:S(2)}, u32[]{:S(2)}) collective-permute-start(f32[1040,256]{1,0:T(8,128)S(1)} %get-tuple-element.37.own), channel_id=1, source_target_pairs={{0,1},{1,0},{2,3},{3,2},{4,5},{5,4},{6,7},{7,6},{8,9},{9,8},{10,11... | collective-permute-start | bytes 3194888 | tf_op jit(solution)/shard_map/ppermute | solution.py:23
  61.5 16.1 %collective-permute-start.13 = (bf16[256,1024]{1,0:T(8,128)(2,1)S(1)}, bf16[256,1024]{1,0:T(8,128)(2,1)S(1)}, u32[]{:S(2)}, u32[]{:S(2)}) collective-permute-start(bf16[256,1024]{1,0:T(8,128)(2,1)S(1)} %collective-permute-done.11.refs_2_.refs_0_), channel_id=1, source_target_pairs={{0,8},{1,9},{2,10},{3,11},{4,12},{5,13},{6,14},{7,15},{8,16},{9,17... | collective-permute-start | bytes 1572872 | tf_op jit(solution)/shard_map/ppermute | solution.py:23
  65.9 13.2 %collective-permute-start.16 = (bf16[256,1024]{1,0:T(8,128)(2,1)S(1)}, bf16[256,1024]{1,0:T(8,128)(2,1)S(1)}, u32[]{:S(2)}, u32[]{:S(2)}) collective-permute-start(bf16[256,1024]{1,0:T(8,128)(2,1)S(1)} %collective-permute-done.10.refs_1_), channel_id=1, source_target_pairs={{0,4},{1,5},{2,6},{3,7},{4,0},{5,1},{6,2},{7,3},{8,12},{9,13},{10,... | collective-permute-start | bytes 1572872 | tf_op jit(solution)/shard_map/ppermute | solution.py:23
  77.1 25.6 %collective-permute-start.12 = (bf16[256,1024]{1,0:T(8,128)(2,1)S(1)}, bf16[256,1024]{1,0:T(8,128)(2,1)S(1)}, u32[]{:S(2)}, u32[]{:S(2)}) collective-permute-start(bf16[256,1024]{1,0:T(8,128)(2,1)S(1)} %collective-permute-done.11.refs_2_.refs_0_), channel_id=1, source_target_pairs={{0,4},{1,5},{2,6},{3,7},{4,0},{5,1},{6,2},{7,3},{8,12},{9,13},{10,... | collective-permute-start | bytes 1572872 | tf_op jit(solution)/shard_map/ppermute | solution.py:23
  77.7 25.0 %collective-permute-start.14 = (bf16[256,1024]{1,0:T(8,128)(2,1)S(1)}, bf16[256,1024]{1,0:T(8,128)(2,1)S(1)}, u32[]{:S(2)}, u32[]{:S(2)}) collective-permute-start(bf16[256,1024]{1,0:T(8,128)(2,1)S(1)} %collective-permute-done.13.refs_3_), channel_id=1, source_target_pairs={{0,4},{1,5},{2,6},{3,7},{4,0},{5,1},{6,2},{7,3},{8,12},{9,13},{10,... | collective-permute-start | bytes 1572872 | tf_op jit(solution)/shard_map/ppermute | solution.py:23
  100.3 2.4 %copy-start.3 = (f32[512,1024]{1,0:T(8,128)}, f32[512,1024]{1,0:T(8,128)S(1)}, u32[]{:S(2)}) copy-start(f32[512,1024]{1,0:T(8,128)S(1)} %get-tuple-element.34.refs_3_) | copy-start | bytes 6291460
  105.8 2.7 %collective-permute-start.23 = (bf16[512,1024]{1,0:T(8,128)(2,1)S(1)}, bf16[512,1024]{1,0:T(8,128)(2,1)S(1)}, u32[]{:S(2)}, u32[]{:S(2)}) collective-permute-start(bf16[512,1024]{1,0:T(8,128)(2,1)S(1)} %get-tuple-element.41), channel_id=1, source_target_pairs={{0,1},{1,0},{2,3},{3,2},{4,5},{5,4},{6,7},{7,6},{8,9},{9,8},{10,11... | collective-permute-start | bytes 3145736 | tf_op jit(solution)/shard_map/ppermute | solution.py:23
  109.0 1.6 %copy-start.17 = (f32[512,1024]{1,0:T(8,128)}, f32[512,1024]{1,0:T(8,128)S(1)}, u32[]{:S(2)}) copy-start(f32[512,1024]{1,0:T(8,128)S(1)} %convert_add_fusion) | copy-start | bytes 6291460
  109.1 15.4 %collective-permute-start.24 = (bf16[256,1024]{1,0:T(8,128)(2,1)S(1)}, bf16[256,1024]{1,0:T(8,128)(2,1)S(1)}, u32[]{:S(2)}, u32[]{:S(2)}) collective-permute-start(bf16[256,1024]{1,0:T(8,128)(2,1)S(1)} %slice.64), channel_id=1, source_target_pairs={{0,2},{1,3},{2,0},{3,1},{4,6},{5,7},{6,4},{7,5},{8,10},{9,11},{10,... | collective-permute-start | bytes 1572872 | tf_op jit(solution)/shard_map/ppermute | solution.py:23
  110.6 24.9 %all-to-all-start = ((bf16[16,96,256]{2,1,0:T(8,128)(2,1)}), bf16[16,96,256]{2,1,0:T(8,128)(2,1)S(1)}, u32[]{:S(2)}, u32[]{:S(2)}) async-start(bf16[16,96,256]{2,1,0:T(8,128)(2,1)} %get-tuple-element.42), calls=%async_computation | async-start | bytes 1572864 | tf_op jit(solution)/shard_map/all_to_all | solution.py:463
  126.6 10.4 %collective-permute-start.25 = (bf16[128,1024]{1,0:T(8,128)(2,1)S(1)}, bf16[128,1024]{1,0:T(8,128)(2,1)S(1)}, u32[]{:S(2)}, u32[]{:S(2)}) collective-permute-start(bf16[128,1024]{1,0:T(8,128)(2,1)S(1)} %get-tuple-element.47), channel_id=1, source_target_pairs={{0,1},{1,2},{2,3},{3,4},{4,5},{5,6},{6,7},{7,8},{8,9},{9,10},{10,1... | collective-permute-start | bytes 786440 | tf_op jit(solution)/shard_map/ppermute | solution.py:36
  127.9 9.1 %collective-permute-start.26 = (bf16[128,1024]{1,0:T(8,128)(2,1)S(1)}, bf16[128,1024]{1,0:T(8,128)(2,1)S(1)}, u32[]{:S(2)}, u32[]{:S(2)}) collective-permute-start(bf16[128,1024]{1,0:T(8,128)(2,1)S(1)} %get-tuple-element.48), channel_id=1, source_target_pairs={{1,0},{2,1},{3,2},{4,3},{5,4},{6,5},{7,6},{8,7},{9,8},{10,9},{11,1... | collective-permute-start | bytes 786440 | tf_op jit(solution)/shard_map/ppermute | solution.py:36
